TPU v7x, 512 devices: a whole 4x8x8 slice. The times are simulated.
512 devices in a mesh: rep: 8 (over y_hi, core), dap: 64 (over z, y_lo, x).
Axes of the slice: x: 4, y: 8 (y_hi: 4, y_lo: 2; y = y_hi * 2 + y_lo), z: 8, core: 2. Of those that a mesh axis runs over, the one named last changes fastest.
Arguments:
- pair_act: bfloat16 [8, 256, 256, 128], P('rep', 'dap'), may hold values from -6 to 6
- cotangent: bfloat16 [8, 256, 256, 128], P('rep', 'dap'), may hold values from -6 to 6
- outgoing_in: bfloat16 [128, 640], replicated, may hold values from -0.5 to 0.5
- outgoing_out: bfloat16 [128, 128], replicated, may hold values from -0.5 to 0.5
- incoming_in: bfloat16 [128, 640], replicated, may hold values from -0.5 to 0.5
- incoming_out: bfloat16 [128, 128], replicated, may hold values from -0.5 to 0.5
Outputs:
- pair_grad: bfloat16 [8, 256, 256, 128], P('rep', 'dap')
- outgoing_in_grad: float32 [128, 640], replicated
- outgoing_out_grad: float32 [128, 128], replicated
- incoming_in_grad: float32 [128, 640], replicated
- incoming_out_grad: float32 [128, 128], replicated
All inputs are finite; a program needn't handle non-finite values.
Results may differ from a plain program's by a relative error of at most 0.019.
Values may be sent and summed in bfloat16 or wider, within the bound.
No kernel may reach another device: no remote copies, remote signals or barrier semaphores. Data moves between devices by JAX's collectives and lax.ppermute only.
A program may use at most 64 MiB of HBM per device.

v0:
```python
import math

import jax
import jax.numpy as jnp
from jax import lax
from jax.sharding import PartitionSpec as P

EPS = 1e-05


def normalize(values, along):
    average = jnp.mean(values, axis=along, keepdims=True)
    centred = values - average
    spread = jnp.mean(centred * centred, axis=along, keepdims=True)
    inv_std = lax.rsqrt(spread + EPS)
    return (centred * inv_std, inv_std)


def norm_back(normed, inv_std, incoming_grad, along):
    first = jnp.mean(incoming_grad, axis=along, keepdims=True)
    second = jnp.mean(incoming_grad * normed, axis=along, keepdims=True)
    return inv_std * (incoming_grad - first - normed * second)


def tri_product(left_ch, right_ch, incoming):
    if incoming:
        return jnp.einsum("cki,ckj->cij", left_ch, right_ch, preferred_element_type=jnp.float32)
    return jnp.einsum("cik,cjk->cij", left_ch, right_ch, preferred_element_type=jnp.float32)


def tri_grads(grad_ch, left_ch, right_ch, incoming):
    if incoming:
        grad_left = jnp.einsum(
            "cij,ckj->cki", grad_ch, right_ch, preferred_element_type=jnp.float32
        )
        grad_right = jnp.einsum(
            "cij,cki->ckj", grad_ch, left_ch, preferred_element_type=jnp.float32
        )
    else:
        grad_left = jnp.einsum(
            "cij,cjk->cik", grad_ch, right_ch, preferred_element_type=jnp.float32
        )
        grad_right = jnp.einsum(
            "cij,cik->cjk", grad_ch, left_ch, preferred_element_type=jnp.float32
        )
    return (grad_left.astype(jnp.bfloat16), grad_right.astype(jnp.bfloat16))


def module_forward(state, w_in, w_out, incoming):
    hidden = w_out.shape[0]
    normed, inv_std = normalize(state, 2)
    normed_in = normed.astype(jnp.bfloat16)
    pre_act = jnp.einsum(
        "rnc,cd->drn", normed_in, w_in[:, : 4 * hidden], preferred_element_type=jnp.float32
    )
    gate_logits = jnp.einsum(
        "rnc,cd->rnd", normed_in, w_in[:, 4 * hidden :], preferred_element_type=jnp.float32
    )
    left_proj = pre_act[:hidden]
    left_gate = pre_act[hidden : 2 * hidden]
    right_proj = pre_act[2 * hidden : 3 * hidden]
    right_gate = pre_act[3 * hidden :]
    left_op = (jax.nn.sigmoid(left_gate) * left_proj).astype(jnp.bfloat16)
    right_op = (jax.nn.sigmoid(right_gate) * right_proj).astype(jnp.bfloat16)
    left_ch, right_ch = (
        lax.all_to_all(left_op, "dap", split_axis=0, concat_axis=1, tiled=True),
        lax.all_to_all(right_op, "dap", split_axis=0, concat_axis=1, tiled=True),
    )
    product = tri_product(left_ch, right_ch, incoming).astype(jnp.bfloat16)
    kept_left, kept_right = (left_ch, right_ch)
    out_rows = lax.all_to_all(product, "dap", split_axis=1, concat_axis=0, tiled=True)
    out_normed, out_inv = normalize(out_rows.astype(jnp.float32), 0)
    out_bf = out_normed.astype(jnp.bfloat16)
    mixed = jnp.einsum("crn,cd->rnd", out_bf, w_out, preferred_element_type=jnp.float32)
    gate_val = jax.nn.sigmoid(gate_logits)
    saved = (
        normed,
        inv_std,
        normed_in,
        left_proj,
        left_gate,
        right_proj,
        right_gate,
        kept_left,
        kept_right,
        out_normed,
        out_inv,
        out_bf,
        mixed,
        gate_val,
    )
    return (state + gate_val * mixed, saved)


def module_backward(grad_u, saved, w_in, w_out, incoming):
    (
        normed,
        inv_std,
        normed_in,
        left_proj,
        left_gate,
        right_proj,
        right_gate,
        kept_left,
        kept_right,
        out_normed,
        out_inv,
        out_bf,
        mixed,
        gate_val,
    ) = saved
    hidden = w_out.shape[0]
    grad_mix = (grad_u * gate_val).astype(jnp.bfloat16)
    grad_gate = grad_u * mixed * gate_val * (1.0 - gate_val)
    grad_out_w = jnp.einsum("crn,rnd->cd", out_bf, grad_mix, preferred_element_type=jnp.float32)
    grad_on = jnp.einsum("rnd,cd->crn", grad_mix, w_out, preferred_element_type=jnp.float32)
    grad_prod = norm_back(out_normed, out_inv, grad_on, 0).astype(jnp.bfloat16)
    grad_ch = lax.all_to_all(grad_prod, "dap", split_axis=0, concat_axis=1, tiled=True)
    grad_left, grad_right = tri_grads(grad_ch, kept_left, kept_right, incoming)
    grad_left, grad_right = (
        lax.all_to_all(grad_left, "dap", split_axis=1, concat_axis=0, tiled=True),
        lax.all_to_all(grad_right, "dap", split_axis=1, concat_axis=0, tiled=True),
    )
    sig_left = jax.nn.sigmoid(left_gate)
    sig_right = jax.nn.sigmoid(right_gate)
    grad_pre = jnp.concatenate(
        [
            grad_left * sig_left,
            grad_left * left_proj * sig_left * (1.0 - sig_left),
            grad_right * sig_right,
            grad_right * right_proj * sig_right * (1.0 - sig_right),
        ],
        0,
    ).astype(jnp.bfloat16)
    grad_gate_bf = grad_gate.astype(jnp.bfloat16)
    grad_in_w = jnp.concatenate(
        [
            jnp.einsum("rnc,drn->cd", normed_in, grad_pre, preferred_element_type=jnp.float32),
            jnp.einsum("rnc,rnd->cd", normed_in, grad_gate_bf, preferred_element_type=jnp.float32),
        ],
        1,
    )
    grad_normed = jnp.einsum(
        "drn,cd->rnc", grad_pre, w_in[:, : 4 * hidden], preferred_element_type=jnp.float32
    )
    grad_normed = grad_normed + jnp.einsum(
        "rnd,cd->rnc", grad_gate_bf, w_in[:, 4 * hidden :], preferred_element_type=jnp.float32
    )
    return (grad_u + norm_back(normed, inv_std, grad_normed, 2), grad_in_w, grad_out_w)


def local(pair_act, cotangent, outgoing_in, outgoing_out, incoming_in, incoming_out):
    start = pair_act[0].astype(jnp.float32)
    middle, saved_out = module_forward(start, outgoing_in, outgoing_out, False)
    finish, saved_in = module_forward(middle, incoming_in, incoming_out, True)
    grad_mid, grad_ii, grad_io = module_backward(
        cotangent[0].astype(jnp.float32), saved_in, incoming_in, incoming_out, True
    )
    grad_start, grad_oi, grad_oo = module_backward(
        grad_mid, saved_out, outgoing_in, outgoing_out, False
    )
    grad_oi, grad_oo, grad_ii, grad_io = lax.psum(
        (grad_oi, grad_oo, grad_ii, grad_io), ("rep", "dap")
    )
    crop_count = lax.axis_size("rep") * pair_act.shape[0]
    length = pair_act.shape[2]
    grad_scale = 1.0 / math.sqrt(crop_count * length * length)
    return (
        grad_start.astype(jnp.bfloat16)[None],
        grad_oi * grad_scale,
        grad_oo * grad_scale,
        grad_ii * grad_scale,
        grad_io * grad_scale,
    )


def solution(mesh):
    return jax.shard_map(
        local,
        mesh=mesh,
        in_specs=(P("rep", "dap", None, None), P("rep", "dap", None, None), P(), P(), P(), P()),
        out_specs=(P("rep", "dap", None, None), P(), P(), P(), P()),
        check_vma=False,
    )
```

profile of v0, /device:TPU:17, one launch (start us, length us, event | category | flops | bytes accessed | tf_op | source)
XLA Modules:
  0.0 562.8 jit_solution(13345848372551362090)
XLA Ops:
  8.5 1.4 convolution_bitcast_fusion.1
  11.0 14.5 %all-to-all-start.1 = ((bf16[128,4,256]{2,1,0:T(4,128)(2,1)}), bf16[128,4,256]{2,1,0:T(4,128)(2,1)S(1)}, u32[]{:S(2)}, u32[]{:S(2)}) async-start(bf16[128,4,256]{2,1,0:T(4,128)(2,1)} %copy.113), calls=%async_computation.1 | async-start | bytes 524288 | tf_op jit(solution)/shard_map/all_to_all | solution.py:67
  26.4 10.8 %all-to-all-done.1 = bf16[128,4,256]{2,1,0:T(4,128)(2,1)S(1)} async-done(((bf16[128,4,256]{2,1,0:T(4,128)(2,1)}), bf16[128,4,256]{2,1,0:T(4,128)(2,1)S(1)}, u32[]{:S(2)}, u32[]{:S(2)}) %all-to-all-start.1) | async-done | bytes 262176 | tf_op jit(solution)/shard_map/all_to_all | solution.py:67
  37.2 6.1 %all-to-all-start = ((bf16[128,4,256]{2,1,0:T(4,128)(2,1)}), bf16[128,4,256]{2,1,0:T(4,128)(2,1)S(1)}, u32[]{:S(2)}, u32[]{:S(2)}) async-start(bf16[128,4,256]{2,1,0:T(4,128)(2,1)} %copy.111), calls=%async_computation | async-start | bytes 524288 | tf_op jit(solution)/shard_map/all_to_all | solution.py:66
  43.5 11.0 %all-to-all-done = bf16[128,4,256]{2,1,0:T(4,128)(2,1)S(1)} async-done(((bf16[128,4,256]{2,1,0:T(4,128)(2,1)}), bf16[128,4,256]{2,1,0:T(4,128)(2,1)S(1)}, u32[]{:S(2)}, u32[]{:S(2)}) %all-to-all-start) | async-done | bytes 262176 | tf_op jit(solution)/shard_map/all_to_all | solution.py:66
  55.4 17.3 %all_to_all.162 = bf16[2,256,256]{2,0,1:T(2,128)(2,1)S(1)} all-to-all(bf16[2,256,256]{2,0,1:T(2,128)(2,1)S(1)} %copy.115), channel_id=1, replica_groups=mesh['rep'=8,'dap'=64] {'dap'}, dimensions={1} | all-to-all | bytes 524288 | tf_op jit(solution)/shard_map/all_to_all | solution.py:71
  74.1 2.1 fusion.84
  80.0 6.6 %all-to-all-start.4 = ((bf16[128,4,256]{2,1,0:T(4,128)(2,1)}), bf16[128,4,256]{2,1,0:T(4,128)(2,1)S(1)}, u32[]{:S(2)}, u32[]{:S(2)}) async-start(bf16[128,4,256]{2,1,0:T(4,128)(2,1)} %copy.121), calls=%async_computation.4 | async-start | bytes 524288 | tf_op jit(solution)/shard_map/all_to_all | solution.py:66
  87.5 10.1 %all-to-all-done.4 = bf16[128,4,256]{2,1,0:T(4,128)(2,1)S(1)} async-done(((bf16[128,4,256]{2,1,0:T(4,128)(2,1)}), bf16[128,4,256]{2,1,0:T(4,128)(2,1)S(1)}, u32[]{:S(2)}, u32[]{:S(2)}) %all-to-all-start.4) | async-done | bytes 262176 | tf_op jit(solution)/shard_map/all_to_all | solution.py:66
  97.6 6.8 %all-to-all-start.3 = ((bf16[128,4,256]{2,1,0:T(4,128)(2,1)}), bf16[128,4,256]{2,1,0:T(4,128)(2,1)}, u32[]{:S(2)}, u32[]{:S(2)}) async-start(bf16[128,4,256]{2,1,0:T(4,128)(2,1)} %copy.119), calls=%async_computation.3 | async-start | bytes 524288 | tf_op jit(solution)/shard_map/all_to_all | solution.py:67
  104.6 10.7 %all-to-all-done.3 = bf16[128,4,256]{2,1,0:T(4,128)(2,1)} async-done(((bf16[128,4,256]{2,1,0:T(4,128)(2,1)}), bf16[128,4,256]{2,1,0:T(4,128)(2,1)}, u32[]{:S(2)}, u32[]{:S(2)}) %all-to-all-start.3) | async-done | bytes 262176 | tf_op jit(solution)/shard_map/all_to_all | solution.py:67
  115.4 1.7 copy.120
  119.4 6.8 %all-to-all-start.5 = ((bf16[2,256,256]{2,0,1:T(2,128)(2,1)}), bf16[2,256,256]{2,0,1:T(2,128)(2,1)}, u32[]{:S(2)}, u32[]{:S(2)}) async-start(bf16[2,256,256]{2,0,1:T(2,128)(2,1)} %copy.124), calls=%async_computation.5 | async-start | bytes 524288 | tf_op jit(solution)/shard_map/all_to_all | solution.py:71
  127.3 1.9 fusion.5
  129.2 7.8 %all-to-all-done.5 = bf16[2,256,256]{2,0,1:T(2,128)(2,1)} async-done(((bf16[2,256,256]{2,0,1:T(2,128)(2,1)}), bf16[2,256,256]{2,0,1:T(2,128)(2,1)}, u32[]{:S(2)}, u32[]{:S(2)}) %all-to-all-start.5) | async-done | bytes 262176 | tf_op jit(solution)/shard_map/all_to_all | solution.py:71
  138.6 1.9 copy_bitcast_fusion
  140.5 1.4 reshape.123
  143.5 17.1 %all_to_all.163 = bf16[128,4,256]{2,1,0:T(4,128)(2,1)S(1)} all-to-all(bf16[128,4,256]{2,1,0:T(4,128)(2,1)S(1)} %copy.129), channel_id=1, replica_groups=mesh['rep'=8,'dap'=64] {'dap'}, dimensions={0} | all-to-all | bytes 524288 | tf_op jit(solution)/shard_map/all_to_all | solution.py:118
  161.4 1.7 all_to_all.141
  165.4 6.8 %all-to-all-start.7 = ((bf16[2,256,256]{2,0,1:T(2,128)(2,1)}), bf16[2,256,256]{2,0,1:T(2,128)(2,1)}, u32[]{:S(2)}, u32[]{:S(2)}) async-start(bf16[2,256,256]{2,0,1:T(2,128)(2,1)} %copy.131), calls=%async_computation.7 | async-start | bytes 524288 | tf_op jit(solution)/shard_map/all_to_all | solution.py:121
  174.5 8.7 %all-to-all-done.7 = bf16[2,256,256]{2,0,1:T(2,128)(2,1)} async-done(((bf16[2,256,256]{2,0,1:T(2,128)(2,1)}), bf16[2,256,256]{2,0,1:T(2,128)(2,1)}, u32[]{:S(2)}, u32[]{:S(2)}) %all-to-all-start.7) | async-done | bytes 262176 | tf_op jit(solution)/shard_map/all_to_all | solution.py:121
  183.2 6.6 %all-to-all-start.8 = ((bf16[2,256,256]{2,0,1:T(2,128)(2,1)}), bf16[2,256,256]{2,0,1:T(2,128)(2,1)}, u32[]{:S(2)}, u32[]{:S(2)}) async-start(bf16[2,256,256]{2,0,1:T(2,128)(2,1)} %copy.136), calls=%async_computation.8 | async-start | bytes 524288 | tf_op jit(solution)/shard_map/all_to_all | solution.py:122
  191.9 1.8 fusion.63
  193.7 1.8 copy.132
  195.5 2.0 copy.133
  197.6 3.2 all-to-all-done.8
  200.8 1.9 copy.137
  202.7 2.0 copy.138
  204.7 2.4 multiply_convert_fusion.10
  211.8 7.6 %all-to-all-start.9 = ((bf16[128,4,256]{2,1,0:T(4,128)(2,1)}), bf16[128,4,256]{2,1,0:T(4,128)(2,1)}, u32[]{:S(2)}, u32[]{:S(2)}) async-start(bf16[128,4,256]{2,1,0:T(4,128)(2,1)} %copy.145), calls=%async_computation.9 | async-start | bytes 524288 | tf_op jit(solution)/shard_map/all_to_all | solution.py:118
  219.4 1.9 convolution_bitcast_fusion.6
  221.3 8.9 %all-to-all-done.9 = bf16[128,4,256]{2,1,0:T(4,128)(2,1)} async-done(((bf16[128,4,256]{2,1,0:T(4,128)(2,1)}), bf16[128,4,256]{2,1,0:T(4,128)(2,1)}, u32[]{:S(2)}, u32[]{:S(2)}) %all-to-all-start.9) | async-done | bytes 262176 | tf_op jit(solution)/shard_map/all_to_all | solution.py:118
  230.2 1.7 copy.213
  231.9 1.7 all_to_all.147
  235.9 5.7 %all-to-all-start.10 = ((bf16[2,256,256]{2,0,1:T(2,128)(2,1)}), bf16[2,256,256]{2,0,1:T(2,128)(2,1)}, u32[]{:S(2)}, u32[]{:S(2)}) async-start(bf16[2,256,256]{2,0,1:T(2,128)(2,1)} %copy.147), calls=%async_computation.10 | async-start | bytes 524288 | tf_op jit(solution)/shard_map/all_to_all | solution.py:121
  241.9 2.3 convolution_bitcast_fusion.4
  245.4 6.7 %all-to-all-done.10 = bf16[2,256,256]{2,0,1:T(2,128)(2,1)} async-done(((bf16[2,256,256]{2,0,1:T(2,128)(2,1)}), bf16[2,256,256]{2,0,1:T(2,128)(2,1)}, u32[]{:S(2)}, u32[]{:S(2)}) %all-to-all-start.10) | async-done | bytes 262176 | tf_op jit(solution)/shard_map/all_to_all | solution.py:121
  252.1 5.5 all-to-all-start.11
  257.6 1.9 convolution_bitcast_fusion.9
  259.5 1.7 pad_maximum_fusion.3
  262.1 1.8 fusion.58
  265.9 2.2 all-to-all-done.11
  270.2 1.7 multiply_convert_fusion.4
  275.8 273.7 %all-reduce.3.cloned.1.call-done = (f32[128,640]{1,0:T(8,128)}, f32[128,128]{1,0:T(8,128)}, f32[128,640]{1,0:T(8,128)}, f32[128,128]{1,0:T(8,128)}) async-done(((f32[128,640]{1,0:T(8,128)}, f32[128,128]{1,0:T(8,128)}, f32[128,640]{1,0:T(8,128)}, f32[128,128]{1,0:T(8,128)}), (f32[128,640]{1,0:T(8,128)}, f32[128,128]{1,0:T(8,128)}, f32[128,640]{1,0:T(8,128)}, ...) | async-done | bytes 786448 | tf_op jit(solution)/shard_map/psum | solution.py:162
  549.5 1.7 broadcast_multiply_fusion.1
  551.2 1.5 broadcast_multiply_fusion.3
  552.7 1.5 broadcast_multiply_fusion.2
  554.2 1.7 broadcast_multiply_fusion
  (152 shorter events, 41.7 us)
Async XLA Ops:
  7.2 134.7 %copy-start = (bf16[128,128]{1,0:T(8,128)(2,1)S(1)}, bf16[128,128]{1,0:T(8,128)(2,1)}, u32[]{:S(2)}) copy-start(bf16[128,128]{1,0:T(8,128)(2,1)} %param.11) | copy-start | bytes 98308
  8.3 65.8 %copy-start.5 = (bf16[1,4,256,128]{2,3,1,0:T(8,128)(2,1)}, bf16[1,4,256,128]{2,3,1,0:T(8,128)(2,1)S(1)}, u32[]{:S(2)}) copy-start(bf16[1,4,256,128]{2,3,1,0:T(8,128)(2,1)S(1)} %copy.107) | copy-start | bytes 786436
  11.0 26.2 %all-to-all-start.1 = ((bf16[128,4,256]{2,1,0:T(4,128)(2,1)}), bf16[128,4,256]{2,1,0:T(4,128)(2,1)S(1)}, u32[]{:S(2)}, u32[]{:S(2)}) async-start(bf16[128,4,256]{2,1,0:T(4,128)(2,1)} %copy.113), calls=%async_computation.1 | async-start | bytes 524288 | tf_op jit(solution)/shard_map/all_to_all | solution.py:67
  37.2 17.3 %all-to-all-start = ((bf16[128,4,256]{2,1,0:T(4,128)(2,1)}), bf16[128,4,256]{2,1,0:T(4,128)(2,1)S(1)}, u32[]{:S(2)}, u32[]{:S(2)}) async-start(bf16[128,4,256]{2,1,0:T(4,128)(2,1)} %copy.111), calls=%async_computation | async-start | bytes 524288 | tf_op jit(solution)/shard_map/all_to_all | solution.py:66
  43.5 11.7 %copy-start.10 = (bf16[2,256,256]{2,1,0:T(8,128)(2,1)}, bf16[2,256,256]{2,1,0:T(8,128)(2,1)S(1)}, u32[]{:S(2)}) copy-start(bf16[2,256,256]{2,1,0:T(8,128)(2,1)S(1)} %all_to_all.127) | copy-start | bytes 786436
  54.6 0.7 copy-start.8
  55.4 18.5 %copy-start.35 = (bf16[128,128]{1,0:T(8,128)(2,1)S(1)}, bf16[128,128]{1,0:T(8,128)(2,1)}, u32[]{:S(2)}) copy-start(bf16[128,128]{1,0:T(8,128)(2,1)} %param.9) | copy-start | bytes 98308
  74.1 2.9 copy-start.20
  74.1 2.9 copy-start.32
  76.2 0.8 copy-start.2
  77.1 50.2 %copy-start.11 = (bf16[4,256,128]{1,2,0:T(8,128)(2,1)}, bf16[4,256,128]{1,2,0:T(8,128)(2,1)S(1)}, u32[]{:S(2)}) copy-start(bf16[4,256,128]{1,2,0:T(8,128)(2,1)S(1)} %fusion.35) | copy-start | bytes 786436
  77.5 1.3 copy-start.1
  80.0 17.6 %all-to-all-start.4 = ((bf16[128,4,256]{2,1,0:T(4,128)(2,1)}), bf16[128,4,256]{2,1,0:T(4,128)(2,1)S(1)}, u32[]{:S(2)}, u32[]{:S(2)}) async-start(bf16[128,4,256]{2,1,0:T(4,128)(2,1)} %copy.121), calls=%async_computation.4 | async-start | bytes 524288 | tf_op jit(solution)/shard_map/all_to_all | solution.py:66
  97.6 17.8 %all-to-all-start.3 = ((bf16[128,4,256]{2,1,0:T(4,128)(2,1)}), bf16[128,4,256]{2,1,0:T(4,128)(2,1)}, u32[]{:S(2)}, u32[]{:S(2)}) async-start(bf16[128,4,256]{2,1,0:T(4,128)(2,1)} %copy.119), calls=%async_computation.3 | async-start | bytes 524288 | tf_op jit(solution)/shard_map/all_to_all | solution.py:67
  104.6 14.8 %copy-start.15 = (bf16[2,64,4,256]{3,0,2,1:T(2,128)(2,1)}, bf16[2,64,4,256]{3,0,2,1:T(2,128)(2,1)S(1)}, u32[]{:S(2)}) copy-start(bf16[2,64,4,256]{3,0,2,1:T(2,128)(2,1)S(1)} %copy.122) | copy-start | bytes 786436
  118.1 11.1 %copy-start.16 = (bf16[2,256,256]{2,1,0:T(8,128)(2,1)}, bf16[2,256,256]{2,1,0:T(8,128)(2,1)S(1)}, u32[]{:S(2)}) copy-start(bf16[2,256,256]{2,1,0:T(8,128)(2,1)S(1)} %all_to_all.132) | copy-start | bytes 786436
  119.4 17.6 %all-to-all-start.5 = ((bf16[2,256,256]{2,0,1:T(2,128)(2,1)}), bf16[2,256,256]{2,0,1:T(2,128)(2,1)}, u32[]{:S(2)}, u32[]{:S(2)}) async-start(bf16[2,256,256]{2,0,1:T(2,128)(2,1)} %copy.124), calls=%async_computation.5 | async-start | bytes 524288 | tf_op jit(solution)/shard_map/all_to_all | solution.py:71
  165.4 17.8 %all-to-all-start.7 = ((bf16[2,256,256]{2,0,1:T(2,128)(2,1)}), bf16[2,256,256]{2,0,1:T(2,128)(2,1)}, u32[]{:S(2)}, u32[]{:S(2)}) async-start(bf16[2,256,256]{2,0,1:T(2,128)(2,1)} %copy.131), calls=%async_computation.7 | async-start | bytes 524288 | tf_op jit(solution)/shard_map/all_to_all | solution.py:121
  183.2 17.6 %all-to-all-start.8 = ((bf16[2,256,256]{2,0,1:T(2,128)(2,1)}), bf16[2,256,256]{2,0,1:T(2,128)(2,1)}, u32[]{:S(2)}, u32[]{:S(2)}) async-start(bf16[2,256,256]{2,0,1:T(2,128)(2,1)} %copy.136), calls=%async_computation.8 | async-start | bytes 524288 | tf_op jit(solution)/shard_map/all_to_all | solution.py:122
  191.2 0.7 copy-start.13
  204.7 2.5 copy-start.3
  204.7 2.5 copy-start.26
  204.7 2.5 copy-start.33
  207.2 0.7 copy-start.28
  207.2 0.8 copy-start.29
  207.2 0.9 copy-start.30
  207.2 0.9 copy-start.31
  207.2 1.4 copy-start.21
  207.3 1.5 copy-start.27
  208.1 2.6 copy-start.22
  209.7 0.7 copy-start.18
  211.8 18.4 %all-to-all-start.9 = ((bf16[128,4,256]{2,1,0:T(4,128)(2,1)}), bf16[128,4,256]{2,1,0:T(4,128)(2,1)}, u32[]{:S(2)}, u32[]{:S(2)}) async-start(bf16[128,4,256]{2,1,0:T(4,128)(2,1)} %copy.145), calls=%async_computation.9 | async-start | bytes 524288 | tf_op jit(solution)/shard_map/all_to_all | solution.py:118
  221.3 20.3 %copy-start.12 = (bf16[4,256,128]{1,2,0:T(8,128)(2,1)S(1)}, bf16[4,256,128]{1,2,0:T(8,128)(2,1)}, u32[]{:S(2)}) copy-start(bf16[4,256,128]{1,2,0:T(8,128)(2,1)} %copy-done.11) | copy-start | bytes 786436
  221.3 20.3 %copy-start.14 = (bf16[4,256,128]{1,2,0:T(8,128)(2,1)S(1)}, bf16[4,256,128]{1,2,0:T(8,128)(2,1)}, u32[]{:S(2)}) copy-start(bf16[4,256,128]{1,2,0:T(8,128)(2,1)} %copy-done.13) | copy-start | bytes 786436
  235.9 16.2 %all-to-all-start.10 = ((bf16[2,256,256]{2,0,1:T(2,128)(2,1)}), bf16[2,256,256]{2,0,1:T(2,128)(2,1)}, u32[]{:S(2)}, u32[]{:S(2)}) async-start(bf16[2,256,256]{2,0,1:T(2,128)(2,1)} %copy.147), calls=%async_computation.10 | async-start | bytes 524288 | tf_op jit(solution)/shard_map/all_to_all | solution.py:121
  241.9 2.3 copy-start.9
  241.9 2.3 copy-start.17
  241.9 15.7 %copy-start.6 = (bf16[1,4,256,128]{2,3,1,0:T(8,128)(2,1)S(1)}, bf16[1,4,256,128]{2,3,1,0:T(8,128)(2,1)}, u32[]{:S(2)}) copy-start(bf16[1,4,256,128]{2,3,1,0:T(8,128)(2,1)} %copy-done.5) | copy-start | bytes 786436
  244.2 17.0 %copy-start.19 = (bf16[4,256,128]{1,2,0:T(8,128)(2,1)S(1)}, bf16[4,256,128]{1,2,0:T(8,128)(2,1)}, u32[]{:S(2)}) copy-start(bf16[4,256,128]{1,2,0:T(8,128)(2,1)} %copy-done.18) | copy-start | bytes 786436
  252.1 16.0 %all-to-all-start.11 = ((bf16[2,256,256]{2,0,1:T(2,128)(2,1)}), bf16[2,256,256]{2,0,1:T(2,128)(2,1)}, u32[]{:S(2)}, u32[]{:S(2)}) async-start(bf16[2,256,256]{2,0,1:T(2,128)(2,1)} %copy.152), calls=%async_computation.11 | async-start | bytes 524288 | tf_op jit(solution)/shard_map/all_to_all | solution.py:122
  257.5 292.0 %all-reduce.3.cloned.1.call-start = ((), (), s32[]{:S(2)}) async-start(), calls=%async_computation.12 | async-start | bytes 1572864 | tf_op jit(solution)/shard_map/psum | solution.py:162
  257.6 4.5 copy-start.24
  271.9 1.0 copy-start.7
  271.9 1.1 copy-start.25
  271.9 1.1 copy-start.34
  273.0 0.8 copy-start.36
  273.0 1.6 copy-start.4
  273.0 1.6 copy-start.23
Sparse Core Ops, SparseCore 0:
  274.8 274.6 all-reduce.2
where the time goes:
time: 565 us; the launch traced here: 563 us
  waiting for transfers between devices  354 us (63%)
  starting transfers between devices  73 us (13%)
  local copies, waits for them, and re-layouts  41.6 us (7%)
  blocking collectives  34.4 us (6%)
  matrix products  25.5 us (5%)
  other arithmetic  19.7 us (3%)
  between operations  14.8 us (3%)
    psum x1, waiting for transfers between devices, local(): lax.psum((grad_oi, grad_oo, grad_ii, grad_io), ('rep', 'dap'))  274 us
    all_to_all x2, waiting for transfers between devices, module_forward(): lax.all_to_all(right_op, 'dap', split_axis=0, concat_axis=1, tiled=True)  21.5 us
    all_to_all x2, starting transfers between devices, module_forward(): lax.all_to_all(right_op, 'dap', split_axis=0, concat_axis=1, tiled=True)  21.3 us
    all_to_all x2, waiting for transfers between devices, module_forward(): lax.all_to_all(left_op, 'dap', split_axis=0, concat_axis=1, tiled=True)  21.1 us
    all_to_all x1, blocking collectives, module_forward(): lax.all_to_all(product, 'dap', split_axis=1, concat_axis=0, tiled=True)  17.3 us
    all_to_all x1, blocking collectives, module_backward(): lax.all_to_all(grad_prod, 'dap', split_axis=0, concat_axis=1, tiled=True)  17.1 us
    all_to_all x2, waiting for transfers between devices, module_backward(): lax.all_to_all(grad_left, 'dap', split_axis=1, concat_axis=0, tiled=True)  15.4 us
    all_to_all x2, starting transfers between devices, module_forward(): lax.all_to_all(left_op, 'dap', split_axis=0, concat_axis=1, tiled=True)  12.7 us
  transfers between devices with their start and end apart: 11, of which 11 were waited for; matrix products, arithmetic and copies ran while one was open for 5% of the time, Pallas kernels for 0%

commit v1 on v0

v1 whole, which is shorter than its diff:
```python
import math

import jax
import jax.numpy as jnp
from jax import lax
from jax.experimental import pallas as pl
from jax.experimental.pallas import tpu as pltpu
from jax.sharding import PartitionSpec as P

EPS = 1e-05
ROWS = 4
N = 256
C = 128
BF = jnp.bfloat16
F32 = jnp.float32
VMEM_LIMIT = 48 * 1024 * 1024


def dot(a, b, ca, cb):
    return lax.dot_general(a, b, (((ca,), (cb,)), ((), ())), preferred_element_type=F32)


def swap():
    row = lax.broadcasted_iota(jnp.int32, (256, 256), 0)
    col = lax.broadcasted_iota(jnp.int32, (256, 256), 1)
    hit = ((row & 15) == (col >> 4)) & ((row >> 4) == (col & 15))
    return jnp.where(hit, 1.0, 0.0).astype(BF)


def column_order():
    row = lax.broadcasted_iota(jnp.int32, (N, N), 0)
    col = lax.broadcasted_iota(jnp.int32, (N, N), 1)
    return jnp.where(col == 4 * (row & 63) + (row >> 6), 1.0, 0.0).astype(BF)


def norm(x):
    centred = x - jnp.mean(x, axis=0, keepdims=True)
    inv = lax.rsqrt(jnp.mean(centred * centred, axis=0, keepdims=True) + EPS)
    return centred * inv, inv


def norm_back(normed, inv, grad):
    first = jnp.mean(grad, axis=0, keepdims=True)
    second = jnp.mean(grad * normed, axis=0, keepdims=True)
    return inv * (grad - first - normed * second)


def pack(msg, piece):
    s = swap()
    for big in range(4):
        x = jnp.concatenate([piece(q, big) for q in range(16)], axis=0)
        msg[pl.ds(256 * big, 256), :] = dot(s, x, 1, 0).astype(BF)


def unpack(msg, put):
    s = swap()
    for big in range(4):
        y = dot(s, msg[pl.ds(256 * big, 256), :], 1, 0).astype(BF)
        for q in range(16):
            put(q, big, y[16 * q : 16 * q + 16, :])


def pack_pair(msg, cells):
    def piece(q, big):
        t, m, r = q // 8, (q // 4) % 2, q % 4
        return cells[pl.ds((t * ROWS + r) * C + m * 64 + 16 * big, 16), :]

    pack(msg, piece)


def unpack_pair(msg, cells):
    def put(q, big, rows):
        t, m, r = q // 8, (q // 4) % 2, q % 4
        cells[pl.ds((t * ROWS + r) * C + m * 64 + 16 * big, 16), :] = rows

    unpack(msg, put)


def pack_one(msg, cells):
    def piece(q, big):
        h, m, r = q // 8, (q // 4) % 2, q % 4
        return cells[pl.ds(r * C + m * 64 + 16 * big, 16), pl.ds(128 * h, 128)]

    pack(msg, piece)


def unpack_one(msg, cells):
    def put(q, big, rows):
        h, m, r = q // 8, (q // 4) % 2, q % 4
        cells[pl.ds(r * C + m * 64 + 16 * big, 16), pl.ds(128 * h, 128)] = rows

    unpack(msg, put)


def row(ref, r):
    return ref[pl.ds(r * C, C), :]


def gated(nb, w):
    pre = dot(w[:, : 4 * C], nb, 0, 0)
    return pre[:C], jax.nn.sigmoid(pre[C : 2 * C]), pre[2 * C : 3 * C], jax.nn.sigmoid(pre[3 * C :])


def gate_of(nb, w):
    return jax.nn.sigmoid(dot(w[:, 4 * C :], nb, 0, 0))


def operands(state, w, r, cells):
    normed, _ = norm(state)
    left, left_s, right, right_s = gated(normed.astype(BF), w)
    cells[pl.ds(r * C, C), :] = (left_s * left).astype(BF)
    cells[pl.ds((ROWS + r) * C, C), :] = (right_s * right).astype(BF)


def first_kernel(u, w1, msg, u_t, cells):
    order = column_order()
    w = w1[...]
    for r in range(ROWS):
        state = dot(u[r], order, 0, 1)
        u_t[pl.ds(r * C, C), :] = state.astype(BF)
        operands(state, w, r, cells)
    pack_pair(msg, cells)


def product_kernel(incoming, msg, kept, out, prod):
    def put(q, big, rows):
        t, m, r = q // 8, (q // 4) % 2, q % 4
        kept[pl.ds((2 * t + m) * N + 64 * r + 16 * big, 16), :] = rows

    unpack(msg, put)
    over = 0 if incoming else 1
    for m in range(2):
        left = kept[pl.ds(m * N, N), :]
        right = kept[pl.ds((2 + m) * N, N), :]
        prod[pl.ds(m * N, N), :] = dot(left, right, over, over).astype(BF)

    def piece(q, big):
        h, m, r = q // 8, (q // 4) % 2, q % 4
        return prod[pl.ds(m * N + 64 * r + 16 * big, 16), pl.ds(128 * h, 128)]

    pack(out, piece)


def middle_kernel(pmsg, u_t, w1, v1, w2, msg, z1, prod, cells):
    unpack_one(pmsg, prod)
    w, v, w_next = w1[...], v1[...], w2[...]
    for r in range(ROWS):
        state = row(u_t, r).astype(F32)
        gate = gate_of(norm(state)[0].astype(BF), w)
        out_bf = norm(row(prod, r).astype(F32))[0].astype(BF)
        state = state + gate * dot(v, out_bf, 0, 0)
        z1[pl.ds(r * C, C), :] = state
        operands(state, w_next, r, cells)
    pack_pair(msg, cells)


def cotangent_kernel(cot, z1, w2, v2, cot_t, mix, grad_on):
    order = column_order()
    w, v = w2[...], v2[...]
    for r in range(ROWS):
        grad_u = dot(cot[r], order, 0, 1)
        cot_t[pl.ds(r * C, C), :] = grad_u.astype(BF)
        gate = gate_of(norm(row(z1, r))[0].astype(BF), w)
        grad_mix = (grad_u * gate).astype(BF)
        mix[pl.ds(r * C, C), :] = grad_mix
        grad_on[pl.ds(r * C, C), :] = dot(v, grad_mix, 1, 0)


def turn_kernel(pmsg, grad_on, msg, prod, cells):
    unpack_one(pmsg, prod)
    for r in range(ROWS):
        normed, inv = norm(row(prod, r).astype(F32))
        cells[pl.ds(r * C, C), :] = norm_back(normed, inv, row(grad_on, r)).astype(BF)
    pack_one(msg, cells)


def gate_grads(grad_u, mix, prod, state, w, v):
    nb = norm(state)[0].astype(BF)
    gate = gate_of(nb, w)
    out_bf = norm(prod.astype(F32))[0].astype(BF)
    mixed = dot(v, out_bf, 0, 0)
    grad_gate = (grad_u * mixed * gate * (1.0 - gate)).astype(BF)
    return grad_gate, dot(out_bf, mix, 1, 1), dot(nb, grad_gate, 1, 1)


def late_kernel(grad_u, mix, prod, state, w_ref, v_ref, grad_gate, sums):
    w, v = w_ref[...], v_ref[...]
    grad_v = grad_w = 0.0
    for r in range(ROWS):
        gg, gv, gw = gate_grads(
            row(grad_u, r).astype(F32), row(mix, r), row(prod, r), row(state, r).astype(F32), w, v
        )
        grad_gate[pl.ds(r * C, C), :] = gg
        grad_v = grad_v + gv
        grad_w = grad_w + gw
    sums[pl.ds(0, C), :] = grad_w.astype(BF)
    sums[pl.ds(C, C), :] = grad_v.astype(BF)


def grads_kernel(incoming, gmsg, kept, msg, prod, sides):
    def put(q, big, rows):
        h, m, r = q // 8, (q // 4) % 2, q % 4
        prod[pl.ds(m * N + 64 * r + 16 * big, 16), pl.ds(128 * h, 128)] = rows

    unpack(gmsg, put)
    for m in range(2):
        left = kept[pl.ds(m * N, N), :]
        right = kept[pl.ds((2 + m) * N, N), :]
        grad = prod[pl.ds(m * N, N), :]
        if incoming:
            grad_left, grad_right = dot(right, grad, 1, 1), dot(left, grad, 1, 0)
        else:
            grad_left, grad_right = dot(grad, right, 1, 0), dot(grad, left, 0, 0)
        sides[pl.ds(m * N, N), :] = grad_left.astype(BF)
        sides[pl.ds((2 + m) * N, N), :] = grad_right.astype(BF)

    def piece(q, big):
        t, m, r = q // 8, (q // 4) % 2, q % 4
        return sides[pl.ds((2 * t + m) * N + 64 * r + 16 * big, 16), :]

    pack(msg, piece)


def project_grad(cells, r, nb, w):
    left, left_s, right, right_s = gated(nb, w)
    grad_left = cells[pl.ds(r * C, C), :].astype(F32) * left_s
    grad_right = cells[pl.ds((ROWS + r) * C, C), :].astype(F32) * right_s
    return jnp.concatenate(
        [
            grad_left.astype(BF),
            (grad_left * left * (1.0 - left_s)).astype(BF),
            grad_right.astype(BF),
            (grad_right * right * (1.0 - right_s)).astype(BF),
        ],
        0,
    )


def input_grad(grad_u, normed, inv, grad_proj, grad_gate, w):
    grad = dot(w[:, : 4 * C], grad_proj, 1, 0) + dot(w[:, 4 * C :], grad_gate, 1, 0)
    return grad_u + norm_back(normed, inv, grad)


def back_kernel(
    gmsg, z1, gg2, cot_t, w2, u_t, prod1, w1, v1, msg, proj, grad_u, mix, cells, grad_prod
):
    unpack_pair(gmsg, cells)
    w_in, w, v = w2[...], w1[...], v1[...]
    for r in range(ROWS):
        normed, inv = norm(row(z1, r))
        grad_proj = project_grad(cells, r, normed.astype(BF), w_in)
        proj[pl.ds(4 * r * C, 4 * C), :] = grad_proj
        grad = input_grad(row(cot_t, r).astype(F32), normed, inv, grad_proj, row(gg2, r), w_in)
        grad_u[pl.ds(r * C, C), :] = grad
        gate = gate_of(norm(row(u_t, r).astype(F32))[0].astype(BF), w)
        grad_mix = (grad * gate).astype(BF)
        mix[pl.ds(r * C, C), :] = grad_mix
        normed, inv = norm(row(prod1, r).astype(F32))
        grad_prod[pl.ds(r * C, C), :] = norm_back(normed, inv, dot(v, grad_mix, 1, 0)).astype(BF)
    pack_one(msg, grad_prod)


def weight_kernel(state, proj, sums):
    total = 0.0
    for r in range(ROWS):
        nb = norm(row(state, r).astype(F32))[0].astype(BF)
        total = total + dot(proj[pl.ds(4 * r * C, 4 * C), :], nb, 1, 1)
    sums[...] = total.astype(BF)


def last_kernel(gmsg, u_t, w1, lr2, gv2, gv1, msg, proj, cells):
    unpack_pair(gmsg, cells)
    w = w1[...]
    total = 0.0
    for r in range(ROWS):
        nb = norm(row(u_t, r).astype(F32))[0].astype(BF)
        grad_proj = project_grad(cells, r, nb, w)
        proj[pl.ds(4 * r * C, 4 * C), :] = grad_proj
        total = total + dot(grad_proj, nb, 1, 1)
    msg[pl.ds(0, 4 * C), :] = total.astype(BF)
    msg[pl.ds(4 * C, 2 * C), :] = gv1[...]
    msg[pl.ds(6 * C, 4 * C), :] = lr2[...]
    msg[pl.ds(10 * C, 2 * C), :] = gv2[...]


def pair_kernel(u_t, proj, gg1, grad_u, w1, out):
    order = column_order()
    w = w1[...]
    for r in range(ROWS):
        normed, inv = norm(row(u_t, r).astype(F32))
        grad = input_grad(
            row(grad_u, r), normed, inv, proj[pl.ds(4 * r * C, 4 * C), :], row(gg1, r), w
        )
        out[r] = dot(order, grad.astype(BF), 0, 1).astype(BF)


def finish_kernel(sums, oi, oo, ii, io):
    for base, w, v in ((0, oi, oo), (6 * C, ii, io)):
        for b in range(4):
            w[:, pl.ds(b * C, C)] = sums[pl.ds(base + b * C, C), :].astype(F32).T
        w[:, pl.ds(4 * C, C)] = sums[pl.ds(base + 4 * C, C), :].astype(F32)
        v[...] = sums[pl.ds(base + 5 * C, C), :].astype(F32)


def call(kernel, outs, scratch, *args, name, flops=2e8):
    shapes = [jax.ShapeDtypeStruct(s, d) for s, d in outs]
    moved = sum(a.size * a.dtype.itemsize for a in args)
    moved += sum(s.size * s.dtype.itemsize for s in shapes)
    return pl.pallas_call(
        kernel,
        out_shape=shapes,
        scratch_shapes=[pltpu.VMEM(s, d) for s, d in scratch],
        compiler_params=pltpu.CompilerParams(vmem_limit_bytes=VMEM_LIMIT),
        cost_estimate=pl.CostEstimate(
            flops=int(flops), bytes_accessed=int(moved), transcendentals=0
        ),
        name=name,
    )(*args)


def exchange(msg):
    shape = msg.shape
    out = lax.all_to_all(msg.reshape(64, 16, shape[1]), "dap", 0, 0, tiled=True)
    return out.reshape(shape)


ONE = (ROWS * C, N)
TWO = (2 * ROWS * C, N)
ONE_MSG = (64 * 16, 128)
TWO_MSG = (64 * 16, 256)
PROJ = (4 * ROWS * C, N)


def product(msg, incoming):
    def kernel(*refs):
        product_kernel(incoming, *refs)

    return call(
        kernel, [((4 * N, N), BF), (ONE_MSG, BF)], [((2 * N, N), BF)], msg, name="product"
    )


def grads(gmsg, kept, incoming):
    def kernel(*refs):
        grads_kernel(incoming, *refs)

    return call(
        kernel, [(TWO_MSG, BF)], [((2 * N, N), BF), ((4 * N, N), BF)], gmsg, kept, name="grads"
    )[0]


def local(pair_act, cotangent, w1, v1, w2, v2):
    lr1, u_t = call(
        first_kernel, [(TWO_MSG, BF), (ONE, BF)], [(TWO, BF)], pair_act[0], w1, name="first"
    )
    kept1, pmsg1 = product(exchange(lr1), False)
    lr2, z1, prod1 = call(
        middle_kernel,
        [(TWO_MSG, BF), (ONE, F32), (ONE, BF)],
        [(TWO, BF)],
        exchange(pmsg1), u_t, w1, v1, w2,
        name="middle",
    )
    cot_t, mix2, grad_on2 = call(
        cotangent_kernel,
        [(ONE, BF), (ONE, BF), (ONE, F32)],
        [],
        cotangent[0], z1, w2, v2,
        name="cotangent",
    )
    kept2, pmsg2 = product(exchange(lr2), True)
    gmsg2, prod2 = call(
        turn_kernel, [(ONE_MSG, BF), (ONE, BF)], [(ONE, BF)], exchange(pmsg2), grad_on2, name="turn"
    )
    gg2, gv2 = call(
        late_kernel,
        [(ONE, BF), ((2 * C, C), BF)],
        [],
        cot_t, mix2, prod2, z1, w2, v2,
        name="late_incoming",
    )
    gsides2 = grads(exchange(gmsg2), kept2, True)
    gmsg1, proj2, grad_u1, mix1 = call(
        back_kernel,
        [(ONE_MSG, BF), (PROJ, BF), (ONE, F32), (ONE, BF)],
        [(TWO, BF), (ONE, BF)],
        exchange(gsides2), z1, gg2, cot_t, w2, u_t, prod1, w1, v1,
        name="back",
    )
    sums2 = call(weight_kernel, [((4 * C, C), BF)], [], z1, proj2, name="weights_incoming")[0]
    gg1, gv1 = call(
        late_kernel,
        [(ONE, BF), ((2 * C, C), BF)],
        [],
        grad_u1, mix1, prod1, u_t, w1, v1,
        name="late_outgoing",
    )
    gsides1 = grads(exchange(gmsg1), kept1, False)
    wmsg, proj1 = call(
        last_kernel,
        [((12 * C, C), BF), (PROJ, BF)],
        [(TWO, BF)],
        exchange(gsides1), u_t, w1, sums2, gv2, gv1,
        name="last",
    )
    pair_grad = call(
        pair_kernel, [((ROWS, N, C), BF)], [], u_t, proj1, gg1, grad_u1, w1, name="pair"
    )[0]

    scale = 1.0 / math.sqrt(lax.axis_size("rep") * pair_act.shape[0] * N * N)
    parts = lax.all_to_all(wmsg.reshape(64, 24, C), "dap", 0, 0, tiled=True)
    part = jnp.sum(parts.astype(F32), axis=0)
    reps = lax.axis_size("rep")
    across = lax.all_to_all(jnp.broadcast_to(part, (reps, 24, C)), "rep", 0, 0, tiled=True)
    whole = (jnp.sum(across, axis=0) * scale).astype(BF)
    everywhere = lax.all_to_all(jnp.broadcast_to(whole, (64, 24, C)), "dap", 0, 0, tiled=True)
    oi, oo, ii, io = call(
        finish_kernel,
        [((C, 5 * C), F32), ((C, C), F32), ((C, 5 * C), F32), ((C, C), F32)],
        [],
        everywhere.reshape(12 * C, C),
        name="finish",
    )
    return pair_grad[None], oi, oo, ii, io


def solution(mesh):
    return jax.shard_map(
        local,
        mesh=mesh,
        in_specs=(P("rep", "dap", None, None), P("rep", "dap", None, None), P(), P(), P(), P()),
        out_specs=(P("rep", "dap", None, None), P(), P(), P(), P()),
        check_vma=False,
    )
```

time: 565 us -> 248 us (0.44)
  the two profiles are of different devices: /device:TPU:17 before, /device:TPU:8 now
where the time goes in v1:
time: 248 us; the launch traced here: 247 us
  blocking collectives  144 us (58%)
  waiting for transfers between devices  56.9 us (23%)
  starting transfers between devices  20.6 us (8%)
  Pallas kernels  19.6 us (8%)
  local copies, waits for them, and re-layouts  4.76 us (2%)
    all_to_all x5, blocking collectives, exchange(): out = lax.all_to_all(msg.reshape(64, 16, shape[1]), 'dap', 0, 0, tiled=True)  109 us
    all_to_all x3, waiting for transfers between devices, exchange(): out = lax.all_to_all(msg.reshape(64, 16, shape[1]), 'dap', 0, 0, tiled=True)  43.7 us
    all_to_all x1, blocking collectives, local(): parts = lax.all_to_all(wmsg.reshape(64, 24, C), 'dap', 0, 0, tiled=True)  20.6 us
    pallas_call x15, Pallas kernels, call(): pl.pallas_call(kernel, out_shape=shapes, scratch_shapes=[pltpu.VMEM(s, d)...  19.6 us
    all_to_all x3, starting transfers between devices, exchange(): out = lax.all_to_all(msg.reshape(64, 16, shape[1]), 'dap', 0, 0, tiled=True)  15.5 us
    all_to_all x1, blocking collectives, local(): lax.all_to_all(jnp.broadcast_to(part, (reps, 24, C)), 'rep', 0, 0, tiled=...  14.9 us
    all_to_all x1, waiting for transfers between devices, local(): lax.all_to_all(jnp.broadcast_to(whole, (64, 24, C)), 'dap', 0, 0, tiled=T...  13.2 us
    all_to_all x1, starting transfers between devices, local(): lax.all_to_all(jnp.broadcast_to(whole, (64, 24, C)), 'dap', 0, 0, tiled=T...  5.08 us
  transfers between devices with their start and end apart: 4, of which 4 were waited for; matrix products, arithmetic and copies ran while one was open for 0% of the time, Pallas kernels for 2%

profile of v1, /device:TPU:8, one launch (start us, length us, event | category | flops | bytes accessed | tf_op | source)
XLA Modules:
  0.0 247.1 jit_solution(4375912058450217)
XLA Ops:
  0.6 0.0 copy-start
  0.6 0.9 copy-done
  1.6 0.9 copy-done.16
  2.5 1.3 first.1
  3.8 32.7 %all_to_all.55 = bf16[64,16,256]{2,1,0:T(8,128)(2,1)S(1)} all-to-all(bf16[64,16,256]{2,1,0:T(8,128)(2,1)S(1)} %bitcast.30), channel_id=1, replica_groups=mesh['rep'=8,'dap'=64] {'dap'}, dimensions={0} | all-to-all | bytes 1048576 | tf_op jit(solution)/shard_map/all_to_all | solution.py:323
  36.5 0.8 product.2
  37.4 0.0 copy-start.5
  37.4 0.0 copy-start.1
  37.4 0.0 copy-start.2
  37.4 0.0 copy-start.7
  37.4 18.2 %all_to_all.56 = bf16[64,16,128]{2,1,0:T(8,128)(2,1)S(1)} all-to-all(bf16[64,16,128]{2,1,0:T(8,128)(2,1)S(1)} %bitcast.35), channel_id=1, replica_groups=mesh['rep'=8,'dap'=64] {'dap'}, dimensions={0} | all-to-all | bytes 524288 | tf_op jit(solution)/shard_map/all_to_all | solution.py:323
  55.6 0.0 copy-done.5
  55.6 0.0 copy-done.1
  55.6 1.7 middle.1
  57.3 22.4 %all_to_all.57 = bf16[64,16,256]{2,1,0:T(8,128)(2,1)S(1)} all-to-all(bf16[64,16,256]{2,1,0:T(8,128)(2,1)S(1)} %bitcast.27), channel_id=1, replica_groups=mesh['rep'=8,'dap'=64] {'dap'}, dimensions={0} | all-to-all | bytes 1048576 | tf_op jit(solution)/shard_map/all_to_all | solution.py:323
  79.7 1.5 product.3
  81.2 5.6 %all-to-all-start.3 = ((bf16[64,16,128]{2,1,0:T(8,128)(2,1)}), bf16[64,16,128]{2,1,0:T(8,128)(2,1)S(1)}, u32[]{:S(2)}, u32[]{:S(2)}) async-start(bf16[64,16,128]{2,1,0:T(8,128)(2,1)} %bitcast.7), calls=%async_computation.3 | async-start | bytes 524288 | tf_op jit(solution)/shard_map/all_to_all | solution.py:323
  86.8 1.0 cotangent.1
  87.9 11.8 %all-to-all-done.3 = bf16[64,16,128]{2,1,0:T(8,128)(2,1)S(1)} async-done(((bf16[64,16,128]{2,1,0:T(8,128)(2,1)}), bf16[64,16,128]{2,1,0:T(8,128)(2,1)S(1)}, u32[]{:S(2)}, u32[]{:S(2)}) %all-to-all-start.3) | async-done | bytes 262176 | tf_op jit(solution)/shard_map/all_to_all | solution.py:323
  99.6 0.9 turn.1
  100.5 0.0 copy-start.11
  100.5 17.4 %all_to_all.58 = bf16[64,16,128]{2,1,0:T(8,128)(2,1)S(1)} all-to-all(bf16[64,16,128]{2,1,0:T(8,128)(2,1)S(1)} %bitcast.34), channel_id=1, replica_groups=mesh['rep'=8,'dap'=64] {'dap'}, dimensions={0} | all-to-all | bytes 524288 | tf_op jit(solution)/shard_map/all_to_all | solution.py:323
  117.9 1.7 grads.2
  119.6 5.0 %all-to-all-start.5 = ((bf16[64,16,256]{2,1,0:T(8,128)(2,1)}), bf16[64,16,256]{2,1,0:T(8,128)(2,1)S(1)}, u32[]{:S(2)}, u32[]{:S(2)}) async-start(bf16[64,16,256]{2,1,0:T(8,128)(2,1)} %bitcast.12), calls=%async_computation.5 | async-start | bytes 1048576 | tf_op jit(solution)/shard_map/all_to_all | solution.py:323
  124.7 0.9 late_incoming.1
  125.6 0.0 copy-start.14
  125.6 0.6 copy-done.14
  126.2 16.1 %all-to-all-done.5 = bf16[64,16,256]{2,1,0:T(8,128)(2,1)S(1)} async-done(((bf16[64,16,256]{2,1,0:T(8,128)(2,1)}), bf16[64,16,256]{2,1,0:T(8,128)(2,1)S(1)}, u32[]{:S(2)}, u32[]{:S(2)}) %all-to-all-start.5) | async-done | bytes 524320 | tf_op jit(solution)/shard_map/all_to_all | solution.py:323
  142.3 2.4 back.1
  144.7 1.0 copy-done.3
  145.7 18.2 %all_to_all.59 = bf16[64,16,128]{2,1,0:T(8,128)(2,1)S(1)} all-to-all(bf16[64,16,128]{2,1,0:T(8,128)(2,1)S(1)} %bitcast.33), channel_id=1, replica_groups=mesh['rep'=8,'dap'=64] {'dap'}, dimensions={0} | all-to-all | bytes 524288 | tf_op jit(solution)/shard_map/all_to_all | solution.py:323
  163.9 1.7 grads.3
  165.5 4.9 %all-to-all-start.7 = ((bf16[64,16,256]{2,1,0:T(8,128)(2,1)}), bf16[64,16,256]{2,1,0:T(8,128)(2,1)S(1)}, u32[]{:S(2)}, u32[]{:S(2)}) async-start(bf16[64,16,256]{2,1,0:T(8,128)(2,1)} %bitcast.16), calls=%async_computation.7 | async-start | bytes 1048576 | tf_op jit(solution)/shard_map/all_to_all | solution.py:323
  170.4 0.0 copy-start.10
  170.4 0.5 weights_incoming.1.lr2
  171.0 0.4 copy-done.10
  171.4 0.9 late_outgoing.1
  172.3 15.8 %all-to-all-done.7 = bf16[64,16,256]{2,1,0:T(8,128)(2,1)S(1)} async-done(((bf16[64,16,256]{2,1,0:T(8,128)(2,1)}), bf16[64,16,256]{2,1,0:T(8,128)(2,1)S(1)}, u32[]{:S(2)}, u32[]{:S(2)}) %all-to-all-start.7) | async-done | bytes 524320 | tf_op jit(solution)/shard_map/all_to_all | solution.py:323
  188.2 0.0 copy-done.15
  188.2 1.2 last.1
  189.3 20.6 %all_to_all.60 = bf16[64,24,128]{2,1,0:T(8,128)(2,1)S(1)} all-to-all(bf16[64,24,128]{2,1,0:T(8,128)(2,1)S(1)} %bitcast.32), channel_id=1, replica_groups=mesh['rep'=8,'dap'=64] {'dap'}, dimensions={0} | all-to-all | bytes 786432 | tf_op jit(solution)/shard_map/all_to_all | solution.py:411
  209.9 0.1 convert_reduce_fusion
  210.0 14.9 %all_to_all.61 = f32[8,24,128]{2,1,0:T(8,128)S(1)} all-to-all(f32[8,24,128]{2,1,0:T(8,128)S(1)} %broadcast_in_dim.10), channel_id=1, replica_groups=mesh['rep'=8,'dap'=64] {'rep'}, dimensions={0} | all-to-all | bytes 196608 | tf_op jit(solution)/shard_map/all_to_all | solution.py:414
  224.9 0.8 broadcast_in_dim.11
  225.7 5.1 %all-to-all-start.10 = ((bf16[64,24,128]{2,1,0:T(8,128)(2,1)}), bf16[64,24,128]{2,1,0:T(8,128)(2,1)S(1)}, u32[]{:S(2)}, u32[]{:S(2)}) async-start(bf16[64,24,128]{2,1,0:T(8,128)(2,1)} %broadcast_in_dim.11), calls=%async_computation.10 | async-start | bytes 786432 | tf_op jit(solution)/shard_map/all_to_all | solution.py:416
  230.8 2.2 pair.1
  233.0 13.2 %all-to-all-done.10 = bf16[64,24,128]{2,1,0:T(8,128)(2,1)S(1)} async-done(((bf16[64,24,128]{2,1,0:T(8,128)(2,1)}), bf16[64,24,128]{2,1,0:T(8,128)(2,1)S(1)}, u32[]{:S(2)}, u32[]{:S(2)}) %all-to-all-start.10) | async-done | bytes 393248 | tf_op jit(solution)/shard_map/all_to_all | solution.py:416
  246.2 0.9 finish.1
  (21 shorter events, 0.1 us)
Async XLA Ops:
  0.6 0.9 copy-start
  1.5 0.9 copy-start.16
  37.4 18.3 %copy-start.5 = (bf16[1024,256]{1,0:T(8,128)(2,1)}, bf16[1024,256]{1,0:T(8,128)(2,1)S(1)}, u32[]{:S(2)}) copy-start(bf16[1024,256]{1,0:T(8,128)(2,1)S(1)} %get-tuple-element.48.refs_1_) | copy-start | bytes 1572868
  37.4 18.2 %copy-start.1 = (bf16[128,640]{1,0:T(8,128)(2,1)S(1)}, bf16[128,640]{1,0:T(8,128)(2,1)}, u32[]{:S(2)}) copy-start(bf16[128,640]{1,0:T(8,128)(2,1)} %w1.9) | copy-start | bytes 491524
  37.4 18.2 %copy-start.2 = (bf16[128,640]{1,0:T(8,128)(2,1)S(1)}, bf16[128,640]{1,0:T(8,128)(2,1)}, u32[]{:S(2)}) copy-start(bf16[128,640]{1,0:T(8,128)(2,1)} %w2.5) | copy-start | bytes 491524
  37.4 18.2 %copy-start.7 = (bf16[128,128]{1,0:T(8,128)(2,1)S(1)}, bf16[128,128]{1,0:T(8,128)(2,1)}, u32[]{:S(2)}) copy-start(bf16[128,128]{1,0:T(8,128)(2,1)} %v_ref.3) | copy-start | bytes 98308
  81.2 5.6 %copy-start.8 = (bf16[1,4,256,128]{3,2,1,0:T(8,128)(2,1)S(1)}, bf16[1,4,256,128]{3,2,1,0:T(8,128)(2,1)}, u32[]{:S(2)}) copy-start(bf16[1,4,256,128]{3,2,1,0:T(8,128)(2,1)} %param.7) | copy-start | bytes 786436
  81.2 5.6 %copy-start.13 = (bf16[128,128]{1,0:T(8,128)(2,1)S(1)}, bf16[128,128]{1,0:T(8,128)(2,1)}, u32[]{:S(2)}) copy-start(bf16[128,128]{1,0:T(8,128)(2,1)} %v_ref.2) | copy-start | bytes 98308
  81.2 18.4 %all-to-all-start.3 = ((bf16[64,16,128]{2,1,0:T(8,128)(2,1)}), bf16[64,16,128]{2,1,0:T(8,128)(2,1)S(1)}, u32[]{:S(2)}, u32[]{:S(2)}) async-start(bf16[64,16,128]{2,1,0:T(8,128)(2,1)} %bitcast.7), calls=%async_computation.3 | async-start | bytes 524288 | tf_op jit(solution)/shard_map/all_to_all | solution.py:323
  100.5 17.4 %copy-start.11 = (bf16[512,256]{1,0:T(8,128)(2,1)}, bf16[512,256]{1,0:T(8,128)(2,1)S(1)}, u32[]{:S(2)}) copy-start(bf16[512,256]{1,0:T(8,128)(2,1)S(1)} %get-tuple-element.44.prod) | copy-start | bytes 786436
  119.6 5.1 %copy-start.12 = (bf16[512,256]{1,0:T(8,128)(2,1)S(1)}, bf16[512,256]{1,0:T(8,128)(2,1)}, u32[]{:S(2)}) copy-start(bf16[512,256]{1,0:T(8,128)(2,1)} %copy-done.11) | copy-start | bytes 786436
  119.6 22.7 %all-to-all-start.5 = ((bf16[64,16,256]{2,1,0:T(8,128)(2,1)}), bf16[64,16,256]{2,1,0:T(8,128)(2,1)S(1)}, u32[]{:S(2)}, u32[]{:S(2)}) async-start(bf16[64,16,256]{2,1,0:T(8,128)(2,1)} %bitcast.12), calls=%async_computation.5 | async-start | bytes 1048576 | tf_op jit(solution)/shard_map/all_to_all | solution.py:323
  125.6 0.6 copy-start.14
  144.7 1.0 copy-start.3
  145.7 18.2 %copy-start.9 = (bf16[512,256]{1,0:T(8,128)(2,1)}, bf16[512,256]{1,0:T(8,128)(2,1)S(1)}, u32[]{:S(2)}) copy-start(bf16[512,256]{1,0:T(8,128)(2,1)S(1)} %get-tuple-element.52.mix) | copy-start | bytes 786436
  145.7 18.2 %copy-start.6 = (bf16[1024,256]{1,0:T(8,128)(2,1)S(1)}, bf16[1024,256]{1,0:T(8,128)(2,1)}, u32[]{:S(2)}) copy-start(bf16[1024,256]{1,0:T(8,128)(2,1)} %copy-done.5) | copy-start | bytes 1572868
  163.9 6.6 %copy-start.4 = (bf16[2048,256]{1,0:T(8,128)(2,1)S(1)}, bf16[2048,256]{1,0:T(8,128)(2,1)}, u32[]{:S(2)}) copy-start(bf16[2048,256]{1,0:T(8,128)(2,1)} %copy-done.3) | copy-start | bytes 3145732
  165.5 22.6 %all-to-all-start.7 = ((bf16[64,16,256]{2,1,0:T(8,128)(2,1)}), bf16[64,16,256]{2,1,0:T(8,128)(2,1)S(1)}, u32[]{:S(2)}, u32[]{:S(2)}) async-start(bf16[64,16,256]{2,1,0:T(8,128)(2,1)} %bitcast.16), calls=%async_computation.7 | async-start | bytes 1048576 | tf_op jit(solution)/shard_map/all_to_all | solution.py:323
  170.4 1.0 copy-start.10
  171.4 16.8 %copy-start.15 = (bf16[256,128]{1,0:T(8,128)(2,1)S(1)}, bf16[256,128]{1,0:T(8,128)(2,1)}, u32[]{:S(2)}) copy-start(bf16[256,128]{1,0:T(8,128)(2,1)} %copy-done.14) | copy-start | bytes 196612
  225.7 20.4 %all-to-all-start.10 = ((bf16[64,24,128]{2,1,0:T(8,128)(2,1)}), bf16[64,24,128]{2,1,0:T(8,128)(2,1)S(1)}, u32[]{:S(2)}, u32[]{:S(2)}) async-start(bf16[64,24,128]{2,1,0:T(8,128)(2,1)} %broadcast_in_dim.11), calls=%async_computation.10 | async-start | bytes 786432 | tf_op jit(solution)/shard_map/all_to_all | solution.py:416

commit v2 on v1

--- a/solution.py
+++ b/solution.py
@@ -112,7 +112,23 @@
     cells[pl.ds((ROWS + r) * C, C), :] = (right_s * right).astype(BF)
 
 
-def first_kernel(u, w1, msg, u_t, cells):
+def prepare(state, cot, w, order, r, cot_t, gate, nb, factors):
+    cot_t[pl.ds(r * C, C), :] = dot(cot[r], order, 0, 1).astype(BF)
+    normed_in = norm(state)[0].astype(BF)
+    nb[pl.ds(r * C, C), :] = normed_in
+    gate[pl.ds(r * C, C), :] = gate_of(normed_in, w)
+    store_factors(factors, r, gated(normed_in, w))
+
+
+def store_factors(factors, r, sides):
+    left, left_s, right, right_s = sides
+    for b, x in enumerate(
+        (left_s, left * left_s * (1.0 - left_s), right_s, right * right_s * (1.0 - right_s))
+    ):
+        factors[pl.ds((4 * r + b) * C, C), :] = x.astype(BF)
+
+
+def first_kernel(core, u, cot, w1, msg, u_t, cot_t, gate, nb, factors, cells):
     order = column_order()
     w = w1[...]
     for r in range(ROWS):
@@ -120,6 +136,27 @@
         u_t[pl.ds(r * C, C), :] = state.astype(BF)
         operands(state, w, r, cells)
     pack_pair(msg, cells)
+
+    @pl.when(core[0] == 0)
+    def _():
+        for r in range(ROWS):
+            prepare(row(u_t, r).astype(F32), cot, w, order, r, cot_t, gate, nb, factors)
+
+
+def second_kernel(core, u_t, cot, w1, *refs):
+    made, kept = refs[:4], refs[4:]
+
+    @pl.when(core[0] == 0)
+    def _():
+        for old, new in zip(made, kept):
+            new[...] = old[...]
+
+    @pl.when(core[0] != 0)
+    def _():
+        order = column_order()
+        w = w1[...]
+        for r in range(ROWS):
+            prepare(row(u_t, r).astype(F32), cot, w, order, r, *kept)
 
 
 def product_kernel(incoming, msg, kept, out, prod):
@@ -141,29 +178,25 @@
     pack(out, piece)
 
 
-def middle_kernel(pmsg, u_t, w1, v1, w2, msg, z1, prod, cells):
+def middle_kernel(pmsg, u_t, gate, v1, w2, msg, z1, prod, cells):
     unpack_one(pmsg, prod)
-    w, v, w_next = w1[...], v1[...], w2[...]
-    for r in range(ROWS):
-        state = row(u_t, r).astype(F32)
-        gate = gate_of(norm(state)[0].astype(BF), w)
+    v, w_next = v1[...], w2[...]
+    for r in range(ROWS):
         out_bf = norm(row(prod, r).astype(F32))[0].astype(BF)
-        state = state + gate * dot(v, out_bf, 0, 0)
+        state = row(u_t, r).astype(F32) + row(gate, r) * dot(v, out_bf, 0, 0)
         z1[pl.ds(r * C, C), :] = state
         operands(state, w_next, r, cells)
     pack_pair(msg, cells)
 
 
-def cotangent_kernel(cot, z1, w2, v2, cot_t, mix, grad_on):
-    order = column_order()
+def cotangent_kernel(cot_t, z1, w2, v2, mix, grad_on, factors):
     w, v = w2[...], v2[...]
     for r in range(ROWS):
-        grad_u = dot(cot[r], order, 0, 1)
-        cot_t[pl.ds(r * C, C), :] = grad_u.astype(BF)
-        gate = gate_of(norm(row(z1, r))[0].astype(BF), w)
-        grad_mix = (grad_u * gate).astype(BF)
+        nb = norm(row(z1, r))[0].astype(BF)
+        grad_mix = (row(cot_t, r).astype(F32) * gate_of(nb, w)).astype(BF)
         mix[pl.ds(r * C, C), :] = grad_mix
         grad_on[pl.ds(r * C, C), :] = dot(v, grad_mix, 1, 0)
+        store_factors(factors, r, gated(nb, w))
 
 
 def turn_kernel(pmsg, grad_on, msg, prod, cells):
@@ -221,19 +254,13 @@
     pack(msg, piece)
 
 
-def project_grad(cells, r, nb, w):
-    left, left_s, right, right_s = gated(nb, w)
-    grad_left = cells[pl.ds(r * C, C), :].astype(F32) * left_s
-    grad_right = cells[pl.ds((ROWS + r) * C, C), :].astype(F32) * right_s
-    return jnp.concatenate(
-        [
-            grad_left.astype(BF),
-            (grad_left * left * (1.0 - left_s)).astype(BF),
-            grad_right.astype(BF),
-            (grad_right * right * (1.0 - right_s)).astype(BF),
-        ],
-        0,
-    )
+def project_grad(cells, r, factors):
+    grad_left = cells[pl.ds(r * C, C), :].astype(F32)
+    grad_right = cells[pl.ds((ROWS + r) * C, C), :].astype(F32)
+    blocks = []
+    for b, grad in enumerate((grad_left, grad_left, grad_right, grad_right)):
+        blocks.append((grad * factors[pl.ds((4 * r + b) * C, C), :].astype(F32)).astype(BF))
+    return jnp.concatenate(blocks, 0)
 
 
 def input_grad(grad_u, normed, inv, grad_proj, grad_gate, w):
@@ -242,18 +269,17 @@
 
 
 def back_kernel(
-    gmsg, z1, gg2, cot_t, w2, u_t, prod1, w1, v1, msg, proj, grad_u, mix, cells, grad_prod
+    gmsg, z1, gg2, cot_t, factors2, w2, gate1, prod1, v1, msg, proj, grad_u, mix, cells, grad_prod
 ):
     unpack_pair(gmsg, cells)
-    w_in, w, v = w2[...], w1[...], v1[...]
+    w_in, v = w2[...], v1[...]
     for r in range(ROWS):
         normed, inv = norm(row(z1, r))
-        grad_proj = project_grad(cells, r, normed.astype(BF), w_in)
+        grad_proj = project_grad(cells, r, factors2)
         proj[pl.ds(4 * r * C, 4 * C), :] = grad_proj
         grad = input_grad(row(cot_t, r).astype(F32), normed, inv, grad_proj, row(gg2, r), w_in)
         grad_u[pl.ds(r * C, C), :] = grad
-        gate = gate_of(norm(row(u_t, r).astype(F32))[0].astype(BF), w)
-        grad_mix = (grad * gate).astype(BF)
+        grad_mix = (grad * row(gate1, r)).astype(BF)
         mix[pl.ds(r * C, C), :] = grad_mix
         normed, inv = norm(row(prod1, r).astype(F32))
         grad_prod[pl.ds(r * C, C), :] = norm_back(normed, inv, dot(v, grad_mix, 1, 0)).astype(BF)
@@ -268,15 +294,13 @@
     sums[...] = total.astype(BF)
 
 
-def last_kernel(gmsg, u_t, w1, lr2, gv2, gv1, msg, proj, cells):
+def last_kernel(gmsg, nb, factors1, lr2, gv2, gv1, msg, proj, cells):
     unpack_pair(gmsg, cells)
-    w = w1[...]
     total = 0.0
     for r in range(ROWS):
-        nb = norm(row(u_t, r).astype(F32))[0].astype(BF)
-        grad_proj = project_grad(cells, r, nb, w)
+        grad_proj = project_grad(cells, r, factors1)
         proj[pl.ds(4 * r * C, 4 * C), :] = grad_proj
-        total = total + dot(grad_proj, nb, 1, 1)
+        total = total + dot(grad_proj, row(nb, r), 1, 1)
     msg[pl.ds(0, 4 * C), :] = total.astype(BF)
     msg[pl.ds(4 * C, 2 * C), :] = gv1[...]
     msg[pl.ds(6 * C, 4 * C), :] = lr2[...]
@@ -302,13 +326,17 @@
         v[...] = sums[pl.ds(base + 5 * C, C), :].astype(F32)
 
 
-def call(kernel, outs, scratch, *args, name, flops=2e8):
+def call(kernel, outs, scratch, *args, name, flops=2e8, scalar=False):
     shapes = [jax.ShapeDtypeStruct(s, d) for s, d in outs]
     moved = sum(a.size * a.dtype.itemsize for a in args)
     moved += sum(s.size * s.dtype.itemsize for s in shapes)
     return pl.pallas_call(
         kernel,
         out_shape=shapes,
+        in_specs=[
+            pl.BlockSpec(memory_space=pltpu.SMEM if scalar and i == 0 else pltpu.VMEM)
+            for i in range(len(args))
+        ],
         scratch_shapes=[pltpu.VMEM(s, d) for s, d in scratch],
         compiler_params=pltpu.CompilerParams(vmem_limit_bytes=VMEM_LIMIT),
         cost_estimate=pl.CostEstimate(
@@ -350,22 +378,37 @@
 
 
 def local(pair_act, cotangent, w1, v1, w2, v2):
-    lr1, u_t = call(
-        first_kernel, [(TWO_MSG, BF), (ONE, BF)], [(TWO, BF)], pair_act[0], w1, name="first"
+    core = (lax.axis_index("rep") % 2).astype(jnp.int32).reshape(1)
+    prepared = [(ONE, BF), (ONE, F32), (ONE, BF), (PROJ, BF)]
+    lr1, u_t, *early = call(
+        first_kernel,
+        [(TWO_MSG, BF), (ONE, BF)] + prepared,
+        [(TWO, BF)],
+        core, pair_act[0], cotangent[0], w1,
+        name="first",
+        scalar=True,
+    )
+    cot_t, gate1, nb1, factors1 = call(
+        second_kernel,
+        prepared,
+        [],
+        core, u_t, cotangent[0], w1, *early,
+        name="second",
+        scalar=True,
     )
     kept1, pmsg1 = product(exchange(lr1), False)
     lr2, z1, prod1 = call(
         middle_kernel,
         [(TWO_MSG, BF), (ONE, F32), (ONE, BF)],
         [(TWO, BF)],
-        exchange(pmsg1), u_t, w1, v1, w2,
+        exchange(pmsg1), u_t, gate1, v1, w2,
         name="middle",
     )
-    cot_t, mix2, grad_on2 = call(
+    mix2, grad_on2, factors2 = call(
         cotangent_kernel,
-        [(ONE, BF), (ONE, BF), (ONE, F32)],
+        [(ONE, BF), (ONE, F32), (PROJ, BF)],
         [],
-        cotangent[0], z1, w2, v2,
+        cot_t, z1, w2, v2,
         name="cotangent",
     )
     kept2, pmsg2 = product(exchange(lr2), True)
@@ -384,7 +427,7 @@
         back_kernel,
         [(ONE_MSG, BF), (PROJ, BF), (ONE, F32), (ONE, BF)],
         [(TWO, BF), (ONE, BF)],
-        exchange(gsides2), z1, gg2, cot_t, w2, u_t, prod1, w1, v1,
+        exchange(gsides2), z1, gg2, cot_t, factors2, w2, gate1, prod1, v1,
         name="back",
     )
     sums2 = call(weight_kernel, [((4 * C, C), BF)], [], z1, proj2, name="weights_incoming")[0]
@@ -400,7 +443,7 @@
         last_kernel,
         [((12 * C, C), BF), (PROJ, BF)],
         [(TWO, BF)],
-        exchange(gsides1), u_t, w1, sums2, gv2, gv1,
+        exchange(gsides1), nb1, factors1, sums2, gv2, gv1,
         name="last",
     )
     pair_grad = call(

time: 248 us -> 255 us (1.028)
  blocking collectives: 144 us -> 126 us
  local copies, waits for them, and re-layouts: 4.76 us -> 16.3 us
  waiting for transfers between devices: 56.9 us -> 64.4 us
  starting transfers between devices: 20.6 us -> 26.1 us
    all_to_all x5 -> x4, blocking collectives: 109 us -> 90 us  [exchange(): out = lax.all_to_all(msg.reshape(64, 16, shape[1]), 'dap', 0, 0, tiled=True)]
    unnamed x34 -> x60, local copies, waits for them, and re-layouts: 3.94 us -> 15.5 us
    all_to_all x3 -> x4, waiting for transfers between devices: 43.7 us -> 51.3 us  [exchange(): out = lax.all_to_all(msg.reshape(64, 16, shape[1]), 'dap', 0, 0, tiled=True)]
    all_to_all x3 -> x4, starting transfers between devices: 15.5 us -> 21.1 us  [exchange(): out = lax.all_to_all(msg.reshape(64, 16, shape[1]), 'dap', 0, 0, tiled=True)]
    pallas_call x15 -> x16, Pallas kernels: 19.6 us -> 20 us  [call(): pl.pallas_call(kernel, out_shape=shapes, in_specs=[pl.BlockSpec(memory_sp...]
  transfers between devices with their start and end apart: 4 -> 5, of which waited for: 4 -> 5; matrix products, arithmetic and copies ran while one was open for 0% -> 0% of each run, Pallas kernels for 2% -> 2%
where the time goes in v2:
time: 255 us; the launch traced here: 253 us
  blocking collectives  126 us (49%)
  waiting for transfers between devices  64.4 us (25%)
  starting transfers between devices  26.1 us (10%)
  Pallas kernels  20 us (8%)
  local copies, waits for them, and re-layouts  16.3 us (6%)
    all_to_all x4, blocking collectives, exchange(): out = lax.all_to_all(msg.reshape(64, 16, shape[1]), 'dap', 0, 0, tiled=True)  90 us
    all_to_all x4, waiting for transfers between devices, exchange(): out = lax.all_to_all(msg.reshape(64, 16, shape[1]), 'dap', 0, 0, tiled=True)  51.3 us
    all_to_all x4, starting transfers between devices, exchange(): out = lax.all_to_all(msg.reshape(64, 16, shape[1]), 'dap', 0, 0, tiled=True)  21.1 us
    all_to_all x1, blocking collectives, local(): parts = lax.all_to_all(wmsg.reshape(64, 24, C), 'dap', 0, 0, tiled=True)  20.5 us
    pallas_call x16, Pallas kernels, call(): pl.pallas_call(kernel, out_shape=shapes, in_specs=[pl.BlockSpec(memory_sp...  20 us
    unnamed x60, local copies, waits for them, and re-layouts  15.5 us
    all_to_all x1, blocking collectives, local(): lax.all_to_all(jnp.broadcast_to(part, (reps, 24, C)), 'rep', 0, 0, tiled=...  15 us
    all_to_all x1, waiting for transfers between devices, local(): lax.all_to_all(jnp.broadcast_to(whole, (64, 24, C)), 'dap', 0, 0, tiled=T...  13.2 us
  transfers between devices with their start and end apart: 5, of which 5 were waited for; matrix products, arithmetic and copies ran while one was open for 0% of the time, Pallas kernels for 2%

profile of v2, /device:TPU:8, one launch (start us, length us, event | category | flops | bytes accessed | tf_op | source)
XLA Modules:
  0.0 253.5 jit_solution(3883901869821711724)
XLA Ops:
  0.7 0.9 copy-done.1
  1.6 0.9 copy-done.18
  2.5 0.9 copy-done.29
  3.5 2.0 first.1
  5.5 32.0 %all_to_all.55 = bf16[64,16,256]{2,1,0:T(8,128)(2,1)S(1)} all-to-all(bf16[64,16,256]{2,1,0:T(8,128)(2,1)S(1)} %bitcast.28), channel_id=1, replica_groups=mesh['rep'=8,'dap'=64] {'dap'}, dimensions={0} | all-to-all | bytes 1048576 | tf_op jit(solution)/shard_map/all_to_all | solution.py:351
  37.5 1.5 product.2
  39.0 0.8 copy-done.13
  39.8 5.6 %all-to-all-start.1 = ((bf16[64,16,128]{2,1,0:T(8,128)(2,1)}), bf16[64,16,128]{2,1,0:T(8,128)(2,1)S(1)}, u32[]{:S(2)}, u32[]{:S(2)}) async-start(bf16[64,16,128]{2,1,0:T(8,128)(2,1)} %bitcast.5), calls=%async_computation.1 | async-start | bytes 524288 | tf_op jit(solution)/shard_map/all_to_all | solution.py:351
  45.5 1.2 copy-done.10
  46.8 1.0 copy-done.5
  47.8 0.7 copy-done.24
  48.5 9.7 %all-to-all-done.1 = bf16[64,16,128]{2,1,0:T(8,128)(2,1)S(1)} async-done(((bf16[64,16,128]{2,1,0:T(8,128)(2,1)}), bf16[64,16,128]{2,1,0:T(8,128)(2,1)S(1)}, u32[]{:S(2)}, u32[]{:S(2)}) %all-to-all-start.1) | async-done | bytes 262176 | tf_op jit(solution)/shard_map/all_to_all | solution.py:351
  58.2 1.6 middle.1
  59.8 22.4 %all_to_all.56 = bf16[64,16,256]{2,1,0:T(8,128)(2,1)S(1)} all-to-all(bf16[64,16,256]{2,1,0:T(8,128)(2,1)S(1)} %bitcast.29), channel_id=1, replica_groups=mesh['rep'=8,'dap'=64] {'dap'}, dimensions={0} | all-to-all | bytes 1048576 | tf_op jit(solution)/shard_map/all_to_all | solution.py:351
  82.2 1.5 product.3
  83.7 0.8 copy-done.15
  84.5 5.6 %all-to-all-start.3 = ((bf16[64,16,128]{2,1,0:T(8,128)(2,1)}), bf16[64,16,128]{2,1,0:T(8,128)(2,1)S(1)}, u32[]{:S(2)}, u32[]{:S(2)}) async-start(bf16[64,16,128]{2,1,0:T(8,128)(2,1)} %bitcast.9), calls=%async_computation.3 | async-start | bytes 524288 | tf_op jit(solution)/shard_map/all_to_all | solution.py:351
  90.1 1.0 cotangent.1
  91.1 1.0 copy-done.3
  92.0 10.9 %all-to-all-done.3 = bf16[64,16,128]{2,1,0:T(8,128)(2,1)S(1)} async-done(((bf16[64,16,128]{2,1,0:T(8,128)(2,1)}), bf16[64,16,128]{2,1,0:T(8,128)(2,1)S(1)}, u32[]{:S(2)}, u32[]{:S(2)}) %all-to-all-start.3) | async-done | bytes 262176 | tf_op jit(solution)/shard_map/all_to_all | solution.py:351
  102.9 0.9 turn.1
  103.8 0.7 copy-done.22
  104.5 17.4 %all_to_all.57 = bf16[64,16,128]{2,1,0:T(8,128)(2,1)S(1)} all-to-all(bf16[64,16,128]{2,1,0:T(8,128)(2,1)S(1)} %bitcast.37), channel_id=1, replica_groups=mesh['rep'=8,'dap'=64] {'dap'}, dimensions={0} | all-to-all | bytes 524288 | tf_op jit(solution)/shard_map/all_to_all | solution.py:351
  121.9 1.7 grads.2
  123.5 5.0 %all-to-all-start.5 = ((bf16[64,16,256]{2,1,0:T(8,128)(2,1)}), bf16[64,16,256]{2,1,0:T(8,128)(2,1)S(1)}, u32[]{:S(2)}, u32[]{:S(2)}) async-start(bf16[64,16,256]{2,1,0:T(8,128)(2,1)} %bitcast.13), calls=%async_computation.5 | async-start | bytes 1048576 | tf_op jit(solution)/shard_map/all_to_all | solution.py:351
  128.6 0.9 late_incoming.1
  129.5 0.6 copy-done.27
  130.2 16.1 %all-to-all-done.5 = bf16[64,16,256]{2,1,0:T(8,128)(2,1)S(1)} async-done(((bf16[64,16,256]{2,1,0:T(8,128)(2,1)}), bf16[64,16,256]{2,1,0:T(8,128)(2,1)S(1)}, u32[]{:S(2)}, u32[]{:S(2)}) %all-to-all-start.5) | async-done | bytes 524320 | tf_op jit(solution)/shard_map/all_to_all | solution.py:351
  146.3 1.2 copy-done.4
  147.5 1.9 back.1
  149.4 0.7 copy-done.20
  150.1 18.2 %all_to_all.58 = bf16[64,16,128]{2,1,0:T(8,128)(2,1)S(1)} all-to-all(bf16[64,16,128]{2,1,0:T(8,128)(2,1)S(1)} %bitcast.36), channel_id=1, replica_groups=mesh['rep'=8,'dap'=64] {'dap'}, dimensions={0} | all-to-all | bytes 524288 | tf_op jit(solution)/shard_map/all_to_all | solution.py:351
  168.3 1.6 grads.3
  170.0 4.9 %all-to-all-start.7 = ((bf16[64,16,256]{2,1,0:T(8,128)(2,1)}), bf16[64,16,256]{2,1,0:T(8,128)(2,1)S(1)}, u32[]{:S(2)}, u32[]{:S(2)}) async-start(bf16[64,16,256]{2,1,0:T(8,128)(2,1)} %bitcast.17), calls=%async_computation.7 | async-start | bytes 1048576 | tf_op jit(solution)/shard_map/all_to_all | solution.py:351
  174.9 1.2 copy-done.12
  176.1 0.5 weights_incoming.1.lr2
  177.0 0.9 late_outgoing.1
  178.0 14.6 %all-to-all-done.7 = bf16[64,16,256]{2,1,0:T(8,128)(2,1)S(1)} async-done(((bf16[64,16,256]{2,1,0:T(8,128)(2,1)}), bf16[64,16,256]{2,1,0:T(8,128)(2,1)S(1)}, u32[]{:S(2)}, u32[]{:S(2)}) %all-to-all-start.7) | async-done | bytes 524320 | tf_op jit(solution)/shard_map/all_to_all | solution.py:351
  192.6 1.2 copy-done.6
  193.8 0.7 last.1
  194.6 1.0 copy-done.7
  195.6 20.5 %all_to_all.59 = bf16[64,24,128]{2,1,0:T(8,128)(2,1)S(1)} all-to-all(bf16[64,24,128]{2,1,0:T(8,128)(2,1)S(1)} %bitcast.33), channel_id=1, replica_groups=mesh['rep'=8,'dap'=64] {'dap'}, dimensions={0} | all-to-all | bytes 786432 | tf_op jit(solution)/shard_map/all_to_all | solution.py:454
  216.2 15.0 %all_to_all.60 = f32[8,24,128]{2,1,0:T(8,128)S(1)} all-to-all(f32[8,24,128]{2,1,0:T(8,128)S(1)} %broadcast_in_dim.10), channel_id=1, replica_groups=mesh['rep'=8,'dap'=64] {'rep'}, dimensions={0} | all-to-all | bytes 196608 | tf_op jit(solution)/shard_map/all_to_all | solution.py:457
  231.3 0.8 broadcast_in_dim.11
  232.1 5.1 %all-to-all-start.10 = ((bf16[64,24,128]{2,1,0:T(8,128)(2,1)}), bf16[64,24,128]{2,1,0:T(8,128)(2,1)S(1)}, u32[]{:S(2)}, u32[]{:S(2)}) async-start(bf16[64,24,128]{2,1,0:T(8,128)(2,1)} %broadcast_in_dim.11), calls=%async_computation.10 | async-start | bytes 786432 | tf_op jit(solution)/shard_map/all_to_all | solution.py:459
  237.2 2.2 pair.1
  239.3 13.2 %all-to-all-done.10 = bf16[64,24,128]{2,1,0:T(8,128)(2,1)S(1)} async-done(((bf16[64,24,128]{2,1,0:T(8,128)(2,1)}), bf16[64,24,128]{2,1,0:T(8,128)(2,1)S(1)}, u32[]{:S(2)}, u32[]{:S(2)}) %all-to-all-start.10) | async-done | bytes 393248 | tf_op jit(solution)/shard_map/all_to_all | solution.py:459
  252.5 0.9 finish.1
  (49 shorter events, 0.8 us)
Async XLA Ops:
  0.6 0.9 copy-start.1
  1.6 0.9 copy-start.18
  2.5 0.9 copy-start.29
  5.5 34.4 %copy-start.9 = (bf16[2048,256]{1,0:T(8,128)(2,1)}, bf16[2048,256]{1,0:T(8,128)(2,1)S(1)}, u32[]{:S(2)}) copy-start(bf16[2048,256]{1,0:T(8,128)(2,1)S(1)} %get-tuple-element.47.refs_3_) | copy-start | bytes 3145732
  39.0 0.8 copy-start.13
  39.8 5.6 %copy-start.2 = (bf16[128,640]{1,0:T(8,128)(2,1)S(1)}, bf16[128,640]{1,0:T(8,128)(2,1)}, u32[]{:S(2)}) copy-start(bf16[128,640]{1,0:T(8,128)(2,1)} %w1.5) | copy-start | bytes 491524
  39.8 5.6 %copy-start.19 = (bf16[1,4,256,128]{3,2,1,0:T(8,128)(2,1)S(1)}, bf16[1,4,256,128]{3,2,1,0:T(8,128)(2,1)}, u32[]{:S(2)}) copy-start(bf16[1,4,256,128]{3,2,1,0:T(8,128)(2,1)} %param.7) | copy-start | bytes 786436
  39.8 18.4 %all-to-all-start.1 = ((bf16[64,16,128]{2,1,0:T(8,128)(2,1)}), bf16[64,16,128]{2,1,0:T(8,128)(2,1)S(1)}, u32[]{:S(2)}, u32[]{:S(2)}) async-start(bf16[64,16,128]{2,1,0:T(8,128)(2,1)} %bitcast.5), calls=%async_computation.1 | async-start | bytes 524288 | tf_op jit(solution)/shard_map/all_to_all | solution.py:351
  45.4 1.2 copy-start.10
  46.7 11.6 %copy-start = (bf16[128,640]{1,0:T(8,128)(2,1)S(1)}, bf16[128,640]{1,0:T(8,128)(2,1)}, u32[]{:S(2)}) copy-start(bf16[128,640]{1,0:T(8,128)(2,1)} %w2.5) | copy-start | bytes 491524
  46.7 11.6 %copy-start.17 = (bf16[128,128]{1,0:T(8,128)(2,1)S(1)}, bf16[128,128]{1,0:T(8,128)(2,1)}, u32[]{:S(2)}) copy-start(bf16[128,128]{1,0:T(8,128)(2,1)} %v_ref.3) | copy-start | bytes 98308
  46.8 1.0 copy-start.5
  47.8 0.7 copy-start.24
  83.7 0.8 copy-start.15
  84.5 5.6 %copy-start.26 = (bf16[128,128]{1,0:T(8,128)(2,1)S(1)}, bf16[128,128]{1,0:T(8,128)(2,1)}, u32[]{:S(2)}) copy-start(bf16[128,128]{1,0:T(8,128)(2,1)} %v_ref.2) | copy-start | bytes 98308
  84.5 18.4 %all-to-all-start.3 = ((bf16[64,16,128]{2,1,0:T(8,128)(2,1)}), bf16[64,16,128]{2,1,0:T(8,128)(2,1)S(1)}, u32[]{:S(2)}, u32[]{:S(2)}) async-start(bf16[64,16,128]{2,1,0:T(8,128)(2,1)} %bitcast.9), calls=%async_computation.3 | async-start | bytes 524288 | tf_op jit(solution)/shard_map/all_to_all | solution.py:351
  91.1 1.0 copy-start.3
  102.9 19.0 %copy-start.16 = (bf16[1024,256]{1,0:T(8,128)(2,1)S(1)}, bf16[1024,256]{1,0:T(8,128)(2,1)}, u32[]{:S(2)}) copy-start(bf16[1024,256]{1,0:T(8,128)(2,1)} %copy-done.15) | copy-start | bytes 1572868
  103.8 0.7 copy-start.22
  123.5 5.0 %copy-start.23 = (bf16[512,256]{1,0:T(8,128)(2,1)S(1)}, bf16[512,256]{1,0:T(8,128)(2,1)}, u32[]{:S(2)}) copy-start(bf16[512,256]{1,0:T(8,128)(2,1)} %copy-done.22) | copy-start | bytes 786436
  123.5 22.7 %all-to-all-start.5 = ((bf16[64,16,256]{2,1,0:T(8,128)(2,1)}), bf16[64,16,256]{2,1,0:T(8,128)(2,1)S(1)}, u32[]{:S(2)}, u32[]{:S(2)}) async-start(bf16[64,16,256]{2,1,0:T(8,128)(2,1)} %bitcast.13), calls=%async_computation.5 | async-start | bytes 1048576 | tf_op jit(solution)/shard_map/all_to_all | solution.py:351
  129.5 0.6 copy-start.27
  146.3 1.2 copy-start.4
  149.4 0.7 copy-start.20
  150.1 19.8 %copy-start.11 = (bf16[2048,256]{1,0:T(8,128)(2,1)}, bf16[2048,256]{1,0:T(8,128)(2,1)S(1)}, u32[]{:S(2)}) copy-start(bf16[2048,256]{1,0:T(8,128)(2,1)S(1)} %get-tuple-element.65.proj) | copy-start | bytes 3145732
  150.1 18.2 %copy-start.14 = (bf16[1024,256]{1,0:T(8,128)(2,1)S(1)}, bf16[1024,256]{1,0:T(8,128)(2,1)}, u32[]{:S(2)}) copy-start(bf16[1024,256]{1,0:T(8,128)(2,1)} %copy-done.13) | copy-start | bytes 1572868
  170.0 22.6 %all-to-all-start.7 = ((bf16[64,16,256]{2,1,0:T(8,128)(2,1)}), bf16[64,16,256]{2,1,0:T(8,128)(2,1)S(1)}, u32[]{:S(2)}, u32[]{:S(2)}) async-start(bf16[64,16,256]{2,1,0:T(8,128)(2,1)} %bitcast.17), calls=%async_computation.7 | async-start | bytes 1048576 | tf_op jit(solution)/shard_map/all_to_all | solution.py:351
  174.9 1.2 copy-start.12
  176.1 0.9 copy-start.21
  177.0 15.6 %copy-start.25 = (bf16[512,256]{1,0:T(8,128)(2,1)S(1)}, bf16[512,256]{1,0:T(8,128)(2,1)}, u32[]{:S(2)}) copy-start(bf16[512,256]{1,0:T(8,128)(2,1)} %copy-done.24) | copy-start | bytes 786436
  177.0 15.6 %copy-start.28 = (bf16[256,128]{1,0:T(8,128)(2,1)S(1)}, bf16[256,128]{1,0:T(8,128)(2,1)}, u32[]{:S(2)}) copy-start(bf16[256,128]{1,0:T(8,128)(2,1)} %copy-done.27) | copy-start | bytes 196612
  192.6 1.2 copy-start.6
  194.6 1.0 copy-start.7
  216.1 21.0 %copy-start.8 = (bf16[2048,256]{1,0:T(8,128)(2,1)S(1)}, bf16[2048,256]{1,0:T(8,128)(2,1)}, u32[]{:S(2)}) copy-start(bf16[2048,256]{1,0:T(8,128)(2,1)} %copy-done.7) | copy-start | bytes 3145732
  232.1 20.4 %all-to-all-start.10 = ((bf16[64,24,128]{2,1,0:T(8,128)(2,1)}), bf16[64,24,128]{2,1,0:T(8,128)(2,1)S(1)}, u32[]{:S(2)}, u32[]{:S(2)}) async-start(bf16[64,24,128]{2,1,0:T(8,128)(2,1)} %broadcast_in_dim.11), calls=%async_computation.10 | async-start | bytes 786432 | tf_op jit(solution)/shard_map/all_to_all | solution.py:459

commit v3 on v1

--- a/solution.py
+++ b/solution.py
@@ -112,7 +112,7 @@
     cells[pl.ds((ROWS + r) * C, C), :] = (right_s * right).astype(BF)
 
 
-def first_kernel(u, w1, msg, u_t, cells):
+def first_kernel(u, w1, turn, msg, u_t, cells):
     order = column_order()
     w = w1[...]
     for r in range(ROWS):
@@ -324,6 +324,14 @@
     return out.reshape(shape)
 
 
+def stagger(pair_act):
+    reps, devices = lax.axis_size("rep"), lax.axis_size("dap")
+    pairs = [
+        (rep * devices + d, rep * devices + (d ^ 4)) for rep in range(0, reps, 2) for d in range(devices)
+    ]
+    return lax.ppermute(pair_act[0, 0, :16], ("rep", "dap"), pairs)
+
+
 ONE = (ROWS * C, N)
 TWO = (2 * ROWS * C, N)
 ONE_MSG = (64 * 16, 128)
@@ -351,7 +359,7 @@
 
 def local(pair_act, cotangent, w1, v1, w2, v2):
     lr1, u_t = call(
-        first_kernel, [(TWO_MSG, BF), (ONE, BF)], [(TWO, BF)], pair_act[0], w1, name="first"
+        first_kernel, [(TWO_MSG, BF), (ONE, BF)], [(TWO, BF)], pair_act[0], w1, stagger(pair_act), name="first"
     )
     kept1, pmsg1 = product(exchange(lr1), False)
     lr2, z1, prod1 = call(

time: 248 us -> 239 us (0.964)
  blocking collectives: 144 us -> 127 us
  starting transfers between devices: 20.6 us -> 30.3 us
  waiting for transfers between devices: 56.9 us -> 54.4 us
    all_to_all x5, blocking collectives: 109 us -> 94.1 us  [exchange(): out = lax.all_to_all(msg.reshape(64, 16, shape[1]), 'dap', 0, 0, tiled=True)]
    ppermute x0 -> x1, starting transfers between devices: none -> 7.72 us  [stagger(): return lax.ppermute(pair_act[0, 0, :16], ('rep', 'dap'), pairs)]
    all_to_all x3, waiting for transfers between devices: 43.7 us -> 39.5 us  [exchange(): out = lax.all_to_all(msg.reshape(64, 16, shape[1]), 'dap', 0, 0, tiled=True)]
  transfers between devices with their start and end apart: 4 -> 5, of which waited for: 4 -> 5; matrix products, arithmetic and copies ran while one was open for 0% -> 0% of each run, Pallas kernels for 2% -> 2%
where the time goes in v3:
time: 239 us; the launch traced here: 238 us
  blocking collectives  127 us (53%)
  waiting for transfers between devices  54.4 us (23%)
  starting transfers between devices  30.3 us (13%)
  Pallas kernels  19.5 us (8%)
  local copies, waits for them, and re-layouts  5.45 us (2%)
    all_to_all x5, blocking collectives, exchange(): out = lax.all_to_all(msg.reshape(64, 16, shape[1]), 'dap', 0, 0, tiled=True)  94.1 us
    all_to_all x3, waiting for transfers between devices, exchange(): out = lax.all_to_all(msg.reshape(64, 16, shape[1]), 'dap', 0, 0, tiled=True)  39.5 us
    pallas_call x15, Pallas kernels, call(): pl.pallas_call(kernel, out_shape=shapes, scratch_shapes=[pltpu.VMEM(s, d)...  19.5 us
    all_to_all x1, blocking collectives, local(): parts = lax.all_to_all(wmsg.reshape(64, 24, C), 'dap', 0, 0, tiled=True)  18.2 us
    all_to_all x3, starting transfers between devices, exchange(): out = lax.all_to_all(msg.reshape(64, 16, shape[1]), 'dap', 0, 0, tiled=True)  17.4 us
    all_to_all x1, blocking collectives, local(): lax.all_to_all(jnp.broadcast_to(part, (reps, 24, C)), 'rep', 0, 0, tiled=...  14.7 us
    all_to_all x1, waiting for transfers between devices, local(): lax.all_to_all(jnp.broadcast_to(whole, (64, 24, C)), 'dap', 0, 0, tiled=T...  13.4 us
    ppermute x1, starting transfers between devices, stagger(): return lax.ppermute(pair_act[0, 0, :16], ('rep', 'dap'), pairs)  7.72 us
  transfers between devices with their start and end apart: 5, of which 5 were waited for; matrix products, arithmetic and copies ran while one was open for 0% of the time, Pallas kernels for 2%

profile of v3, /device:TPU:8, one launch (start us, length us, event | category | flops | bytes accessed | tf_op | source)
XLA Modules:
  0.0 237.7 jit_solution(1301789294718183966)
XLA Ops:
  0.6 0.7 slice_bitcast_fusion
  1.3 7.7 %collective-permute-start = (bf16[16,128]{1,0:T(8,128)(2,1)S(1)}, bf16[16,128]{1,0:T(8,128)(2,1)S(1)}, u32[]{:S(2)}, u32[]{:S(2)}) collective-permute-start(bf16[16,128]{1,0:T(8,128)(2,1)S(1)} %slice_bitcast_fusion), channel_id=1, source_target_pairs={{0,4},{1,5},{2,6},{3,7},{4,0},{5,1},{6,2},{7,3},{8,12},{9,13},{10,... | collective-permute-start | bytes 12296 | tf_op jit(solution)/shard_map/ppermute | solution.py:332
  9.0 1.6 collective-permute-done.turn
  10.6 0.9 copy-done
  11.5 0.9 copy-done.16
  12.5 1.3 first.1
  13.8 25.1 %all_to_all.55 = bf16[64,16,256]{2,1,0:T(8,128)(2,1)S(1)} all-to-all(bf16[64,16,256]{2,1,0:T(8,128)(2,1)S(1)} %bitcast.30), channel_id=1, replica_groups=mesh['rep'=8,'dap'=64] {'dap'}, dimensions={0} | all-to-all | bytes 1048576 | tf_op jit(solution)/shard_map/all_to_all | solution.py:323
  38.9 0.8 product.2
  39.8 0.0 copy-start.1
  39.8 0.0 copy-start.2
  39.8 0.0 copy-start.7
  39.8 16.8 %all_to_all.56 = bf16[64,16,128]{2,1,0:T(8,128)(2,1)S(1)} all-to-all(bf16[64,16,128]{2,1,0:T(8,128)(2,1)S(1)} %bitcast.37), channel_id=1, replica_groups=mesh['rep'=8,'dap'=64] {'dap'}, dimensions={0} | all-to-all | bytes 524288 | tf_op jit(solution)/shard_map/all_to_all | solution.py:323
  56.6 0.0 copy-done.1
  56.6 1.7 middle.1
  58.3 18.6 %all_to_all.57 = bf16[64,16,256]{2,1,0:T(8,128)(2,1)S(1)} all-to-all(bf16[64,16,256]{2,1,0:T(8,128)(2,1)S(1)} %bitcast.29), channel_id=1, replica_groups=mesh['rep'=8,'dap'=64] {'dap'}, dimensions={0} | all-to-all | bytes 1048576 | tf_op jit(solution)/shard_map/all_to_all | solution.py:323
  76.9 1.5 product.3
  78.4 5.5 %all-to-all-start.3 = ((bf16[64,16,128]{2,1,0:T(8,128)(2,1)}), bf16[64,16,128]{2,1,0:T(8,128)(2,1)S(1)}, u32[]{:S(2)}, u32[]{:S(2)}) async-start(bf16[64,16,128]{2,1,0:T(8,128)(2,1)} %bitcast.8), calls=%async_computation.3 | async-start | bytes 524288 | tf_op jit(solution)/shard_map/all_to_all | solution.py:323
  83.9 1.0 cotangent.1
  84.9 10.7 %all-to-all-done.3 = bf16[64,16,128]{2,1,0:T(8,128)(2,1)S(1)} async-done(((bf16[64,16,128]{2,1,0:T(8,128)(2,1)}), bf16[64,16,128]{2,1,0:T(8,128)(2,1)S(1)}, u32[]{:S(2)}, u32[]{:S(2)}) %all-to-all-start.3) | async-done | bytes 262176 | tf_op jit(solution)/shard_map/all_to_all | solution.py:323
  95.6 0.9 turn.1
  96.5 0.0 copy-start.11
  96.5 16.4 %all_to_all.58 = bf16[64,16,128]{2,1,0:T(8,128)(2,1)S(1)} all-to-all(bf16[64,16,128]{2,1,0:T(8,128)(2,1)S(1)} %bitcast.36), channel_id=1, replica_groups=mesh['rep'=8,'dap'=64] {'dap'}, dimensions={0} | all-to-all | bytes 524288 | tf_op jit(solution)/shard_map/all_to_all | solution.py:323
  113.0 1.7 grads.2
  114.7 4.9 %all-to-all-start.5 = ((bf16[64,16,256]{2,1,0:T(8,128)(2,1)}), bf16[64,16,256]{2,1,0:T(8,128)(2,1)S(1)}, u32[]{:S(2)}, u32[]{:S(2)}) async-start(bf16[64,16,256]{2,1,0:T(8,128)(2,1)} %bitcast.13), calls=%async_computation.5 | async-start | bytes 1048576 | tf_op jit(solution)/shard_map/all_to_all | solution.py:323
  119.6 0.0 copy-done.12
  119.6 0.9 late_incoming.1
  120.5 0.0 copy-start.14
  120.6 0.6 copy-done.14
  121.2 12.4 %all-to-all-done.5 = bf16[64,16,256]{2,1,0:T(8,128)(2,1)S(1)} async-done(((bf16[64,16,256]{2,1,0:T(8,128)(2,1)}), bf16[64,16,256]{2,1,0:T(8,128)(2,1)S(1)}, u32[]{:S(2)}, u32[]{:S(2)}) %all-to-all-start.5) | async-done | bytes 524320 | tf_op jit(solution)/shard_map/all_to_all | solution.py:323
  133.6 2.4 back.1
  136.0 1.0 copy-done.3
  137.0 17.2 %all_to_all.59 = bf16[64,16,128]{2,1,0:T(8,128)(2,1)S(1)} all-to-all(bf16[64,16,128]{2,1,0:T(8,128)(2,1)S(1)} %bitcast.35), channel_id=1, replica_groups=mesh['rep'=8,'dap'=64] {'dap'}, dimensions={0} | all-to-all | bytes 524288 | tf_op jit(solution)/shard_map/all_to_all | solution.py:323
  154.2 1.7 grads.3
  155.8 7.0 %all-to-all-start.7 = ((bf16[64,16,256]{2,1,0:T(8,128)(2,1)}), bf16[64,16,256]{2,1,0:T(8,128)(2,1)S(1)}, u32[]{:S(2)}, u32[]{:S(2)}) async-start(bf16[64,16,256]{2,1,0:T(8,128)(2,1)} %bitcast.17), calls=%async_computation.7 | async-start | bytes 1048576 | tf_op jit(solution)/shard_map/all_to_all | solution.py:323
  162.8 0.0 copy-start.10
  162.8 0.5 weights_incoming.1.lr2
  163.4 0.4 copy-done.10
  163.8 0.9 late_outgoing.1
  164.7 16.3 %all-to-all-done.7 = bf16[64,16,256]{2,1,0:T(8,128)(2,1)S(1)} async-done(((bf16[64,16,256]{2,1,0:T(8,128)(2,1)}), bf16[64,16,256]{2,1,0:T(8,128)(2,1)S(1)}, u32[]{:S(2)}, u32[]{:S(2)}) %all-to-all-start.7) | async-done | bytes 524320 | tf_op jit(solution)/shard_map/all_to_all | solution.py:323
  181.1 1.2 last.1
  182.2 18.2 %all_to_all.60 = bf16[64,24,128]{2,1,0:T(8,128)(2,1)S(1)} all-to-all(bf16[64,24,128]{2,1,0:T(8,128)(2,1)S(1)} %bitcast.34), channel_id=1, replica_groups=mesh['rep'=8,'dap'=64] {'dap'}, dimensions={0} | all-to-all | bytes 786432 | tf_op jit(solution)/shard_map/all_to_all | solution.py:419
  200.4 0.1 convert_reduce_fusion
  200.5 14.7 %all_to_all.61 = f32[8,24,128]{2,1,0:T(8,128)S(1)} all-to-all(f32[8,24,128]{2,1,0:T(8,128)S(1)} %broadcast_in_dim.10), channel_id=1, replica_groups=mesh['rep'=8,'dap'=64] {'rep'}, dimensions={0} | all-to-all | bytes 196608 | tf_op jit(solution)/shard_map/all_to_all | solution.py:422
  215.3 0.8 broadcast_in_dim.11
  216.1 5.1 %all-to-all-start.10 = ((bf16[64,24,128]{2,1,0:T(8,128)(2,1)}), bf16[64,24,128]{2,1,0:T(8,128)(2,1)S(1)}, u32[]{:S(2)}, u32[]{:S(2)}) async-start(bf16[64,24,128]{2,1,0:T(8,128)(2,1)} %broadcast_in_dim.11), calls=%async_computation.10 | async-start | bytes 786432 | tf_op jit(solution)/shard_map/all_to_all | solution.py:424
  221.2 2.2 pair.1
  223.4 13.4 %all-to-all-done.10 = bf16[64,24,128]{2,1,0:T(8,128)(2,1)S(1)} async-done(((bf16[64,24,128]{2,1,0:T(8,128)(2,1)}), bf16[64,24,128]{2,1,0:T(8,128)(2,1)S(1)}, u32[]{:S(2)}, u32[]{:S(2)}) %all-to-all-start.10) | async-done | bytes 393248 | tf_op jit(solution)/shard_map/all_to_all | solution.py:424
  236.8 0.9 finish.1
  (24 shorter events, 0.1 us)
Async XLA Ops:
  1.3 9.3 %collective-permute-start = (bf16[16,128]{1,0:T(8,128)(2,1)S(1)}, bf16[16,128]{1,0:T(8,128)(2,1)S(1)}, u32[]{:S(2)}, u32[]{:S(2)}) collective-permute-start(bf16[16,128]{1,0:T(8,128)(2,1)S(1)} %slice_bitcast_fusion), channel_id=1, source_target_pairs={{0,4},{1,5},{2,6},{3,7},{4,0},{5,1},{6,2},{7,3},{8,12},{9,13},{10,... | collective-permute-start | bytes 12296 | tf_op jit(solution)/shard_map/ppermute | solution.py:332
  10.6 0.9 copy-start
  11.5 0.9 copy-start.16
  39.7 16.8 %copy-start.5 = (bf16[1024,256]{1,0:T(8,128)(2,1)}, bf16[1024,256]{1,0:T(8,128)(2,1)S(1)}, u32[]{:S(2)}) copy-start(bf16[1024,256]{1,0:T(8,128)(2,1)S(1)} %get-tuple-element.48.refs_1_) | copy-start | bytes 1572868
  39.8 16.8 %copy-start.1 = (bf16[128,640]{1,0:T(8,128)(2,1)S(1)}, bf16[128,640]{1,0:T(8,128)(2,1)}, u32[]{:S(2)}) copy-start(bf16[128,640]{1,0:T(8,128)(2,1)} %w1.9) | copy-start | bytes 491524
  39.8 16.8 %copy-start.2 = (bf16[128,640]{1,0:T(8,128)(2,1)S(1)}, bf16[128,640]{1,0:T(8,128)(2,1)}, u32[]{:S(2)}) copy-start(bf16[128,640]{1,0:T(8,128)(2,1)} %w2.5) | copy-start | bytes 491524
  39.8 16.8 %copy-start.7 = (bf16[128,128]{1,0:T(8,128)(2,1)S(1)}, bf16[128,128]{1,0:T(8,128)(2,1)}, u32[]{:S(2)}) copy-start(bf16[128,128]{1,0:T(8,128)(2,1)} %v_ref.3) | copy-start | bytes 98308
  78.3 5.5 %copy-start.8 = (bf16[1,4,256,128]{3,2,1,0:T(8,128)(2,1)S(1)}, bf16[1,4,256,128]{3,2,1,0:T(8,128)(2,1)}, u32[]{:S(2)}) copy-start(bf16[1,4,256,128]{3,2,1,0:T(8,128)(2,1)} %param.7) | copy-start | bytes 786436
  78.3 5.5 %copy-start.13 = (bf16[128,128]{1,0:T(8,128)(2,1)S(1)}, bf16[128,128]{1,0:T(8,128)(2,1)}, u32[]{:S(2)}) copy-start(bf16[128,128]{1,0:T(8,128)(2,1)} %v_ref.2) | copy-start | bytes 98308
  78.4 17.3 %all-to-all-start.3 = ((bf16[64,16,128]{2,1,0:T(8,128)(2,1)}), bf16[64,16,128]{2,1,0:T(8,128)(2,1)S(1)}, u32[]{:S(2)}, u32[]{:S(2)}) async-start(bf16[64,16,128]{2,1,0:T(8,128)(2,1)} %bitcast.8), calls=%async_computation.3 | async-start | bytes 524288 | tf_op jit(solution)/shard_map/all_to_all | solution.py:323
  96.5 16.5 %copy-start.11 = (bf16[512,256]{1,0:T(8,128)(2,1)}, bf16[512,256]{1,0:T(8,128)(2,1)S(1)}, u32[]{:S(2)}) copy-start(bf16[512,256]{1,0:T(8,128)(2,1)S(1)} %get-tuple-element.44.prod) | copy-start | bytes 786436
  114.7 4.9 %copy-start.12 = (bf16[512,256]{1,0:T(8,128)(2,1)S(1)}, bf16[512,256]{1,0:T(8,128)(2,1)}, u32[]{:S(2)}) copy-start(bf16[512,256]{1,0:T(8,128)(2,1)} %copy-done.11) | copy-start | bytes 786436
  114.7 18.9 %all-to-all-start.5 = ((bf16[64,16,256]{2,1,0:T(8,128)(2,1)}), bf16[64,16,256]{2,1,0:T(8,128)(2,1)S(1)}, u32[]{:S(2)}, u32[]{:S(2)}) async-start(bf16[64,16,256]{2,1,0:T(8,128)(2,1)} %bitcast.13), calls=%async_computation.5 | async-start | bytes 1048576 | tf_op jit(solution)/shard_map/all_to_all | solution.py:323
  120.5 0.6 copy-start.14
  136.0 1.0 copy-start.3
  136.9 17.2 %copy-start.9 = (bf16[512,256]{1,0:T(8,128)(2,1)}, bf16[512,256]{1,0:T(8,128)(2,1)S(1)}, u32[]{:S(2)}) copy-start(bf16[512,256]{1,0:T(8,128)(2,1)S(1)} %get-tuple-element.52.mix) | copy-start | bytes 786436
  137.0 17.2 %copy-start.6 = (bf16[1024,256]{1,0:T(8,128)(2,1)S(1)}, bf16[1024,256]{1,0:T(8,128)(2,1)}, u32[]{:S(2)}) copy-start(bf16[1024,256]{1,0:T(8,128)(2,1)} %copy-done.5) | copy-start | bytes 1572868
  154.2 8.7 %copy-start.4 = (bf16[2048,256]{1,0:T(8,128)(2,1)S(1)}, bf16[2048,256]{1,0:T(8,128)(2,1)}, u32[]{:S(2)}) copy-start(bf16[2048,256]{1,0:T(8,128)(2,1)} %copy-done.3) | copy-start | bytes 3145732
  155.8 25.3 %all-to-all-start.7 = ((bf16[64,16,256]{2,1,0:T(8,128)(2,1)}), bf16[64,16,256]{2,1,0:T(8,128)(2,1)S(1)}, u32[]{:S(2)}, u32[]{:S(2)}) async-start(bf16[64,16,256]{2,1,0:T(8,128)(2,1)} %bitcast.17), calls=%async_computation.7 | async-start | bytes 1048576 | tf_op jit(solution)/shard_map/all_to_all | solution.py:323
  162.8 1.0 copy-start.10
  163.8 17.3 %copy-start.15 = (bf16[256,128]{1,0:T(8,128)(2,1)S(1)}, bf16[256,128]{1,0:T(8,128)(2,1)}, u32[]{:S(2)}) copy-start(bf16[256,128]{1,0:T(8,128)(2,1)} %copy-done.14) | copy-start | bytes 196612
  216.1 20.7 %all-to-all-start.10 = ((bf16[64,24,128]{2,1,0:T(8,128)(2,1)}), bf16[64,24,128]{2,1,0:T(8,128)(2,1)S(1)}, u32[]{:S(2)}, u32[]{:S(2)}) async-start(bf16[64,24,128]{2,1,0:T(8,128)(2,1)} %broadcast_in_dim.11), calls=%async_computation.10 | async-start | bytes 786432 | tf_op jit(solution)/shard_map/all_to_all | solution.py:424

commit v4 on v3

--- a/solution.py
+++ b/solution.py
@@ -197,7 +197,7 @@
     sums[pl.ds(C, C), :] = grad_v.astype(BF)
 
 
-def grads_kernel(incoming, gmsg, kept, msg, prod, sides):
+def grads_kernel(incoming, gmsg, kept, turn, msg, prod, sides):
     def put(q, big, rows):
         h, m, r = q // 8, (q // 4) % 2, q % 4
         prod[pl.ds(m * N + 64 * r + 16 * big, 16), pl.ds(128 * h, 128)] = rows
@@ -302,13 +302,16 @@
         v[...] = sums[pl.ds(base + 5 * C, C), :].astype(F32)
 
 
-def call(kernel, outs, scratch, *args, name, flops=2e8):
+def call(kernel, outs, scratch, *args, name, flops=2e8, ordered=0):
     shapes = [jax.ShapeDtypeStruct(s, d) for s, d in outs]
+    specs = [pl.BlockSpec(memory_space=pltpu.VMEM)] * (len(args) - ordered)
+    specs += [pl.BlockSpec(memory_space=pl.ANY)] * ordered
     moved = sum(a.size * a.dtype.itemsize for a in args)
     moved += sum(s.size * s.dtype.itemsize for s in shapes)
     return pl.pallas_call(
         kernel,
         out_shape=shapes,
+        in_specs=specs,
         scratch_shapes=[pltpu.VMEM(s, d) for s, d in scratch],
         compiler_params=pltpu.CompilerParams(vmem_limit_bytes=VMEM_LIMIT),
         cost_estimate=pl.CostEstimate(
@@ -324,12 +327,14 @@
     return out.reshape(shape)
 
 
-def stagger(pair_act):
+def pass_on(array, core):
     reps, devices = lax.axis_size("rep"), lax.axis_size("dap")
     pairs = [
-        (rep * devices + d, rep * devices + (d ^ 4)) for rep in range(0, reps, 2) for d in range(devices)
+        (rep * devices + d, rep * devices + (d ^ 4))
+        for rep in range(core, reps, 2)
+        for d in range(devices)
     ]
-    return lax.ppermute(pair_act[0, 0, :16], ("rep", "dap"), pairs)
+    return lax.ppermute(array, ("rep", "dap"), pairs)
 
 
 ONE = (ROWS * C, N)
@@ -348,18 +353,18 @@
     )
 
 
-def grads(gmsg, kept, incoming):
+def grads(gmsg, kept, turn, incoming):
     def kernel(*refs):
         grads_kernel(incoming, *refs)
 
     return call(
-        kernel, [(TWO_MSG, BF)], [((2 * N, N), BF), ((4 * N, N), BF)], gmsg, kept, name="grads"
+        kernel, [(TWO_MSG, BF)], [((2 * N, N), BF), ((4 * N, N), BF)], gmsg, kept, turn, name="grads", ordered=1
     )[0]
 
 
 def local(pair_act, cotangent, w1, v1, w2, v2):
     lr1, u_t = call(
-        first_kernel, [(TWO_MSG, BF), (ONE, BF)], [(TWO, BF)], pair_act[0], w1, stagger(pair_act), name="first"
+        first_kernel, [(TWO_MSG, BF), (ONE, BF)], [(TWO, BF)], pair_act[0], w1, pass_on(v1, 0), name="first", ordered=1
     )
     kept1, pmsg1 = product(exchange(lr1), False)
     lr2, z1, prod1 = call(
@@ -387,7 +392,7 @@
         cot_t, mix2, prod2, z1, w2, v2,
         name="late_incoming",
     )
-    gsides2 = grads(exchange(gmsg2), kept2, True)
+    gsides2 = grads(exchange(gmsg2), kept2, v2, True)
     gmsg1, proj2, grad_u1, mix1 = call(
         back_kernel,
         [(ONE_MSG, BF), (PROJ, BF), (ONE, F32), (ONE, BF)],
@@ -403,7 +408,8 @@
         grad_u1, mix1, prod1, u_t, w1, v1,
         name="late_outgoing",
     )
-    gsides1 = grads(exchange(gmsg1), kept1, False)
+    grad_ch = exchange(gmsg1)
+    gsides1 = grads(grad_ch, kept1, pass_on(grad_ch, 1), False)
     wmsg, proj1 = call(
         last_kernel,
         [((12 * C, C), BF), (PROJ, BF)],

time: 239 us -> 232 us (0.971)
  waiting for transfers between devices: 54.4 us -> 50 us
    all_to_all x3, waiting for transfers between devices: 39.5 us -> 34.5 us  [exchange(): out = lax.all_to_all(msg.reshape(64, 16, shape[1]), 'dap', 0, 0, tiled=True)]
    ppermute x1 -> x2, starting transfers between devices: 7.72 us -> 8.4 us  [pass_on(): return lax.ppermute(array, ('rep', 'dap'), pairs)]
  transfers between devices with their start and end apart: 5 -> 6, of which waited for: 5 -> 5; matrix products, arithmetic and copies ran while one was open for 0% -> 0% of each run, Pallas kernels for 2% -> 2%
where the time goes in v4:
time: 232 us
  blocking collectives  127 us (55%)
  waiting for transfers between devices  50 us (22%)
  starting transfers between devices  28.7 us (12%)
  Pallas kernels  19.5 us (8%)
  local copies, waits for them, and re-layouts  5.45 us (2%)
    all_to_all x5, blocking collectives, exchange(): out = lax.all_to_all(msg.reshape(64, 16, shape[1]), 'dap', 0, 0, tiled=True)  93.9 us
    all_to_all x3, waiting for transfers between devices, exchange(): out = lax.all_to_all(msg.reshape(64, 16, shape[1]), 'dap', 0, 0, tiled=True)  34.5 us
    pallas_call x15, Pallas kernels, call(): pl.pallas_call(kernel, out_shape=shapes, in_specs=specs, scratch_shapes=[...  19.5 us
    all_to_all x1, blocking collectives, local(): parts = lax.all_to_all(wmsg.reshape(64, 24, C), 'dap', 0, 0, tiled=True)  18.2 us
    all_to_all x3, starting transfers between devices, exchange(): out = lax.all_to_all(msg.reshape(64, 16, shape[1]), 'dap', 0, 0, tiled=True)  15.2 us
    all_to_all x1, blocking collectives, local(): lax.all_to_all(jnp.broadcast_to(part, (reps, 24, C)), 'rep', 0, 0, tiled=...  14.7 us
    all_to_all x1, waiting for transfers between devices, local(): lax.all_to_all(jnp.broadcast_to(whole, (64, 24, C)), 'dap', 0, 0, tiled=T...  13.4 us
    ppermute x2, starting transfers between devices, pass_on(): return lax.ppermute(array, ('rep', 'dap'), pairs)  8.4 us
  transfers between devices with their start and end apart: 6, of which 5 were waited for; matrix products, arithmetic and copies ran while one was open for 0% of the time, Pallas kernels for 2%

profile of v4, /device:TPU:8, one launch (start us, length us, event | category | flops | bytes accessed | tf_op | source)
XLA Modules:
  0.0 231.5 jit_solution(11154092407690522183)
XLA Ops:
  0.6 7.7 %collective-permute-start = (bf16[128,128]{1,0:T(8,128)(2,1)}, bf16[128,128]{1,0:T(8,128)(2,1)S(1)}, u32[]{:S(2)}, u32[]{:S(2)}) collective-permute-start(bf16[128,128]{1,0:T(8,128)(2,1)} %v_ref.3), channel_id=1, source_target_pairs={{0,4},{1,5},{2,6},{3,7},{4,0},{5,1},{6,2},{7,3},{8,12},{9,13},{10,... | collective-permute-start | bytes 98312 | tf_op jit(solution)/shard_map/ppermute | solution.py:337
  8.4 2.1 collective-permute-done.turn
  10.5 0.9 copy-done
  11.4 0.9 copy-done.18
  12.3 1.3 first.1
  13.7 25.0 %all_to_all.55 = bf16[64,16,256]{2,1,0:T(8,128)(2,1)S(1)} all-to-all(bf16[64,16,256]{2,1,0:T(8,128)(2,1)S(1)} %bitcast.29), channel_id=1, replica_groups=mesh['rep'=8,'dap'=64] {'dap'}, dimensions={0} | all-to-all | bytes 1048576 | tf_op jit(solution)/shard_map/all_to_all | solution.py:326
  38.7 0.8 product.2
  39.5 0.0 copy-start.1
  39.5 0.0 copy-start.2
  39.5 0.0 copy-start.7
  39.5 16.8 %all_to_all.56 = bf16[64,16,128]{2,1,0:T(8,128)(2,1)S(1)} all-to-all(bf16[64,16,128]{2,1,0:T(8,128)(2,1)S(1)} %bitcast.36), channel_id=1, replica_groups=mesh['rep'=8,'dap'=64] {'dap'}, dimensions={0} | all-to-all | bytes 524288 | tf_op jit(solution)/shard_map/all_to_all | solution.py:326
  56.4 1.7 middle.1
  58.1 18.6 %all_to_all.57 = bf16[64,16,256]{2,1,0:T(8,128)(2,1)S(1)} all-to-all(bf16[64,16,256]{2,1,0:T(8,128)(2,1)S(1)} %bitcast.28), channel_id=1, replica_groups=mesh['rep'=8,'dap'=64] {'dap'}, dimensions={0} | all-to-all | bytes 1048576 | tf_op jit(solution)/shard_map/all_to_all | solution.py:326
  76.7 1.5 product.3
  78.1 5.5 %all-to-all-start.3 = ((bf16[64,16,128]{2,1,0:T(8,128)(2,1)}), bf16[64,16,128]{2,1,0:T(8,128)(2,1)S(1)}, u32[]{:S(2)}, u32[]{:S(2)}) async-start(bf16[64,16,128]{2,1,0:T(8,128)(2,1)} %bitcast.7), calls=%async_computation.3 | async-start | bytes 524288 | tf_op jit(solution)/shard_map/all_to_all | solution.py:326
  83.7 1.0 cotangent.1
  84.7 0.0 copy-start.12
  84.7 0.7 copy-done.12
  85.4 10.1 %all-to-all-done.3 = bf16[64,16,128]{2,1,0:T(8,128)(2,1)S(1)} async-done(((bf16[64,16,128]{2,1,0:T(8,128)(2,1)}), bf16[64,16,128]{2,1,0:T(8,128)(2,1)S(1)}, u32[]{:S(2)}, u32[]{:S(2)}) %all-to-all-start.3) | async-done | bytes 262176 | tf_op jit(solution)/shard_map/all_to_all | solution.py:326
  95.5 0.9 turn.1
  96.3 0.0 copy-start.14
  96.4 16.4 %all_to_all.58 = bf16[64,16,128]{2,1,0:T(8,128)(2,1)S(1)} all-to-all(bf16[64,16,128]{2,1,0:T(8,128)(2,1)S(1)} %bitcast.35), channel_id=1, replica_groups=mesh['rep'=8,'dap'=64] {'dap'}, dimensions={0} | all-to-all | bytes 524288 | tf_op jit(solution)/shard_map/all_to_all | solution.py:326
  112.8 1.7 grads.2
  114.5 4.9 %all-to-all-start.5 = ((bf16[64,16,256]{2,1,0:T(8,128)(2,1)}), bf16[64,16,256]{2,1,0:T(8,128)(2,1)S(1)}, u32[]{:S(2)}, u32[]{:S(2)}) async-start(bf16[64,16,256]{2,1,0:T(8,128)(2,1)} %bitcast.12), calls=%async_computation.5 | async-start | bytes 1048576 | tf_op jit(solution)/shard_map/all_to_all | solution.py:326
  119.4 0.9 late_incoming.1
  120.3 0.0 copy-start.16
  120.3 0.6 copy-done.16
  120.9 12.4 %all-to-all-done.5 = bf16[64,16,256]{2,1,0:T(8,128)(2,1)S(1)} async-done(((bf16[64,16,256]{2,1,0:T(8,128)(2,1)}), bf16[64,16,256]{2,1,0:T(8,128)(2,1)S(1)}, u32[]{:S(2)}, u32[]{:S(2)}) %all-to-all-start.5) | async-done | bytes 524320 | tf_op jit(solution)/shard_map/all_to_all | solution.py:326
  133.3 2.4 %back.1 = (bf16[1024,128]{1,0:T(8,128)(2,1)S(1)}, bf16[2048,256]{1,0:T(8,128)(2,1)S(1)}, f32[512,256]{1,0:T(8,128)S(1)}, bf16[512,256]{1,0:T(8,128)(2,1)S(1)}) custom-call(bf16[1024,256]{1,0:T(8,128)(2,1)S(1)} %bitcast.21, f32[512,256]{1,0:T(8,128)S(1)} %get-tuple-element.38.z1.state, bf16[512,256]{1,0:T(8,128)(2,1)S(1)} %get-tuple-element.45.gg2, ...), custom_call_target="tpu_custom_call" | custom-call | flops 200000000 | bytes 4554752 | tf_op jit(solution)/shard_map/back/pallas_call | solution.py:311
  135.7 1.0 copy-done.3
  136.7 17.1 %all_to_all.59 = bf16[64,16,128]{2,1,0:T(8,128)(2,1)S(1)} all-to-all(bf16[64,16,128]{2,1,0:T(8,128)(2,1)S(1)} %bitcast.34), channel_id=1, replica_groups=mesh['rep'=8,'dap'=64] {'dap'}, dimensions={0} | all-to-all | bytes 524288 | tf_op jit(solution)/shard_map/all_to_all | solution.py:326
  153.7 0.7 collective-permute-start.1
  154.5 1.6 grads.3
  156.1 4.8 %all-to-all-start.7 = ((bf16[64,16,256]{2,1,0:T(8,128)(2,1)}), bf16[64,16,256]{2,1,0:T(8,128)(2,1)S(1)}, u32[]{:S(2)}, u32[]{:S(2)}) async-start(bf16[64,16,256]{2,1,0:T(8,128)(2,1)} %bitcast.16), calls=%async_computation.7 | async-start | bytes 1048576 | tf_op jit(solution)/shard_map/all_to_all | solution.py:326
  160.9 0.0 copy-start.11
  160.9 0.5 weights_incoming.1.lr2
  161.5 0.4 copy-done.11
  161.9 0.9 late_outgoing.1
  162.8 12.1 %all-to-all-done.7 = bf16[64,16,256]{2,1,0:T(8,128)(2,1)S(1)} async-done(((bf16[64,16,256]{2,1,0:T(8,128)(2,1)}), bf16[64,16,256]{2,1,0:T(8,128)(2,1)S(1)}, u32[]{:S(2)}, u32[]{:S(2)}) %all-to-all-start.7) | async-done | bytes 524320 | tf_op jit(solution)/shard_map/all_to_all | solution.py:326
  174.9 1.2 last.1
  176.1 18.2 %all_to_all.60 = bf16[64,24,128]{2,1,0:T(8,128)(2,1)S(1)} all-to-all(bf16[64,24,128]{2,1,0:T(8,128)(2,1)S(1)} %bitcast.33), channel_id=1, replica_groups=mesh['rep'=8,'dap'=64] {'dap'}, dimensions={0} | all-to-all | bytes 786432 | tf_op jit(solution)/shard_map/all_to_all | solution.py:425
  194.3 0.1 convert_reduce_fusion
  194.4 14.7 %all_to_all.61 = f32[8,24,128]{2,1,0:T(8,128)S(1)} all-to-all(f32[8,24,128]{2,1,0:T(8,128)S(1)} %broadcast_in_dim.10), channel_id=1, replica_groups=mesh['rep'=8,'dap'=64] {'rep'}, dimensions={0} | all-to-all | bytes 196608 | tf_op jit(solution)/shard_map/all_to_all | solution.py:428
  209.1 0.8 broadcast_in_dim.11
  209.9 5.1 %all-to-all-start.10 = ((bf16[64,24,128]{2,1,0:T(8,128)(2,1)}), bf16[64,24,128]{2,1,0:T(8,128)(2,1)S(1)}, u32[]{:S(2)}, u32[]{:S(2)}) async-start(bf16[64,24,128]{2,1,0:T(8,128)(2,1)} %broadcast_in_dim.11), calls=%async_computation.10 | async-start | bytes 786432 | tf_op jit(solution)/shard_map/all_to_all | solution.py:430
  215.1 2.2 pair.1
  217.2 13.4 %all-to-all-done.10 = bf16[64,24,128]{2,1,0:T(8,128)(2,1)S(1)} async-done(((bf16[64,24,128]{2,1,0:T(8,128)(2,1)}), bf16[64,24,128]{2,1,0:T(8,128)(2,1)S(1)}, u32[]{:S(2)}, u32[]{:S(2)}) %all-to-all-start.10) | async-done | bytes 393248 | tf_op jit(solution)/shard_map/all_to_all | solution.py:430
  230.6 0.9 finish.1
  (29 shorter events, 0.1 us)
Async XLA Ops:
  0.6 9.8 %collective-permute-start = (bf16[128,128]{1,0:T(8,128)(2,1)}, bf16[128,128]{1,0:T(8,128)(2,1)S(1)}, u32[]{:S(2)}, u32[]{:S(2)}) collective-permute-start(bf16[128,128]{1,0:T(8,128)(2,1)} %v_ref.3), channel_id=1, source_target_pairs={{0,4},{1,5},{2,6},{3,7},{4,0},{5,1},{6,2},{7,3},{8,12},{9,13},{10,... | collective-permute-start | bytes 98312 | tf_op jit(solution)/shard_map/ppermute | solution.py:337
  10.5 0.9 copy-start
  11.4 0.9 copy-start.18
  39.5 16.9 %copy-start.5 = (bf16[1024,256]{1,0:T(8,128)(2,1)}, bf16[1024,256]{1,0:T(8,128)(2,1)S(1)}, u32[]{:S(2)}) copy-start(bf16[1024,256]{1,0:T(8,128)(2,1)S(1)} %get-tuple-element.48.refs_1_) | copy-start | bytes 1572868
  39.5 16.9 %copy-start.1 = (bf16[128,640]{1,0:T(8,128)(2,1)S(1)}, bf16[128,640]{1,0:T(8,128)(2,1)}, u32[]{:S(2)}) copy-start(bf16[128,640]{1,0:T(8,128)(2,1)} %w1.9) | copy-start | bytes 491524
  39.5 16.9 %copy-start.2 = (bf16[128,640]{1,0:T(8,128)(2,1)S(1)}, bf16[128,640]{1,0:T(8,128)(2,1)}, u32[]{:S(2)}) copy-start(bf16[128,640]{1,0:T(8,128)(2,1)} %w2.5) | copy-start | bytes 491524
  39.5 16.9 %copy-start.7 = (bf16[128,128]{1,0:T(8,128)(2,1)S(1)}, bf16[128,128]{1,0:T(8,128)(2,1)}, u32[]{:S(2)}) copy-start(bf16[128,128]{1,0:T(8,128)(2,1)} %v_ref.3) | copy-start | bytes 98308
  78.1 5.5 %copy-start.8 = (bf16[128,128]{1,0:T(8,128)(2,1)S(1)}, bf16[128,128]{1,0:T(8,128)(2,1)}, u32[]{:S(2)}) copy-start(bf16[128,128]{1,0:T(8,128)(2,1)} %v_ref.2) | copy-start | bytes 98308
  78.1 5.5 %copy-start.9 = (bf16[1,4,256,128]{3,2,1,0:T(8,128)(2,1)S(1)}, bf16[1,4,256,128]{3,2,1,0:T(8,128)(2,1)}, u32[]{:S(2)}) copy-start(bf16[1,4,256,128]{3,2,1,0:T(8,128)(2,1)} %param.7) | copy-start | bytes 786436
  78.1 17.3 %all-to-all-start.3 = ((bf16[64,16,128]{2,1,0:T(8,128)(2,1)}), bf16[64,16,128]{2,1,0:T(8,128)(2,1)S(1)}, u32[]{:S(2)}, u32[]{:S(2)}) async-start(bf16[64,16,128]{2,1,0:T(8,128)(2,1)} %bitcast.7), calls=%async_computation.3 | async-start | bytes 524288 | tf_op jit(solution)/shard_map/all_to_all | solution.py:326
  84.7 0.7 copy-start.12
  96.3 16.5 %copy-start.14 = (bf16[512,256]{1,0:T(8,128)(2,1)}, bf16[512,256]{1,0:T(8,128)(2,1)S(1)}, u32[]{:S(2)}) copy-start(bf16[512,256]{1,0:T(8,128)(2,1)S(1)} %get-tuple-element.44.prod) | copy-start | bytes 786436
  114.5 4.9 %copy-start.13 = (bf16[512,256]{1,0:T(8,128)(2,1)S(1)}, bf16[512,256]{1,0:T(8,128)(2,1)}, u32[]{:S(2)}) copy-start(bf16[512,256]{1,0:T(8,128)(2,1)} %copy-done.12) | copy-start | bytes 786436
  114.5 4.9 %copy-start.15 = (bf16[512,256]{1,0:T(8,128)(2,1)S(1)}, bf16[512,256]{1,0:T(8,128)(2,1)}, u32[]{:S(2)}) copy-start(bf16[512,256]{1,0:T(8,128)(2,1)} %copy-done.14) | copy-start | bytes 786436
  114.5 18.8 %all-to-all-start.5 = ((bf16[64,16,256]{2,1,0:T(8,128)(2,1)}), bf16[64,16,256]{2,1,0:T(8,128)(2,1)S(1)}, u32[]{:S(2)}, u32[]{:S(2)}) async-start(bf16[64,16,256]{2,1,0:T(8,128)(2,1)} %bitcast.12), calls=%async_computation.5 | async-start | bytes 1048576 | tf_op jit(solution)/shard_map/all_to_all | solution.py:326
  120.3 0.6 copy-start.16
  135.7 1.0 copy-start.3
  136.7 17.1 %copy-start.10 = (bf16[512,256]{1,0:T(8,128)(2,1)}, bf16[512,256]{1,0:T(8,128)(2,1)S(1)}, u32[]{:S(2)}) copy-start(bf16[512,256]{1,0:T(8,128)(2,1)S(1)} %get-tuple-element.52.mix) | copy-start | bytes 786436
  136.7 17.8 %copy-start.6 = (bf16[1024,256]{1,0:T(8,128)(2,1)S(1)}, bf16[1024,256]{1,0:T(8,128)(2,1)}, u32[]{:S(2)}) copy-start(bf16[1024,256]{1,0:T(8,128)(2,1)} %copy-done.5) | copy-start | bytes 1572868
  153.7 0.7 collective-permute-start.1
  154.4 6.5 %copy-start.4 = (bf16[2048,256]{1,0:T(8,128)(2,1)S(1)}, bf16[2048,256]{1,0:T(8,128)(2,1)}, u32[]{:S(2)}) copy-start(bf16[2048,256]{1,0:T(8,128)(2,1)} %copy-done.3) | copy-start | bytes 3145732
  156.1 18.8 %all-to-all-start.7 = ((bf16[64,16,256]{2,1,0:T(8,128)(2,1)}), bf16[64,16,256]{2,1,0:T(8,128)(2,1)S(1)}, u32[]{:S(2)}, u32[]{:S(2)}) async-start(bf16[64,16,256]{2,1,0:T(8,128)(2,1)} %bitcast.16), calls=%async_computation.7 | async-start | bytes 1048576 | tf_op jit(solution)/shard_map/all_to_all | solution.py:326
  160.9 1.0 copy-start.11
  161.9 13.0 %copy-start.17 = (bf16[256,128]{1,0:T(8,128)(2,1)S(1)}, bf16[256,128]{1,0:T(8,128)(2,1)}, u32[]{:S(2)}) copy-start(bf16[256,128]{1,0:T(8,128)(2,1)} %copy-done.16) | copy-start | bytes 196612
  209.9 20.7 %all-to-all-start.10 = ((bf16[64,24,128]{2,1,0:T(8,128)(2,1)}), bf16[64,24,128]{2,1,0:T(8,128)(2,1)S(1)}, u32[]{:S(2)}, u32[]{:S(2)}) async-start(bf16[64,24,128]{2,1,0:T(8,128)(2,1)} %broadcast_in_dim.11), calls=%async_computation.10 | async-start | bytes 786432 | tf_op jit(solution)/shard_map/all_to_all | solution.py:430

commit v5 on v4

--- a/solution.py
+++ b/solution.py
@@ -27,6 +27,16 @@
     return jnp.where(hit, 1.0, 0.0).astype(BF)
 
 
+def identity():
+    row = lax.broadcasted_iota(jnp.int32, (N, N), 0)
+    col = lax.broadcasted_iota(jnp.int32, (N, N), 1)
+    return jnp.where(row == col, 1.0, 0.0).astype(BF)
+
+
+def transposed(x):
+    return dot(identity(), x, 1, 1).astype(BF)
+
+
 def column_order():
     row = lax.broadcasted_iota(jnp.int32, (N, N), 0)
     col = lax.broadcasted_iota(jnp.int32, (N, N), 1)
@@ -112,8 +122,16 @@
     cells[pl.ds((ROWS + r) * C, C), :] = (right_s * right).astype(BF)
 
 
-def first_kernel(u, w1, turn, msg, u_t, cells):
+def first_kernel(u_hbm, w_hbm, turn, msg, u_t, cells, u, w1, sems):
+    loads = [
+        pltpu.make_async_copy(u_hbm, u, sems.at[0]),
+        pltpu.make_async_copy(w_hbm, w1, sems.at[1]),
+    ]
+    for load in loads:
+        load.start()
     order = column_order()
+    for load in loads:
+        load.wait()
     w = w1[...]
     for r in range(ROWS):
         state = dot(u[r], order, 0, 1)
@@ -128,11 +146,14 @@
         kept[pl.ds((2 * t + m) * N + 64 * r + 16 * big, 16), :] = rows
 
     unpack(msg, put)
-    over = 0 if incoming else 1
     for m in range(2):
         left = kept[pl.ds(m * N, N), :]
         right = kept[pl.ds((2 + m) * N, N), :]
-        prod[pl.ds(m * N, N), :] = dot(left, right, over, over).astype(BF)
+        if incoming:
+            both = dot(transposed(left), right, 1, 0)
+        else:
+            both = dot(left, right, 1, 1)
+        prod[pl.ds(m * N, N), :] = both.astype(BF)
 
     def piece(q, big):
         h, m, r = q // 8, (q // 4) % 2, q % 4
@@ -210,7 +231,7 @@
         if incoming:
             grad_left, grad_right = dot(right, grad, 1, 1), dot(left, grad, 1, 0)
         else:
-            grad_left, grad_right = dot(grad, right, 1, 0), dot(grad, left, 0, 0)
+            grad_left, grad_right = dot(grad, right, 1, 0), dot(transposed(grad), left, 1, 0)
         sides[pl.ds(m * N, N), :] = grad_left.astype(BF)
         sides[pl.ds((2 + m) * N, N), :] = grad_right.astype(BF)
 
@@ -242,14 +263,16 @@
 
 
 def back_kernel(
-    gmsg, z1, gg2, cot_t, w2, u_t, prod1, w1, v1, msg, proj, grad_u, mix, cells, grad_prod
+    gmsg, z1, gg2, cot_t, w2, u_t, prod1, w1, v1, msg, sums, grad_u, mix, cells, grad_prod
 ):
     unpack_pair(gmsg, cells)
     w_in, w, v = w2[...], w1[...], v1[...]
+    total = 0.0
     for r in range(ROWS):
         normed, inv = norm(row(z1, r))
-        grad_proj = project_grad(cells, r, normed.astype(BF), w_in)
-        proj[pl.ds(4 * r * C, 4 * C), :] = grad_proj
+        nb = normed.astype(BF)
+        grad_proj = project_grad(cells, r, nb, w_in)
+        total = total + dot(nb, grad_proj, 1, 1)
         grad = input_grad(row(cot_t, r).astype(F32), normed, inv, grad_proj, row(gg2, r), w_in)
         grad_u[pl.ds(r * C, C), :] = grad
         gate = gate_of(norm(row(u_t, r).astype(F32))[0].astype(BF), w)
@@ -258,14 +281,12 @@
         normed, inv = norm(row(prod1, r).astype(F32))
         grad_prod[pl.ds(r * C, C), :] = norm_back(normed, inv, dot(v, grad_mix, 1, 0)).astype(BF)
     pack_one(msg, grad_prod)
-
-
-def weight_kernel(state, proj, sums):
-    total = 0.0
-    for r in range(ROWS):
-        nb = norm(row(state, r).astype(F32))[0].astype(BF)
-        total = total + dot(proj[pl.ds(4 * r * C, 4 * C), :], nb, 1, 1)
-    sums[...] = total.astype(BF)
+    store_blocks(sums, total)
+
+
+def store_blocks(sums, total):
+    for b in range(4):
+        sums[pl.ds(b * C, C), :] = total[:, b * C : (b + 1) * C].astype(BF)
 
 
 def last_kernel(gmsg, u_t, w1, lr2, gv2, gv1, msg, proj, cells):
@@ -276,8 +297,8 @@
         nb = norm(row(u_t, r).astype(F32))[0].astype(BF)
         grad_proj = project_grad(cells, r, nb, w)
         proj[pl.ds(4 * r * C, 4 * C), :] = grad_proj
-        total = total + dot(grad_proj, nb, 1, 1)
-    msg[pl.ds(0, 4 * C), :] = total.astype(BF)
+        total = total + dot(nb, grad_proj, 1, 1)
+    store_blocks(msg, total)
     msg[pl.ds(4 * C, 2 * C), :] = gv1[...]
     msg[pl.ds(6 * C, 4 * C), :] = lr2[...]
     msg[pl.ds(10 * C, 2 * C), :] = gv2[...]
@@ -296,23 +317,22 @@
 
 def finish_kernel(sums, oi, oo, ii, io):
     for base, w, v in ((0, oi, oo), (6 * C, ii, io)):
-        for b in range(4):
-            w[:, pl.ds(b * C, C)] = sums[pl.ds(base + b * C, C), :].astype(F32).T
-        w[:, pl.ds(4 * C, C)] = sums[pl.ds(base + 4 * C, C), :].astype(F32)
+        for b in range(5):
+            w[:, pl.ds(b * C, C)] = sums[pl.ds(base + b * C, C), :].astype(F32)
         v[...] = sums[pl.ds(base + 5 * C, C), :].astype(F32)
 
 
-def call(kernel, outs, scratch, *args, name, flops=2e8, ordered=0):
+def call(kernel, outs, scratch, *args, name, flops=2e8, unread=0):
     shapes = [jax.ShapeDtypeStruct(s, d) for s, d in outs]
-    specs = [pl.BlockSpec(memory_space=pltpu.VMEM)] * (len(args) - ordered)
-    specs += [pl.BlockSpec(memory_space=pl.ANY)] * ordered
+    specs = [pl.BlockSpec(memory_space=pltpu.VMEM)] * (len(args) - unread)
+    specs += [pl.BlockSpec(memory_space=pl.ANY)] * unread
     moved = sum(a.size * a.dtype.itemsize for a in args)
     moved += sum(s.size * s.dtype.itemsize for s in shapes)
     return pl.pallas_call(
         kernel,
         out_shape=shapes,
         in_specs=specs,
-        scratch_shapes=[pltpu.VMEM(s, d) for s, d in scratch],
+        scratch_shapes=[pltpu.VMEM(*s) if isinstance(s, tuple) else s for s in scratch],
         compiler_params=pltpu.CompilerParams(vmem_limit_bytes=VMEM_LIMIT),
         cost_estimate=pl.CostEstimate(
             flops=int(flops), bytes_accessed=int(moved), transcendentals=0
@@ -358,13 +378,18 @@
         grads_kernel(incoming, *refs)
 
     return call(
-        kernel, [(TWO_MSG, BF)], [((2 * N, N), BF), ((4 * N, N), BF)], gmsg, kept, turn, name="grads", ordered=1
+        kernel, [(TWO_MSG, BF)], [((2 * N, N), BF), ((4 * N, N), BF)], gmsg, kept, turn, name="grads", unread=1
     )[0]
 
 
 def local(pair_act, cotangent, w1, v1, w2, v2):
     lr1, u_t = call(
-        first_kernel, [(TWO_MSG, BF), (ONE, BF)], [(TWO, BF)], pair_act[0], w1, pass_on(v1, 0), name="first", ordered=1
+        first_kernel,
+        [(TWO_MSG, BF), (ONE, BF)],
+        [(TWO, BF), ((ROWS, N, C), BF), ((C, 5 * C), BF), pltpu.SemaphoreType.DMA((2,))],
+        pair_act[0], w1, pass_on(v1, 0),
+        name="first",
+        unread=3,
     )
     kept1, pmsg1 = product(exchange(lr1), False)
     lr2, z1, prod1 = call(
@@ -393,14 +418,13 @@
         name="late_incoming",
     )
     gsides2 = grads(exchange(gmsg2), kept2, v2, True)
-    gmsg1, proj2, grad_u1, mix1 = call(
+    gmsg1, sums2, grad_u1, mix1 = call(
         back_kernel,
-        [(ONE_MSG, BF), (PROJ, BF), (ONE, F32), (ONE, BF)],
+        [(ONE_MSG, BF), ((4 * C, C), BF), (ONE, F32), (ONE, BF)],
         [(TWO, BF), (ONE, BF)],
         exchange(gsides2), z1, gg2, cot_t, w2, u_t, prod1, w1, v1,
         name="back",
     )
-    sums2 = call(weight_kernel, [((4 * C, C), BF)], [], z1, proj2, name="weights_incoming")[0]
     gg1, gv1 = call(
         late_kernel,
         [(ONE, BF), ((2 * C, C), BF)],

time: 232 us -> 233 us (level)
    pallas_call x15 -> x14, Pallas kernels: 19.5 us -> 20.1 us  [call(): pl.pallas_call(kernel, out_shape=shapes, in_specs=specs, scratch_shapes=[...]
where the time goes in v5:
time: 233 us
  blocking collectives  127 us (55%)
  waiting for transfers between devices  51 us (22%)
  starting transfers between devices  28.9 us (12%)
  Pallas kernels  20.1 us (9%)
  local copies, waits for them, and re-layouts  4.76 us (2%)
    all_to_all x5, blocking collectives, exchange(): out = lax.all_to_all(msg.reshape(64, 16, shape[1]), 'dap', 0, 0, tiled=True)  93.9 us
    all_to_all x3, waiting for transfers between devices, exchange(): out = lax.all_to_all(msg.reshape(64, 16, shape[1]), 'dap', 0, 0, tiled=True)  35.6 us
    pallas_call x14, Pallas kernels, call(): pl.pallas_call(kernel, out_shape=shapes, in_specs=specs, scratch_shapes=[...  20.1 us
    all_to_all x1, blocking collectives, local(): parts = lax.all_to_all(wmsg.reshape(64, 24, C), 'dap', 0, 0, tiled=True)  18.2 us
    all_to_all x3, starting transfers between devices, exchange(): out = lax.all_to_all(msg.reshape(64, 16, shape[1]), 'dap', 0, 0, tiled=True)  15.4 us
    all_to_all x1, blocking collectives, local(): lax.all_to_all(jnp.broadcast_to(part, (reps, 24, C)), 'rep', 0, 0, tiled=...  14.7 us
    all_to_all x1, waiting for transfers between devices, local(): lax.all_to_all(jnp.broadcast_to(whole, (64, 24, C)), 'dap', 0, 0, tiled=T...  13.4 us
    ppermute x2, starting transfers between devices, pass_on(): return lax.ppermute(array, ('rep', 'dap'), pairs)  8.4 us
  transfers between devices with their start and end apart: 6, of which 5 were waited for; matrix products, arithmetic and copies ran while one was open for 0% of the time, Pallas kernels for 2%

profile of v5, /device:TPU:8, one launch (start us, length us, event | category | flops | bytes accessed | tf_op | source)
XLA Modules:
  0.0 232.6 jit_solution(2758262681005042218)
XLA Ops:
  0.6 7.7 %collective-permute-start = (bf16[128,128]{1,0:T(8,128)(2,1)}, bf16[128,128]{1,0:T(8,128)(2,1)S(1)}, u32[]{:S(2)}, u32[]{:S(2)}) collective-permute-start(bf16[128,128]{1,0:T(8,128)(2,1)} %v_ref.3), channel_id=1, source_target_pairs={{0,4},{1,5},{2,6},{3,7},{4,0},{5,1},{6,2},{7,3},{8,12},{9,13},{10,... | collective-permute-start | bytes 98312 | tf_op jit(solution)/shard_map/ppermute | solution.py:357
  8.4 2.1 collective-permute-done.turn
  10.5 0.9 copy-done
  11.4 0.9 copy-done.18
  12.3 1.6 first.1
  14.0 25.0 %all_to_all.55 = bf16[64,16,256]{2,1,0:T(8,128)(2,1)S(1)} all-to-all(bf16[64,16,256]{2,1,0:T(8,128)(2,1)S(1)} %bitcast.29), channel_id=1, replica_groups=mesh['rep'=8,'dap'=64] {'dap'}, dimensions={0} | all-to-all | bytes 1048576 | tf_op jit(solution)/shard_map/all_to_all | solution.py:346
  38.9 0.8 product.2
  39.8 0.0 copy-start.1
  39.8 0.0 copy-start.2
  39.8 0.0 copy-start.5
  39.8 16.9 %all_to_all.56 = bf16[64,16,128]{2,1,0:T(8,128)(2,1)S(1)} all-to-all(bf16[64,16,128]{2,1,0:T(8,128)(2,1)S(1)} %bitcast.36), channel_id=1, replica_groups=mesh['rep'=8,'dap'=64] {'dap'}, dimensions={0} | all-to-all | bytes 524288 | tf_op jit(solution)/shard_map/all_to_all | solution.py:346
  56.7 1.7 middle.1
  58.3 18.6 %all_to_all.57 = bf16[64,16,256]{2,1,0:T(8,128)(2,1)S(1)} all-to-all(bf16[64,16,256]{2,1,0:T(8,128)(2,1)S(1)} %bitcast.28), channel_id=1, replica_groups=mesh['rep'=8,'dap'=64] {'dap'}, dimensions={0} | all-to-all | bytes 1048576 | tf_op jit(solution)/shard_map/all_to_all | solution.py:346
  76.9 1.7 product.3
  78.6 5.5 %all-to-all-start.3 = ((bf16[64,16,128]{2,1,0:T(8,128)(2,1)}), bf16[64,16,128]{2,1,0:T(8,128)(2,1)S(1)}, u32[]{:S(2)}, u32[]{:S(2)}) async-start(bf16[64,16,128]{2,1,0:T(8,128)(2,1)} %bitcast.7), calls=%async_computation.3 | async-start | bytes 524288 | tf_op jit(solution)/shard_map/all_to_all | solution.py:346
  84.1 1.0 cotangent.1
  85.2 0.0 copy-start.10
  85.2 0.7 copy-done.10
  85.9 10.0 %all-to-all-done.3 = bf16[64,16,128]{2,1,0:T(8,128)(2,1)S(1)} async-done(((bf16[64,16,128]{2,1,0:T(8,128)(2,1)}), bf16[64,16,128]{2,1,0:T(8,128)(2,1)S(1)}, u32[]{:S(2)}, u32[]{:S(2)}) %all-to-all-start.3) | async-done | bytes 262176 | tf_op jit(solution)/shard_map/all_to_all | solution.py:346
  95.9 0.9 turn.1
  96.8 0.0 copy-start.12
  96.8 0.7 copy-done.12
  97.5 16.5 %all_to_all.58 = bf16[64,16,128]{2,1,0:T(8,128)(2,1)S(1)} all-to-all(bf16[64,16,128]{2,1,0:T(8,128)(2,1)S(1)} %bitcast.35), channel_id=1, replica_groups=mesh['rep'=8,'dap'=64] {'dap'}, dimensions={0} | all-to-all | bytes 524288 | tf_op jit(solution)/shard_map/all_to_all | solution.py:346
  113.9 1.7 grads.2
  115.6 4.9 %all-to-all-start.5 = ((bf16[64,16,256]{2,1,0:T(8,128)(2,1)}), bf16[64,16,256]{2,1,0:T(8,128)(2,1)S(1)}, u32[]{:S(2)}, u32[]{:S(2)}) async-start(bf16[64,16,256]{2,1,0:T(8,128)(2,1)} %bitcast.12), calls=%async_computation.5 | async-start | bytes 1048576 | tf_op jit(solution)/shard_map/all_to_all | solution.py:346
  120.6 0.9 late_incoming.1
  121.5 0.0 copy-start.16
  121.5 0.6 copy-done.16
  122.1 12.6 %all-to-all-done.5 = bf16[64,16,256]{2,1,0:T(8,128)(2,1)S(1)} async-done(((bf16[64,16,256]{2,1,0:T(8,128)(2,1)}), bf16[64,16,256]{2,1,0:T(8,128)(2,1)S(1)}, u32[]{:S(2)}, u32[]{:S(2)}) %all-to-all-start.5) | async-done | bytes 524320 | tf_op jit(solution)/shard_map/all_to_all | solution.py:346
  134.7 2.6 %back.1 = (bf16[1024,128]{1,0:T(8,128)(2,1)S(1)}, bf16[512,128]{1,0:T(8,128)(2,1)S(1)}, f32[512,256]{1,0:T(8,128)S(1)}, bf16[512,256]{1,0:T(8,128)(2,1)S(1)}) custom-call(bf16[1024,256]{1,0:T(8,128)(2,1)S(1)} %bitcast.21, f32[512,256]{1,0:T(8,128)S(1)} %get-tuple-element.38.z1.state, bf16[512,256]{1,0:T(8,128)(2,1)S(1)} %get-tuple-element.45.gg2, ...), custom_call_target="tpu_custom_call" | custom-call | flops 200000000 | bytes 3637248 | tf_op jit(solution)/shard_map/back/pallas_call | solution.py:331
  137.3 0.0 copy-start.8
  137.3 0.0 copy-start.14
  137.3 17.0 %all_to_all.59 = bf16[64,16,128]{2,1,0:T(8,128)(2,1)S(1)} all-to-all(bf16[64,16,128]{2,1,0:T(8,128)(2,1)S(1)} %bitcast.34), channel_id=1, replica_groups=mesh['rep'=8,'dap'=64] {'dap'}, dimensions={0} | all-to-all | bytes 524288 | tf_op jit(solution)/shard_map/all_to_all | solution.py:346
  154.3 0.7 collective-permute-start.1
  155.0 1.9 grads.3
  156.9 4.9 %all-to-all-start.7 = ((bf16[64,16,256]{2,1,0:T(8,128)(2,1)}), bf16[64,16,256]{2,1,0:T(8,128)(2,1)S(1)}, u32[]{:S(2)}, u32[]{:S(2)}) async-start(bf16[64,16,256]{2,1,0:T(8,128)(2,1)} %bitcast.16), calls=%async_computation.7 | async-start | bytes 1048576 | tf_op jit(solution)/shard_map/all_to_all | solution.py:346
  161.8 0.0 copy-start.17
  161.9 0.9 late_outgoing.1
  162.8 13.0 %all-to-all-done.7 = bf16[64,16,256]{2,1,0:T(8,128)(2,1)S(1)} async-done(((bf16[64,16,256]{2,1,0:T(8,128)(2,1)}), bf16[64,16,256]{2,1,0:T(8,128)(2,1)S(1)}, u32[]{:S(2)}, u32[]{:S(2)}) %all-to-all-start.7) | async-done | bytes 524320 | tf_op jit(solution)/shard_map/all_to_all | solution.py:346
  175.8 1.4 last.1
  177.2 18.2 %all_to_all.60 = bf16[64,24,128]{2,1,0:T(8,128)(2,1)S(1)} all-to-all(bf16[64,24,128]{2,1,0:T(8,128)(2,1)S(1)} %bitcast.33), channel_id=1, replica_groups=mesh['rep'=8,'dap'=64] {'dap'}, dimensions={0} | all-to-all | bytes 786432 | tf_op jit(solution)/shard_map/all_to_all | solution.py:449
  195.5 0.1 convert_reduce_fusion
  195.5 14.7 %all_to_all.61 = f32[8,24,128]{2,1,0:T(8,128)S(1)} all-to-all(f32[8,24,128]{2,1,0:T(8,128)S(1)} %broadcast_in_dim.10), channel_id=1, replica_groups=mesh['rep'=8,'dap'=64] {'rep'}, dimensions={0} | all-to-all | bytes 196608 | tf_op jit(solution)/shard_map/all_to_all | solution.py:452
  210.3 0.8 broadcast_in_dim.11
  211.1 5.1 %all-to-all-start.10 = ((bf16[64,24,128]{2,1,0:T(8,128)(2,1)}), bf16[64,24,128]{2,1,0:T(8,128)(2,1)S(1)}, u32[]{:S(2)}, u32[]{:S(2)}) async-start(bf16[64,24,128]{2,1,0:T(8,128)(2,1)} %broadcast_in_dim.11), calls=%async_computation.10 | async-start | bytes 786432 | tf_op jit(solution)/shard_map/all_to_all | solution.py:454
  216.2 2.2 pair.1
  218.4 13.4 %all-to-all-done.10 = bf16[64,24,128]{2,1,0:T(8,128)(2,1)S(1)} async-done(((bf16[64,24,128]{2,1,0:T(8,128)(2,1)}), bf16[64,24,128]{2,1,0:T(8,128)(2,1)S(1)}, u32[]{:S(2)}, u32[]{:S(2)}) %all-to-all-start.10) | async-done | bytes 393248 | tf_op jit(solution)/shard_map/all_to_all | solution.py:454
  231.8 0.9 finish.1
  (28 shorter events, 0.1 us)
Async XLA Ops:
  0.6 9.8 %collective-permute-start = (bf16[128,128]{1,0:T(8,128)(2,1)}, bf16[128,128]{1,0:T(8,128)(2,1)S(1)}, u32[]{:S(2)}, u32[]{:S(2)}) collective-permute-start(bf16[128,128]{1,0:T(8,128)(2,1)} %v_ref.3), channel_id=1, source_target_pairs={{0,4},{1,5},{2,6},{3,7},{4,0},{5,1},{6,2},{7,3},{8,12},{9,13},{10,... | collective-permute-start | bytes 98312 | tf_op jit(solution)/shard_map/ppermute | solution.py:357
  10.5 0.9 copy-start
  11.4 0.9 copy-start.18
  39.8 16.9 %copy-start.1 = (bf16[128,640]{1,0:T(8,128)(2,1)S(1)}, bf16[128,640]{1,0:T(8,128)(2,1)}, u32[]{:S(2)}) copy-start(bf16[128,640]{1,0:T(8,128)(2,1)} %w1.7) | copy-start | bytes 491524
  39.8 16.9 %copy-start.2 = (bf16[128,640]{1,0:T(8,128)(2,1)S(1)}, bf16[128,640]{1,0:T(8,128)(2,1)}, u32[]{:S(2)}) copy-start(bf16[128,640]{1,0:T(8,128)(2,1)} %w2.5) | copy-start | bytes 491524
  39.8 16.9 %copy-start.5 = (bf16[128,128]{1,0:T(8,128)(2,1)S(1)}, bf16[128,128]{1,0:T(8,128)(2,1)}, u32[]{:S(2)}) copy-start(bf16[128,128]{1,0:T(8,128)(2,1)} %v_ref.3) | copy-start | bytes 98308
  78.6 5.5 %copy-start.3 = (bf16[1024,256]{1,0:T(8,128)(2,1)}, bf16[1024,256]{1,0:T(8,128)(2,1)S(1)}, u32[]{:S(2)}) copy-start(bf16[1024,256]{1,0:T(8,128)(2,1)S(1)} %get-tuple-element.41.refs_1_) | copy-start | bytes 1572868
  78.6 5.5 %copy-start.6 = (bf16[128,128]{1,0:T(8,128)(2,1)S(1)}, bf16[128,128]{1,0:T(8,128)(2,1)}, u32[]{:S(2)}) copy-start(bf16[128,128]{1,0:T(8,128)(2,1)} %v_ref.2) | copy-start | bytes 98308
  78.6 5.5 %copy-start.7 = (bf16[1,4,256,128]{3,2,1,0:T(8,128)(2,1)S(1)}, bf16[1,4,256,128]{3,2,1,0:T(8,128)(2,1)}, u32[]{:S(2)}) copy-start(bf16[1,4,256,128]{3,2,1,0:T(8,128)(2,1)} %param.7) | copy-start | bytes 786436
  78.6 17.3 %all-to-all-start.3 = ((bf16[64,16,128]{2,1,0:T(8,128)(2,1)}), bf16[64,16,128]{2,1,0:T(8,128)(2,1)S(1)}, u32[]{:S(2)}, u32[]{:S(2)}) async-start(bf16[64,16,128]{2,1,0:T(8,128)(2,1)} %bitcast.7), calls=%async_computation.3 | async-start | bytes 524288 | tf_op jit(solution)/shard_map/all_to_all | solution.py:346
  85.2 0.7 copy-start.10
  95.9 18.1 %copy-start.4 = (bf16[1024,256]{1,0:T(8,128)(2,1)S(1)}, bf16[1024,256]{1,0:T(8,128)(2,1)}, u32[]{:S(2)}) copy-start(bf16[1024,256]{1,0:T(8,128)(2,1)} %copy-done.3) | copy-start | bytes 1572868
  96.8 0.7 copy-start.12
  115.6 5.0 %copy-start.11 = (bf16[512,256]{1,0:T(8,128)(2,1)S(1)}, bf16[512,256]{1,0:T(8,128)(2,1)}, u32[]{:S(2)}) copy-start(bf16[512,256]{1,0:T(8,128)(2,1)} %copy-done.10) | copy-start | bytes 786436
  115.6 5.0 %copy-start.13 = (bf16[512,256]{1,0:T(8,128)(2,1)S(1)}, bf16[512,256]{1,0:T(8,128)(2,1)}, u32[]{:S(2)}) copy-start(bf16[512,256]{1,0:T(8,128)(2,1)} %copy-done.12) | copy-start | bytes 786436
  115.6 19.1 %all-to-all-start.5 = ((bf16[64,16,256]{2,1,0:T(8,128)(2,1)}), bf16[64,16,256]{2,1,0:T(8,128)(2,1)S(1)}, u32[]{:S(2)}, u32[]{:S(2)}) async-start(bf16[64,16,256]{2,1,0:T(8,128)(2,1)} %bitcast.12), calls=%async_computation.5 | async-start | bytes 1048576 | tf_op jit(solution)/shard_map/all_to_all | solution.py:346
  121.5 0.6 copy-start.16
  137.3 17.0 %copy-start.8 = (bf16[512,256]{1,0:T(8,128)(2,1)}, bf16[512,256]{1,0:T(8,128)(2,1)S(1)}, u32[]{:S(2)}) copy-start(bf16[512,256]{1,0:T(8,128)(2,1)S(1)} %get-tuple-element.52.mix) | copy-start | bytes 786436
  137.3 17.0 %copy-start.14 = (bf16[512,128]{1,0:T(8,128)(2,1)}, bf16[512,128]{1,0:T(8,128)(2,1)S(1)}, u32[]{:S(2)}) copy-start(bf16[512,128]{1,0:T(8,128)(2,1)S(1)} %get-tuple-element.49.lr2) | copy-start | bytes 393220
  154.3 0.7 collective-permute-start.1
  156.9 4.9 %copy-start.9 = (bf16[512,256]{1,0:T(8,128)(2,1)S(1)}, bf16[512,256]{1,0:T(8,128)(2,1)}, u32[]{:S(2)}) copy-start(bf16[512,256]{1,0:T(8,128)(2,1)} %copy-done.8) | copy-start | bytes 786436
  156.9 18.9 %all-to-all-start.7 = ((bf16[64,16,256]{2,1,0:T(8,128)(2,1)}), bf16[64,16,256]{2,1,0:T(8,128)(2,1)S(1)}, u32[]{:S(2)}, u32[]{:S(2)}) async-start(bf16[64,16,256]{2,1,0:T(8,128)(2,1)} %bitcast.16), calls=%async_computation.7 | async-start | bytes 1048576 | tf_op jit(solution)/shard_map/all_to_all | solution.py:346
  161.8 14.0 %copy-start.15 = (bf16[512,128]{1,0:T(8,128)(2,1)S(1)}, bf16[512,128]{1,0:T(8,128)(2,1)}, u32[]{:S(2)}) copy-start(bf16[512,128]{1,0:T(8,128)(2,1)} %copy-done.14) | copy-start | bytes 393220
  161.8 14.0 %copy-start.17 = (bf16[256,128]{1,0:T(8,128)(2,1)S(1)}, bf16[256,128]{1,0:T(8,128)(2,1)}, u32[]{:S(2)}) copy-start(bf16[256,128]{1,0:T(8,128)(2,1)} %copy-done.16) | copy-start | bytes 196612
  211.1 20.7 %all-to-all-start.10 = ((bf16[64,24,128]{2,1,0:T(8,128)(2,1)}), bf16[64,24,128]{2,1,0:T(8,128)(2,1)S(1)}, u32[]{:S(2)}, u32[]{:S(2)}) async-start(bf16[64,24,128]{2,1,0:T(8,128)(2,1)} %broadcast_in_dim.11), calls=%async_computation.10 | async-start | bytes 786432 | tf_op jit(solution)/shard_map/all_to_all | solution.py:454

commit v6 on v5

--- a/solution.py
+++ b/solution.py
@@ -14,6 +14,7 @@
 BF = jnp.bfloat16
 F32 = jnp.float32
 VMEM_LIMIT = 48 * 1024 * 1024
+VMEM_WHOLE = 60 * 1024 * 1024
 
 
 def dot(a, b, ca, cb):
@@ -25,16 +26,6 @@
     col = lax.broadcasted_iota(jnp.int32, (256, 256), 1)
     hit = ((row & 15) == (col >> 4)) & ((row >> 4) == (col & 15))
     return jnp.where(hit, 1.0, 0.0).astype(BF)
-
-
-def identity():
-    row = lax.broadcasted_iota(jnp.int32, (N, N), 0)
-    col = lax.broadcasted_iota(jnp.int32, (N, N), 1)
-    return jnp.where(row == col, 1.0, 0.0).astype(BF)
-
-
-def transposed(x):
-    return dot(identity(), x, 1, 1).astype(BF)
 
 
 def column_order():
@@ -122,7 +113,7 @@
     cells[pl.ds((ROWS + r) * C, C), :] = (right_s * right).astype(BF)
 
 
-def first_kernel(u_hbm, w_hbm, turn, msg, u_t, cells, u, w1, sems):
+def first_kernel(u_hbm, w_hbm, msg, u_t, cells, u, w1, sems):
     loads = [
         pltpu.make_async_copy(u_hbm, u, sems.at[0]),
         pltpu.make_async_copy(w_hbm, w1, sems.at[1]),
@@ -146,14 +137,11 @@
         kept[pl.ds((2 * t + m) * N + 64 * r + 16 * big, 16), :] = rows
 
     unpack(msg, put)
+    over = 0 if incoming else 1
     for m in range(2):
         left = kept[pl.ds(m * N, N), :]
         right = kept[pl.ds((2 + m) * N, N), :]
-        if incoming:
-            both = dot(transposed(left), right, 1, 0)
-        else:
-            both = dot(left, right, 1, 1)
-        prod[pl.ds(m * N, N), :] = both.astype(BF)
+        prod[pl.ds(m * N, N), :] = dot(left, right, over, over).astype(BF)
 
     def piece(q, big):
         h, m, r = q // 8, (q // 4) % 2, q % 4
@@ -231,7 +219,7 @@
         if incoming:
             grad_left, grad_right = dot(right, grad, 1, 1), dot(left, grad, 1, 0)
         else:
-            grad_left, grad_right = dot(grad, right, 1, 0), dot(transposed(grad), left, 1, 0)
+            grad_left, grad_right = dot(grad, right, 1, 0), dot(grad, left, 0, 0)
         sides[pl.ds(m * N, N), :] = grad_left.astype(BF)
         sides[pl.ds((2 + m) * N, N), :] = grad_right.astype(BF)
 
@@ -272,7 +260,7 @@
         normed, inv = norm(row(z1, r))
         nb = normed.astype(BF)
         grad_proj = project_grad(cells, r, nb, w_in)
-        total = total + dot(nb, grad_proj, 1, 1)
+        total = total + dot(grad_proj, nb, 1, 1)
         grad = input_grad(row(cot_t, r).astype(F32), normed, inv, grad_proj, row(gg2, r), w_in)
         grad_u[pl.ds(r * C, C), :] = grad
         gate = gate_of(norm(row(u_t, r).astype(F32))[0].astype(BF), w)
@@ -281,12 +269,7 @@
         normed, inv = norm(row(prod1, r).astype(F32))
         grad_prod[pl.ds(r * C, C), :] = norm_back(normed, inv, dot(v, grad_mix, 1, 0)).astype(BF)
     pack_one(msg, grad_prod)
-    store_blocks(sums, total)
-
-
-def store_blocks(sums, total):
-    for b in range(4):
-        sums[pl.ds(b * C, C), :] = total[:, b * C : (b + 1) * C].astype(BF)
+    sums[...] = total.astype(BF)
 
 
 def last_kernel(gmsg, u_t, w1, lr2, gv2, gv1, msg, proj, cells):
@@ -297,8 +280,8 @@
         nb = norm(row(u_t, r).astype(F32))[0].astype(BF)
         grad_proj = project_grad(cells, r, nb, w)
         proj[pl.ds(4 * r * C, 4 * C), :] = grad_proj
-        total = total + dot(nb, grad_proj, 1, 1)
-    store_blocks(msg, total)
+        total = total + dot(grad_proj, nb, 1, 1)
+    msg[pl.ds(0, 4 * C), :] = total.astype(BF)
     msg[pl.ds(4 * C, 2 * C), :] = gv1[...]
     msg[pl.ds(6 * C, 4 * C), :] = lr2[...]
     msg[pl.ds(10 * C, 2 * C), :] = gv2[...]
@@ -317,15 +300,16 @@
 
 def finish_kernel(sums, oi, oo, ii, io):
     for base, w, v in ((0, oi, oo), (6 * C, ii, io)):
-        for b in range(5):
-            w[:, pl.ds(b * C, C)] = sums[pl.ds(base + b * C, C), :].astype(F32)
+        for b in range(4):
+            w[:, pl.ds(b * C, C)] = sums[pl.ds(base + b * C, C), :].astype(F32).T
+        w[:, pl.ds(4 * C, C)] = sums[pl.ds(base + 4 * C, C), :].astype(F32)
         v[...] = sums[pl.ds(base + 5 * C, C), :].astype(F32)
 
 
-def call(kernel, outs, scratch, *args, name, flops=2e8, unread=0):
+def call(kernel, outs, scratch, *args, name, place=pl.ANY, placed=0, vmem=VMEM_LIMIT):
     shapes = [jax.ShapeDtypeStruct(s, d) for s, d in outs]
-    specs = [pl.BlockSpec(memory_space=pltpu.VMEM)] * (len(args) - unread)
-    specs += [pl.BlockSpec(memory_space=pl.ANY)] * unread
+    specs = [pl.BlockSpec(memory_space=pltpu.VMEM)] * (len(args) - placed)
+    specs += [pl.BlockSpec(memory_space=place)] * placed
     moved = sum(a.size * a.dtype.itemsize for a in args)
     moved += sum(s.size * s.dtype.itemsize for s in shapes)
     return pl.pallas_call(
@@ -333,9 +317,9 @@
         out_shape=shapes,
         in_specs=specs,
         scratch_shapes=[pltpu.VMEM(*s) if isinstance(s, tuple) else s for s in scratch],
-        compiler_params=pltpu.CompilerParams(vmem_limit_bytes=VMEM_LIMIT),
+        compiler_params=pltpu.CompilerParams(vmem_limit_bytes=vmem),
         cost_estimate=pl.CostEstimate(
-            flops=int(flops), bytes_accessed=int(moved), transcendentals=0
+            flops=200_000_000, bytes_accessed=int(moved), transcendentals=0
         ),
         name=name,
     )(*args)
@@ -357,6 +341,21 @@
     return lax.ppermute(array, ("rep", "dap"), pairs)
 
 
+def after(msg, turn):
+    def kernel(old, turn, new):
+        pass
+
+    return pl.pallas_call(
+        kernel,
+        out_shape=jax.ShapeDtypeStruct(msg.shape, msg.dtype),
+        in_specs=[pl.BlockSpec(memory_space=pl.ANY)] * 2,
+        out_specs=pl.BlockSpec(memory_space=pl.ANY),
+        input_output_aliases={0: 0},
+        compiler_params=pltpu.CompilerParams(vmem_limit_bytes=VMEM_WHOLE),
+        name="after",
+    )(msg, turn)
+
+
 ONE = (ROWS * C, N)
 TWO = (2 * ROWS * C, N)
 ONE_MSG = (64 * 16, 128)
@@ -378,7 +377,7 @@
         grads_kernel(incoming, *refs)
 
     return call(
-        kernel, [(TWO_MSG, BF)], [((2 * N, N), BF), ((4 * N, N), BF)], gmsg, kept, turn, name="grads", unread=1
+        kernel, [(TWO_MSG, BF)], [((2 * N, N), BF), ((4 * N, N), BF)], gmsg, kept, turn, name="grads", placed=1
     )[0]
 
 
@@ -387,11 +386,13 @@
         first_kernel,
         [(TWO_MSG, BF), (ONE, BF)],
         [(TWO, BF), ((ROWS, N, C), BF), ((C, 5 * C), BF), pltpu.SemaphoreType.DMA((2,))],
-        pair_act[0], w1, pass_on(v1, 0),
+        pair_act[0], w1,
         name="first",
-        unread=3,
-    )
-    kept1, pmsg1 = product(exchange(lr1), False)
+        place=pltpu.HBM,
+        placed=2,
+        vmem=VMEM_WHOLE,
+    )
+    kept1, pmsg1 = product(exchange(after(lr1, pass_on(w1, 0))), False)
     lr2, z1, prod1 = call(
         middle_kernel,
         [(TWO_MSG, BF), (ONE, F32), (ONE, BF)],

time: 233 us -> 241 us (1.034)
  blocking collectives: 127 us -> 132 us
  waiting for transfers between devices: 51 us -> 54.1 us
    all_to_all x3, waiting for transfers between devices: 35.6 us -> 40.6 us  [exchange(): out = lax.all_to_all(msg.reshape(64, 16, shape[1]), 'dap', 0, 0, tiled=True)]
    all_to_all x1, blocking collectives: 18.2 us -> 21.6 us  [local(): parts = lax.all_to_all(wmsg.reshape(64, 24, C), 'dap', 0, 0, tiled=True)]
  transfers between devices with their start and end apart: 6 -> 6, of which waited for: 5 -> 5; matrix products, arithmetic and copies ran while one was open for 0% -> 0% of each run, Pallas kernels for 2% -> 3%
where the time goes in v6:
time: 241 us
  blocking collectives  132 us (55%)
  waiting for transfers between devices  54.1 us (22%)
  starting transfers between devices  28.8 us (12%)
  Pallas kernels  21 us (9%)
  local copies, waits for them, and re-layouts  3.57 us (1%)
    all_to_all x5, blocking collectives, exchange(): out = lax.all_to_all(msg.reshape(64, 16, shape[1]), 'dap', 0, 0, tiled=True)  95.6 us
    all_to_all x3, waiting for transfers between devices, exchange(): out = lax.all_to_all(msg.reshape(64, 16, shape[1]), 'dap', 0, 0, tiled=True)  40.6 us
    all_to_all x1, blocking collectives, local(): parts = lax.all_to_all(wmsg.reshape(64, 24, C), 'dap', 0, 0, tiled=True)  21.6 us
    pallas_call x14, Pallas kernels, call(): pl.pallas_call(kernel, out_shape=shapes, in_specs=specs, scratch_shapes=[...  21 us
    all_to_all x3, starting transfers between devices, exchange(): out = lax.all_to_all(msg.reshape(64, 16, shape[1]), 'dap', 0, 0, tiled=True)  15.4 us
    all_to_all x1, blocking collectives, local(): lax.all_to_all(jnp.broadcast_to(part, (reps, 24, C)), 'rep', 0, 0, tiled=...  14.9 us
    all_to_all x1, waiting for transfers between devices, local(): lax.all_to_all(jnp.broadcast_to(whole, (64, 24, C)), 'dap', 0, 0, tiled=T...  13.2 us
    ppermute x2, starting transfers between devices, pass_on(): return lax.ppermute(array, ('rep', 'dap'), pairs)  8.4 us
  transfers between devices with their start and end apart: 6, of which 5 were waited for; matrix products, arithmetic and copies ran while one was open for 0% of the time, Pallas kernels for 3%

profile of v6, /device:TPU:8, one launch (start us, length us, event | category | flops | bytes accessed | tf_op | source)
XLA Modules:
  0.0 240.7 jit_solution(7740475815403096037)
XLA Ops:
  0.6 7.7 %collective-permute-start = (bf16[128,640]{1,0:T(8,128)(2,1)}, bf16[128,640]{1,0:T(8,128)(2,1)S(1)}, u32[]{:S(2)}, u32[]{:S(2)}) collective-permute-start(bf16[128,640]{1,0:T(8,128)(2,1)} %w1.7), channel_id=1, source_target_pairs={{0,4},{1,5},{2,6},{3,7},{4,0},{5,1},{6,2},{7,3},{8,12},{9,13},{10,... | collective-permute-start | bytes 491528 | tf_op jit(solution)/shard_map/ppermute | solution.py:341
  8.4 3.1 %first.1 = (bf16[1024,256]{1,0:T(8,128)(2,1)}, bf16[512,256]{1,0:T(8,128)(2,1)}) custom-call(bf16[4,256,128]{2,1,0:T(8,128)(2,1)} %bitcast.39, bf16[128,640]{1,0:T(8,128)(2,1)} %w1.7), custom_call_target="tpu_custom_call" | custom-call | flops 200000000 | bytes 1212416 | tf_op jit(solution)/shard_map/first/pallas_call | solution.py:315
  11.5 0.3 collective-permute-done.turn
  11.9 0.7 copy-done.18
  12.5 25.6 %all_to_all.55 = bf16[64,16,256]{2,1,0:T(8,128)(2,1)S(1)} all-to-all(bf16[64,16,256]{2,1,0:T(8,128)(2,1)} %bitcast.37), channel_id=1, replica_groups=mesh['rep'=8,'dap'=64] {'dap'}, dimensions={0} | all-to-all | bytes 1048576 | tf_op jit(solution)/shard_map/all_to_all | solution.py:330
  38.1 0.8 product.2
  38.9 0.0 copy-start
  39.0 0.0 copy-start.1
  39.0 0.0 copy-start.5
  39.0 17.0 %all_to_all.56 = bf16[64,16,128]{2,1,0:T(8,128)(2,1)S(1)} all-to-all(bf16[64,16,128]{2,1,0:T(8,128)(2,1)S(1)} %bitcast.35), channel_id=1, replica_groups=mesh['rep'=8,'dap'=64] {'dap'}, dimensions={0} | all-to-all | bytes 524288 | tf_op jit(solution)/shard_map/all_to_all | solution.py:330
  56.0 1.7 middle.1
  57.7 19.7 %all_to_all.57 = bf16[64,16,256]{2,1,0:T(8,128)(2,1)S(1)} all-to-all(bf16[64,16,256]{2,1,0:T(8,128)(2,1)S(1)} %bitcast.28), channel_id=1, replica_groups=mesh['rep'=8,'dap'=64] {'dap'}, dimensions={0} | all-to-all | bytes 1048576 | tf_op jit(solution)/shard_map/all_to_all | solution.py:330
  77.4 1.5 product.3
  79.0 5.4 %all-to-all-start.3 = ((bf16[64,16,128]{2,1,0:T(8,128)(2,1)}), bf16[64,16,128]{2,1,0:T(8,128)(2,1)S(1)}, u32[]{:S(2)}, u32[]{:S(2)}) async-start(bf16[64,16,128]{2,1,0:T(8,128)(2,1)} %bitcast.7), calls=%async_computation.3 | async-start | bytes 524288 | tf_op jit(solution)/shard_map/all_to_all | solution.py:330
  84.4 1.0 cotangent.1
  85.5 0.0 copy-start.10
  85.5 0.7 copy-done.10
  86.2 10.0 %all-to-all-done.3 = bf16[64,16,128]{2,1,0:T(8,128)(2,1)S(1)} async-done(((bf16[64,16,128]{2,1,0:T(8,128)(2,1)}), bf16[64,16,128]{2,1,0:T(8,128)(2,1)S(1)}, u32[]{:S(2)}, u32[]{:S(2)}) %all-to-all-start.3) | async-done | bytes 262176 | tf_op jit(solution)/shard_map/all_to_all | solution.py:330
  96.1 0.9 turn.1
  97.0 0.0 copy-start.12
  97.0 0.7 copy-done.12
  97.7 16.4 %all_to_all.58 = bf16[64,16,128]{2,1,0:T(8,128)(2,1)S(1)} all-to-all(bf16[64,16,128]{2,1,0:T(8,128)(2,1)S(1)} %bitcast.34), channel_id=1, replica_groups=mesh['rep'=8,'dap'=64] {'dap'}, dimensions={0} | all-to-all | bytes 524288 | tf_op jit(solution)/shard_map/all_to_all | solution.py:330
  114.1 1.7 grads.2
  115.8 4.9 %all-to-all-start.5 = ((bf16[64,16,256]{2,1,0:T(8,128)(2,1)}), bf16[64,16,256]{2,1,0:T(8,128)(2,1)S(1)}, u32[]{:S(2)}, u32[]{:S(2)}) async-start(bf16[64,16,256]{2,1,0:T(8,128)(2,1)} %bitcast.12), calls=%async_computation.5 | async-start | bytes 1048576 | tf_op jit(solution)/shard_map/all_to_all | solution.py:330
  120.7 0.9 late_incoming.1
  121.7 0.0 copy-start.16
  121.7 0.6 copy-done.16
  122.3 12.9 %all-to-all-done.5 = bf16[64,16,256]{2,1,0:T(8,128)(2,1)S(1)} async-done(((bf16[64,16,256]{2,1,0:T(8,128)(2,1)}), bf16[64,16,256]{2,1,0:T(8,128)(2,1)S(1)}, u32[]{:S(2)}, u32[]{:S(2)}) %all-to-all-start.5) | async-done | bytes 524320 | tf_op jit(solution)/shard_map/all_to_all | solution.py:330
  135.2 2.5 %back.1 = (bf16[1024,128]{1,0:T(8,128)(2,1)S(1)}, bf16[512,128]{1,0:T(8,128)(2,1)S(1)}, f32[512,256]{1,0:T(8,128)S(1)}, bf16[512,256]{1,0:T(8,128)(2,1)S(1)}) custom-call(bf16[1024,256]{1,0:T(8,128)(2,1)S(1)} %bitcast.21, f32[512,256]{1,0:T(8,128)S(1)} %get-tuple-element.38.z1.state, bf16[512,256]{1,0:T(8,128)(2,1)S(1)} %get-tuple-element.45.gg2, ...), custom_call_target="tpu_custom_call" | custom-call | flops 200000000 | bytes 3637248 | tf_op jit(solution)/shard_map/back/pallas_call | solution.py:315
  137.7 0.0 copy-start.8
  137.8 0.0 copy-start.14
  137.8 16.8 %all_to_all.59 = bf16[64,16,128]{2,1,0:T(8,128)(2,1)S(1)} all-to-all(bf16[64,16,128]{2,1,0:T(8,128)(2,1)S(1)} %bitcast.33), channel_id=1, replica_groups=mesh['rep'=8,'dap'=64] {'dap'}, dimensions={0} | all-to-all | bytes 524288 | tf_op jit(solution)/shard_map/all_to_all | solution.py:330
  154.6 0.7 collective-permute-start.1
  155.3 1.6 grads.3
  156.9 5.0 %all-to-all-start.7 = ((bf16[64,16,256]{2,1,0:T(8,128)(2,1)}), bf16[64,16,256]{2,1,0:T(8,128)(2,1)S(1)}, u32[]{:S(2)}, u32[]{:S(2)}) async-start(bf16[64,16,256]{2,1,0:T(8,128)(2,1)} %bitcast.16), calls=%async_computation.7 | async-start | bytes 1048576 | tf_op jit(solution)/shard_map/all_to_all | solution.py:330
  161.9 0.0 copy-start.15
  161.9 0.0 copy-start.17
  161.9 0.9 late_outgoing.1
  162.9 17.8 %all-to-all-done.7 = bf16[64,16,256]{2,1,0:T(8,128)(2,1)S(1)} async-done(((bf16[64,16,256]{2,1,0:T(8,128)(2,1)}), bf16[64,16,256]{2,1,0:T(8,128)(2,1)S(1)}, u32[]{:S(2)}, u32[]{:S(2)}) %all-to-all-start.7) | async-done | bytes 524320 | tf_op jit(solution)/shard_map/all_to_all | solution.py:330
  180.6 1.2 last.1
  181.8 21.6 %all_to_all.60 = bf16[64,24,128]{2,1,0:T(8,128)(2,1)S(1)} all-to-all(bf16[64,24,128]{2,1,0:T(8,128)(2,1)S(1)} %bitcast.32), channel_id=1, replica_groups=mesh['rep'=8,'dap'=64] {'dap'}, dimensions={0} | all-to-all | bytes 786432 | tf_op jit(solution)/shard_map/all_to_all | solution.py:450
  203.5 0.1 convert_reduce_fusion
  203.6 14.9 %all_to_all.61 = f32[8,24,128]{2,1,0:T(8,128)S(1)} all-to-all(f32[8,24,128]{2,1,0:T(8,128)S(1)} %broadcast_in_dim.10), channel_id=1, replica_groups=mesh['rep'=8,'dap'=64] {'rep'}, dimensions={0} | all-to-all | bytes 196608 | tf_op jit(solution)/shard_map/all_to_all | solution.py:453
  218.5 0.8 broadcast_in_dim.11
  219.3 5.1 %all-to-all-start.10 = ((bf16[64,24,128]{2,1,0:T(8,128)(2,1)}), bf16[64,24,128]{2,1,0:T(8,128)(2,1)S(1)}, u32[]{:S(2)}, u32[]{:S(2)}) async-start(bf16[64,24,128]{2,1,0:T(8,128)(2,1)} %broadcast_in_dim.11), calls=%async_computation.10 | async-start | bytes 786432 | tf_op jit(solution)/shard_map/all_to_all | solution.py:455
  224.4 2.2 pair.1
  226.6 13.2 %all-to-all-done.10 = bf16[64,24,128]{2,1,0:T(8,128)(2,1)S(1)} async-done(((bf16[64,24,128]{2,1,0:T(8,128)(2,1)}), bf16[64,24,128]{2,1,0:T(8,128)(2,1)S(1)}, u32[]{:S(2)}, u32[]{:S(2)}) %all-to-all-start.10) | async-done | bytes 393248 | tf_op jit(solution)/shard_map/all_to_all | solution.py:455
  239.7 0.9 finish.1
  (29 shorter events, 0.1 us)
Async XLA Ops:
  0.6 11.2 %collective-permute-start = (bf16[128,640]{1,0:T(8,128)(2,1)}, bf16[128,640]{1,0:T(8,128)(2,1)S(1)}, u32[]{:S(2)}, u32[]{:S(2)}) collective-permute-start(bf16[128,640]{1,0:T(8,128)(2,1)} %w1.7), channel_id=1, source_target_pairs={{0,4},{1,5},{2,6},{3,7},{4,0},{5,1},{6,2},{7,3},{8,12},{9,13},{10,... | collective-permute-start | bytes 491528 | tf_op jit(solution)/shard_map/ppermute | solution.py:341
  11.9 0.7 copy-start.18
  38.1 17.9 %copy-start.2 = (bf16[128,640]{1,0:T(8,128)(2,1)S(1)}, bf16[128,640]{1,0:T(8,128)(2,1)}, u32[]{:S(2)}) copy-start(bf16[128,640]{1,0:T(8,128)(2,1)} %w2.5) | copy-start | bytes 491524
  38.9 17.1 %copy-start = (bf16[512,256]{1,0:T(8,128)(2,1)S(1)}, bf16[512,256]{1,0:T(8,128)(2,1)}, u32[]{:S(2)}) copy-start(bf16[512,256]{1,0:T(8,128)(2,1)} %get-tuple-element.33.u_t.state) | copy-start | bytes 786436
  39.0 17.1 %copy-start.1 = (bf16[128,640]{1,0:T(8,128)(2,1)S(1)}, bf16[128,640]{1,0:T(8,128)(2,1)}, u32[]{:S(2)}) copy-start(bf16[128,640]{1,0:T(8,128)(2,1)} %w1.7) | copy-start | bytes 491524
  39.0 17.1 %copy-start.5 = (bf16[128,128]{1,0:T(8,128)(2,1)S(1)}, bf16[128,128]{1,0:T(8,128)(2,1)}, u32[]{:S(2)}) copy-start(bf16[128,128]{1,0:T(8,128)(2,1)} %v_ref.3) | copy-start | bytes 98308
  78.9 5.5 %copy-start.3 = (bf16[1024,256]{1,0:T(8,128)(2,1)}, bf16[1024,256]{1,0:T(8,128)(2,1)S(1)}, u32[]{:S(2)}) copy-start(bf16[1024,256]{1,0:T(8,128)(2,1)S(1)} %get-tuple-element.41.refs_1_) | copy-start | bytes 1572868
  78.9 5.5 %copy-start.6 = (bf16[128,128]{1,0:T(8,128)(2,1)S(1)}, bf16[128,128]{1,0:T(8,128)(2,1)}, u32[]{:S(2)}) copy-start(bf16[128,128]{1,0:T(8,128)(2,1)} %v_ref.2) | copy-start | bytes 98308
  78.9 5.5 %copy-start.7 = (bf16[1,4,256,128]{3,2,1,0:T(8,128)(2,1)S(1)}, bf16[1,4,256,128]{3,2,1,0:T(8,128)(2,1)}, u32[]{:S(2)}) copy-start(bf16[1,4,256,128]{3,2,1,0:T(8,128)(2,1)} %param.7) | copy-start | bytes 786436
  79.0 17.2 %all-to-all-start.3 = ((bf16[64,16,128]{2,1,0:T(8,128)(2,1)}), bf16[64,16,128]{2,1,0:T(8,128)(2,1)S(1)}, u32[]{:S(2)}, u32[]{:S(2)}) async-start(bf16[64,16,128]{2,1,0:T(8,128)(2,1)} %bitcast.7), calls=%async_computation.3 | async-start | bytes 524288 | tf_op jit(solution)/shard_map/all_to_all | solution.py:330
  85.5 0.7 copy-start.10
  96.1 18.0 %copy-start.4 = (bf16[1024,256]{1,0:T(8,128)(2,1)S(1)}, bf16[1024,256]{1,0:T(8,128)(2,1)}, u32[]{:S(2)}) copy-start(bf16[1024,256]{1,0:T(8,128)(2,1)} %copy-done.3) | copy-start | bytes 1572868
  97.0 0.7 copy-start.12
  115.8 5.0 %copy-start.11 = (bf16[512,256]{1,0:T(8,128)(2,1)S(1)}, bf16[512,256]{1,0:T(8,128)(2,1)}, u32[]{:S(2)}) copy-start(bf16[512,256]{1,0:T(8,128)(2,1)} %copy-done.10) | copy-start | bytes 786436
  115.8 5.0 %copy-start.13 = (bf16[512,256]{1,0:T(8,128)(2,1)S(1)}, bf16[512,256]{1,0:T(8,128)(2,1)}, u32[]{:S(2)}) copy-start(bf16[512,256]{1,0:T(8,128)(2,1)} %copy-done.12) | copy-start | bytes 786436
  115.8 19.4 %all-to-all-start.5 = ((bf16[64,16,256]{2,1,0:T(8,128)(2,1)}), bf16[64,16,256]{2,1,0:T(8,128)(2,1)S(1)}, u32[]{:S(2)}, u32[]{:S(2)}) async-start(bf16[64,16,256]{2,1,0:T(8,128)(2,1)} %bitcast.12), calls=%async_computation.5 | async-start | bytes 1048576 | tf_op jit(solution)/shard_map/all_to_all | solution.py:330
  121.7 0.6 copy-start.16
  137.7 16.8 %copy-start.8 = (bf16[512,256]{1,0:T(8,128)(2,1)}, bf16[512,256]{1,0:T(8,128)(2,1)S(1)}, u32[]{:S(2)}) copy-start(bf16[512,256]{1,0:T(8,128)(2,1)S(1)} %get-tuple-element.52.mix) | copy-start | bytes 786436
  137.8 16.8 %copy-start.14 = (bf16[512,128]{1,0:T(8,128)(2,1)}, bf16[512,128]{1,0:T(8,128)(2,1)S(1)}, u32[]{:S(2)}) copy-start(bf16[512,128]{1,0:T(8,128)(2,1)S(1)} %get-tuple-element.49.lr2) | copy-start | bytes 393220
  154.6 0.7 collective-permute-start.1
  156.9 5.0 %copy-start.9 = (bf16[512,256]{1,0:T(8,128)(2,1)S(1)}, bf16[512,256]{1,0:T(8,128)(2,1)}, u32[]{:S(2)}) copy-start(bf16[512,256]{1,0:T(8,128)(2,1)} %copy-done.8) | copy-start | bytes 786436
  156.9 23.7 %all-to-all-start.7 = ((bf16[64,16,256]{2,1,0:T(8,128)(2,1)}), bf16[64,16,256]{2,1,0:T(8,128)(2,1)S(1)}, u32[]{:S(2)}, u32[]{:S(2)}) async-start(bf16[64,16,256]{2,1,0:T(8,128)(2,1)} %bitcast.16), calls=%async_computation.7 | async-start | bytes 1048576 | tf_op jit(solution)/shard_map/all_to_all | solution.py:330
  161.9 18.7 %copy-start.15 = (bf16[512,128]{1,0:T(8,128)(2,1)S(1)}, bf16[512,128]{1,0:T(8,128)(2,1)}, u32[]{:S(2)}) copy-start(bf16[512,128]{1,0:T(8,128)(2,1)} %copy-done.14) | copy-start | bytes 393220
  161.9 18.7 %copy-start.17 = (bf16[256,128]{1,0:T(8,128)(2,1)S(1)}, bf16[256,128]{1,0:T(8,128)(2,1)}, u32[]{:S(2)}) copy-start(bf16[256,128]{1,0:T(8,128)(2,1)} %copy-done.16) | copy-start | bytes 196612
  219.3 20.4 %all-to-all-start.10 = ((bf16[64,24,128]{2,1,0:T(8,128)(2,1)}), bf16[64,24,128]{2,1,0:T(8,128)(2,1)S(1)}, u32[]{:S(2)}, u32[]{:S(2)}) async-start(bf16[64,24,128]{2,1,0:T(8,128)(2,1)} %broadcast_in_dim.11), calls=%async_computation.10 | async-start | bytes 786432 | tf_op jit(solution)/shard_map/all_to_all | solution.py:455

commit v7 on v3

--- a/solution.py
+++ b/solution.py
@@ -242,14 +242,16 @@
 
 
 def back_kernel(
-    gmsg, z1, gg2, cot_t, w2, u_t, prod1, w1, v1, msg, proj, grad_u, mix, cells, grad_prod
+    gmsg, z1, gg2, cot_t, w2, u_t, prod1, w1, v1, msg, sums, grad_u, mix, cells, grad_prod
 ):
     unpack_pair(gmsg, cells)
     w_in, w, v = w2[...], w1[...], v1[...]
+    total = 0.0
     for r in range(ROWS):
         normed, inv = norm(row(z1, r))
-        grad_proj = project_grad(cells, r, normed.astype(BF), w_in)
-        proj[pl.ds(4 * r * C, 4 * C), :] = grad_proj
+        nb = normed.astype(BF)
+        grad_proj = project_grad(cells, r, nb, w_in)
+        total = total + dot(grad_proj, nb, 1, 1)
         grad = input_grad(row(cot_t, r).astype(F32), normed, inv, grad_proj, row(gg2, r), w_in)
         grad_u[pl.ds(r * C, C), :] = grad
         gate = gate_of(norm(row(u_t, r).astype(F32))[0].astype(BF), w)
@@ -258,17 +260,10 @@
         normed, inv = norm(row(prod1, r).astype(F32))
         grad_prod[pl.ds(r * C, C), :] = norm_back(normed, inv, dot(v, grad_mix, 1, 0)).astype(BF)
     pack_one(msg, grad_prod)
-
-
-def weight_kernel(state, proj, sums):
-    total = 0.0
-    for r in range(ROWS):
-        nb = norm(row(state, r).astype(F32))[0].astype(BF)
-        total = total + dot(proj[pl.ds(4 * r * C, 4 * C), :], nb, 1, 1)
     sums[...] = total.astype(BF)
 
 
-def last_kernel(gmsg, u_t, w1, lr2, gv2, gv1, msg, proj, cells):
+def last_kernel(gmsg, u_t, w1, own, other, msg, proj, cells):
     unpack_pair(gmsg, cells)
     w = w1[...]
     total = 0.0
@@ -277,10 +272,9 @@
         grad_proj = project_grad(cells, r, nb, w)
         proj[pl.ds(4 * r * C, 4 * C), :] = grad_proj
         total = total + dot(grad_proj, nb, 1, 1)
-    msg[pl.ds(0, 4 * C), :] = total.astype(BF)
-    msg[pl.ds(4 * C, 2 * C), :] = gv1[...]
-    msg[pl.ds(6 * C, 4 * C), :] = lr2[...]
-    msg[pl.ds(10 * C, 2 * C), :] = gv2[...]
+    early = own[...].astype(F32) + other[...].astype(F32)
+    both = jnp.concatenate([total.reshape(64, 1, 8, C), early.reshape(64, 1, 8, C)], axis=1)
+    msg[...] = both.reshape(8 * C, C).astype(BF)
 
 
 def pair_kernel(u_t, proj, gg1, grad_u, w1, out):
@@ -295,20 +289,27 @@
 
 
 def finish_kernel(sums, oi, oo, ii, io):
-    for base, w, v in ((0, oi, oo), (6 * C, ii, io)):
+    groups = sums[...].astype(F32).reshape(64, 3, 8, C)
+    for g, w in ((0, oi), (1, ii)):
+        part = groups[:, g].reshape(4 * C, C)
         for b in range(4):
-            w[:, pl.ds(b * C, C)] = sums[pl.ds(base + b * C, C), :].astype(F32).T
-        w[:, pl.ds(4 * C, C)] = sums[pl.ds(base + 4 * C, C), :].astype(F32)
-        v[...] = sums[pl.ds(base + 5 * C, C), :].astype(F32)
-
-
-def call(kernel, outs, scratch, *args, name, flops=2e8):
+            w[:, pl.ds(b * C, C)] = part[b * C : (b + 1) * C].T
+    part = groups[:, 2].reshape(4 * C, C)
+    for g, w, v in ((0, ii, io), (2, oi, oo)):
+        w[:, pl.ds(4 * C, C)] = part[g * C : (g + 1) * C]
+        v[...] = part[(g + 1) * C : (g + 2) * C]
+
+
+def call(kernel, outs, scratch, *args, name, flops=2e8, ordered=0):
     shapes = [jax.ShapeDtypeStruct(s, d) for s, d in outs]
+    specs = [pl.BlockSpec(memory_space=pltpu.VMEM)] * (len(args) - ordered)
+    specs += [pl.BlockSpec(memory_space=pl.ANY)] * ordered
     moved = sum(a.size * a.dtype.itemsize for a in args)
     moved += sum(s.size * s.dtype.itemsize for s in shapes)
     return pl.pallas_call(
         kernel,
         out_shape=shapes,
+        in_specs=specs,
         scratch_shapes=[pltpu.VMEM(s, d) for s, d in scratch],
         compiler_params=pltpu.CompilerParams(vmem_limit_bytes=VMEM_LIMIT),
         cost_estimate=pl.CostEstimate(
@@ -324,12 +325,14 @@
     return out.reshape(shape)
 
 
-def stagger(pair_act):
+def pass_on(array):
     reps, devices = lax.axis_size("rep"), lax.axis_size("dap")
     pairs = [
-        (rep * devices + d, rep * devices + (d ^ 4)) for rep in range(0, reps, 2) for d in range(devices)
+        (rep * devices + d, rep * devices + (d ^ 4))
+        for rep in range(0, reps, 2)
+        for d in range(devices)
     ]
-    return lax.ppermute(pair_act[0, 0, :16], ("rep", "dap"), pairs)
+    return lax.ppermute(array, ("rep", "dap"), pairs)
 
 
 ONE = (ROWS * C, N)
@@ -359,7 +362,7 @@
 
 def local(pair_act, cotangent, w1, v1, w2, v2):
     lr1, u_t = call(
-        first_kernel, [(TWO_MSG, BF), (ONE, BF)], [(TWO, BF)], pair_act[0], w1, stagger(pair_act), name="first"
+        first_kernel, [(TWO_MSG, BF), (ONE, BF)], [(TWO, BF)], pair_act[0], w1, pass_on(v1), name="first", ordered=1
     )
     kept1, pmsg1 = product(exchange(lr1), False)
     lr2, z1, prod1 = call(
@@ -388,14 +391,13 @@
         name="late_incoming",
     )
     gsides2 = grads(exchange(gmsg2), kept2, True)
-    gmsg1, proj2, grad_u1, mix1 = call(
+    gmsg1, sums2, grad_u1, mix1 = call(
         back_kernel,
-        [(ONE_MSG, BF), (PROJ, BF), (ONE, F32), (ONE, BF)],
+        [(ONE_MSG, BF), ((4 * C, C), BF), (ONE, F32), (ONE, BF)],
         [(TWO, BF), (ONE, BF)],
         exchange(gsides2), z1, gg2, cot_t, w2, u_t, prod1, w1, v1,
         name="back",
     )
-    sums2 = call(weight_kernel, [((4 * C, C), BF)], [], z1, proj2, name="weights_incoming")[0]
     gg1, gv1 = call(
         late_kernel,
         [(ONE, BF), ((2 * C, C), BF)],
@@ -403,12 +405,17 @@
         grad_u1, mix1, prod1, u_t, w1, v1,
         name="late_outgoing",
     )
+    gates = jnp.concatenate([gv2, gv1], 0)
+    first_core = lax.axis_index("rep") % 2 == 0
+    own = jnp.where(first_core, sums2, gates)
+    swaps = [(rep, rep ^ 1) for rep in range(lax.axis_size("rep"))]
+    other = lax.ppermute(jnp.where(first_core, gates, sums2), "rep", swaps)
     gsides1 = grads(exchange(gmsg1), kept1, False)
     wmsg, proj1 = call(
         last_kernel,
-        [((12 * C, C), BF), (PROJ, BF)],
+        [((8 * C, C), BF), (PROJ, BF)],
         [(TWO, BF)],
-        exchange(gsides1), u_t, w1, sums2, gv2, gv1,
+        exchange(gsides1), u_t, w1, own, other,
         name="last",
     )
     pair_grad = call(
@@ -416,11 +423,15 @@
     )[0]
 
     scale = 1.0 / math.sqrt(lax.axis_size("rep") * pair_act.shape[0] * N * N)
-    parts = lax.all_to_all(wmsg.reshape(64, 24, C), "dap", 0, 0, tiled=True)
+    parts = lax.all_to_all(wmsg.reshape(64, 16, C), "dap", 0, 0, tiled=True)
     part = jnp.sum(parts.astype(F32), axis=0)
     reps = lax.axis_size("rep")
-    across = lax.all_to_all(jnp.broadcast_to(part, (reps, 24, C)), "rep", 0, 0, tiled=True)
-    whole = (jnp.sum(across, axis=0) * scale).astype(BF)
+    across = lax.all_to_all(jnp.broadcast_to(part, (reps, 16, C)), "rep", 0, 0, tiled=True)
+    across = across.reshape(reps // 2, 2, 2, 8, C)
+    whole = jnp.concatenate(
+        [jnp.sum(across[:, :, 0], axis=(0, 1)), jnp.sum(across[:, :, 1], axis=0).reshape(16, C)], 0
+    )
+    whole = (whole * scale).astype(BF)
     everywhere = lax.all_to_all(jnp.broadcast_to(whole, (64, 24, C)), "dap", 0, 0, tiled=True)
     oi, oo, ii, io = call(
         finish_kernel,

time: 239 us -> 235 us (0.983)
  waiting for transfers between devices: 54.4 us -> 47.9 us
    all_to_all x3, waiting for transfers between devices: 39.5 us -> 31.2 us  [exchange(): out = lax.all_to_all(msg.reshape(64, 16, shape[1]), 'dap', 0, 0, tiled=True)]
    all_to_all x5, blocking collectives: 94.1 us -> 97.7 us  [exchange(): out = lax.all_to_all(msg.reshape(64, 16, shape[1]), 'dap', 0, 0, tiled=True)]
    unnamed x34 -> x39, local copies, waits for them, and re-layouts: 3.94 us -> 6.26 us
    ppermute x1 -> x2, starting transfers between devices: 7.72 us -> 9.65 us  [the longest x1 7.73 us: pass_on(): return lax.ppermute(array, ('rep', 'dap'), pairs)]
    pallas_call x15 -> x14, Pallas kernels: 19.5 us -> 19.2 us  [call(): pl.pallas_call(kernel, out_shape=shapes, in_specs=specs, scratch_shapes=[...]
  transfers between devices with their start and end apart: 5 -> 6, of which waited for: 5 -> 6; matrix products, arithmetic and copies ran while one was open for 0% -> 0% of each run, Pallas kernels for 2% -> 2%
where the time goes in v7:
time: 235 us
  blocking collectives  129 us (55%)
  waiting for transfers between devices  47.9 us (20%)
  starting transfers between devices  30.5 us (13%)
  Pallas kernels  19.2 us (8%)
  local copies, waits for them, and re-layouts  7.08 us (3%)
    all_to_all x5, blocking collectives, exchange(): out = lax.all_to_all(msg.reshape(64, 16, shape[1]), 'dap', 0, 0, tiled=True)  97.7 us
    all_to_all x3, waiting for transfers between devices, exchange(): out = lax.all_to_all(msg.reshape(64, 16, shape[1]), 'dap', 0, 0, tiled=True)  31.2 us
    pallas_call x14, Pallas kernels, call(): pl.pallas_call(kernel, out_shape=shapes, in_specs=specs, scratch_shapes=[...  19.2 us
    all_to_all x1, blocking collectives, local(): parts = lax.all_to_all(wmsg.reshape(64, 16, C), 'dap', 0, 0, tiled=True)  17 us
    all_to_all x3, starting transfers between devices, exchange(): out = lax.all_to_all(msg.reshape(64, 16, shape[1]), 'dap', 0, 0, tiled=True)  16.1 us
    all_to_all x1, blocking collectives, local(): lax.all_to_all(jnp.broadcast_to(part, (reps, 16, C)), 'rep', 0, 0, tiled=...  14.2 us
    all_to_all x1, waiting for transfers between devices, local(): lax.all_to_all(jnp.broadcast_to(whole, (64, 24, C)), 'dap', 0, 0, tiled=T...  13.3 us
    ppermute x1, starting transfers between devices, pass_on(): return lax.ppermute(array, ('rep', 'dap'), pairs)  7.73 us
  transfers between devices with their start and end apart: 6, of which 6 were waited for; matrix products, arithmetic and copies ran while one was open for 0% of the time, Pallas kernels for 2%

profile of v7, /device:TPU:8, one launch (start us, length us, event | category | flops | bytes accessed | tf_op | source)
XLA Modules:
  0.0 234.6 jit_solution(10914907492967871195)
XLA Ops:
  0.6 7.7 %collective-permute-start = (bf16[128,128]{1,0:T(8,128)(2,1)}, bf16[128,128]{1,0:T(8,128)(2,1)S(1)}, u32[]{:S(2)}, u32[]{:S(2)}) collective-permute-start(bf16[128,128]{1,0:T(8,128)(2,1)} %v_ref.3), channel_id=1, source_target_pairs={{0,4},{1,5},{2,6},{3,7},{4,0},{5,1},{6,2},{7,3},{8,12},{9,13},{10,... | collective-permute-start | bytes 98312 | tf_op jit(solution)/shard_map/ppermute | solution.py:335
  8.4 2.1 collective-permute-done.turn
  10.5 0.9 copy-done
  11.4 0.9 copy-done.18
  12.3 1.3 first.1
  13.7 25.0 %all_to_all.55 = bf16[64,16,256]{2,1,0:T(8,128)(2,1)S(1)} all-to-all(bf16[64,16,256]{2,1,0:T(8,128)(2,1)S(1)} %bitcast.30), channel_id=1, replica_groups=mesh['rep'=8,'dap'=64] {'dap'}, dimensions={0} | all-to-all | bytes 1048576 | tf_op jit(solution)/shard_map/all_to_all | solution.py:324
  38.7 0.8 product.2
  39.5 0.0 copy-start.1
  39.5 0.0 copy-start.2
  39.5 0.0 copy-start.5
  39.5 16.8 %all_to_all.56 = bf16[64,16,128]{2,1,0:T(8,128)(2,1)S(1)} all-to-all(bf16[64,16,128]{2,1,0:T(8,128)(2,1)S(1)} %bitcast.37), channel_id=1, replica_groups=mesh['rep'=8,'dap'=64] {'dap'}, dimensions={0} | all-to-all | bytes 524288 | tf_op jit(solution)/shard_map/all_to_all | solution.py:324
  56.4 1.7 middle.1
  58.1 18.6 %all_to_all.57 = bf16[64,16,256]{2,1,0:T(8,128)(2,1)S(1)} all-to-all(bf16[64,16,256]{2,1,0:T(8,128)(2,1)S(1)} %bitcast.29), channel_id=1, replica_groups=mesh['rep'=8,'dap'=64] {'dap'}, dimensions={0} | all-to-all | bytes 1048576 | tf_op jit(solution)/shard_map/all_to_all | solution.py:324
  76.6 1.5 product.3
  78.1 0.8 copy-done.3
  78.9 5.5 %all-to-all-start.3 = ((bf16[64,16,128]{2,1,0:T(8,128)(2,1)}), bf16[64,16,128]{2,1,0:T(8,128)(2,1)S(1)}, u32[]{:S(2)}, u32[]{:S(2)}) async-start(bf16[64,16,128]{2,1,0:T(8,128)(2,1)} %bitcast.7), calls=%async_computation.3 | async-start | bytes 524288 | tf_op jit(solution)/shard_map/all_to_all | solution.py:324
  84.4 1.0 cotangent.1
  85.5 0.0 copy-start.9
  85.5 0.7 copy-done.9
  86.2 10.0 %all-to-all-done.3 = bf16[64,16,128]{2,1,0:T(8,128)(2,1)S(1)} async-done(((bf16[64,16,128]{2,1,0:T(8,128)(2,1)}), bf16[64,16,128]{2,1,0:T(8,128)(2,1)S(1)}, u32[]{:S(2)}, u32[]{:S(2)}) %all-to-all-start.3) | async-done | bytes 262176 | tf_op jit(solution)/shard_map/all_to_all | solution.py:324
  96.2 0.9 turn.1
  97.1 0.0 copy-start.11
  97.1 0.7 copy-done.11
  97.8 16.6 %all_to_all.58 = bf16[64,16,128]{2,1,0:T(8,128)(2,1)S(1)} all-to-all(bf16[64,16,128]{2,1,0:T(8,128)(2,1)S(1)} %bitcast.36), channel_id=1, replica_groups=mesh['rep'=8,'dap'=64] {'dap'}, dimensions={0} | all-to-all | bytes 524288 | tf_op jit(solution)/shard_map/all_to_all | solution.py:324
  114.4 1.7 grads.2
  116.1 4.9 %all-to-all-start.5 = ((bf16[64,16,256]{2,1,0:T(8,128)(2,1)}), bf16[64,16,256]{2,1,0:T(8,128)(2,1)S(1)}, u32[]{:S(2)}, u32[]{:S(2)}) async-start(bf16[64,16,256]{2,1,0:T(8,128)(2,1)} %bitcast.12), calls=%async_computation.5 | async-start | bytes 1048576 | tf_op jit(solution)/shard_map/all_to_all | solution.py:324
  121.0 0.9 late_incoming.1
  121.9 0.6 copy-done.16
  122.6 12.4 %all-to-all-done.5 = bf16[64,16,256]{2,1,0:T(8,128)(2,1)S(1)} async-done(((bf16[64,16,256]{2,1,0:T(8,128)(2,1)}), bf16[64,16,256]{2,1,0:T(8,128)(2,1)S(1)}, u32[]{:S(2)}, u32[]{:S(2)}) %all-to-all-start.5) | async-done | bytes 524320 | tf_op jit(solution)/shard_map/all_to_all | solution.py:324
  135.0 2.5 %back.1 = (bf16[1024,128]{1,0:T(8,128)(2,1)S(1)}, bf16[512,128]{1,0:T(8,128)(2,1)S(1)}, f32[512,256]{1,0:T(8,128)S(1)}, bf16[512,256]{1,0:T(8,128)(2,1)S(1)}) custom-call(bf16[1024,256]{1,0:T(8,128)(2,1)S(1)} %bitcast.23, f32[512,256]{1,0:T(8,128)S(1)} %get-tuple-element.38.z1.state, bf16[512,256]{1,0:T(8,128)(2,1)S(1)} %get-tuple-element.45.gg2, ...), custom_call_target="tpu_custom_call" | custom-call | flops 200000000 | bytes 3637248 | tf_op jit(solution)/shard_map/back/pallas_call | solution.py:309
  137.5 0.6 copy-done.13
  138.2 20.7 %all_to_all.59 = bf16[64,16,128]{2,1,0:T(8,128)(2,1)S(1)} all-to-all(bf16[64,16,128]{2,1,0:T(8,128)(2,1)S(1)} %bitcast.34), channel_id=1, replica_groups=mesh['rep'=8,'dap'=64] {'dap'}, dimensions={0} | all-to-all | bytes 524288 | tf_op jit(solution)/shard_map/all_to_all | solution.py:324
  158.9 1.6 grads.3
  160.5 5.7 %all-to-all-start.7 = ((bf16[64,16,256]{2,1,0:T(8,128)(2,1)}), bf16[64,16,256]{2,1,0:T(8,128)(2,1)S(1)}, u32[]{:S(2)}, u32[]{:S(2)}) async-start(bf16[64,16,256]{2,1,0:T(8,128)(2,1)} %bitcast.16), calls=%async_computation.7 | async-start | bytes 1048576 | tf_op jit(solution)/shard_map/all_to_all | solution.py:324
  166.2 0.9 late_outgoing.1
  167.2 0.9 copy-done.14
  168.1 1.9 collective-permute-start.1
  170.1 1.3 collective-permute-done.1.other
  171.4 8.8 %all-to-all-done.7 = bf16[64,16,256]{2,1,0:T(8,128)(2,1)S(1)} async-done(((bf16[64,16,256]{2,1,0:T(8,128)(2,1)}), bf16[64,16,256]{2,1,0:T(8,128)(2,1)S(1)}, u32[]{:S(2)}, u32[]{:S(2)}) %all-to-all-start.7) | async-done | bytes 524320 | tf_op jit(solution)/shard_map/all_to_all | solution.py:324
  180.2 1.2 last.1
  181.3 17.0 %all_to_all.60 = bf16[64,16,128]{2,1,0:T(8,128)(2,1)S(1)} all-to-all(bf16[64,16,128]{2,1,0:T(8,128)(2,1)S(1)} %bitcast.35), channel_id=1, replica_groups=mesh['rep'=8,'dap'=64] {'dap'}, dimensions={0} | all-to-all | bytes 524288 | tf_op jit(solution)/shard_map/all_to_all | solution.py:426
  198.3 0.1 convert_reduce_fusion
  198.4 14.2 %all_to_all.61 = f32[8,16,128]{2,1,0:T(8,128)S(1)} all-to-all(f32[8,16,128]{2,1,0:T(8,128)S(1)} %broadcast_in_dim.10), channel_id=1, replica_groups=mesh['rep'=8,'dap'=64] {'rep'}, dimensions={0} | all-to-all | bytes 131072 | tf_op jit(solution)/shard_map/all_to_all | solution.py:429
  212.6 0.8 broadcast_in_dim.11
  213.4 4.8 %all-to-all-start.10 = ((bf16[64,24,128]{2,1,0:T(8,128)(2,1)}), bf16[64,24,128]{2,1,0:T(8,128)(2,1)S(1)}, u32[]{:S(2)}, u32[]{:S(2)}) async-start(bf16[64,24,128]{2,1,0:T(8,128)(2,1)} %broadcast_in_dim.11), calls=%async_computation.10 | async-start | bytes 786432 | tf_op jit(solution)/shard_map/all_to_all | solution.py:435
  218.2 2.2 pair.1
  220.4 13.3 %all-to-all-done.10 = bf16[64,24,128]{2,1,0:T(8,128)(2,1)S(1)} async-done(((bf16[64,24,128]{2,1,0:T(8,128)(2,1)}), bf16[64,24,128]{2,1,0:T(8,128)(2,1)S(1)}, u32[]{:S(2)}, u32[]{:S(2)}) %all-to-all-start.10) | async-done | bytes 393248 | tf_op jit(solution)/shard_map/all_to_all | solution.py:435
  233.7 0.9 finish.1
  (31 shorter events, 0.1 us)
Async XLA Ops:
  0.6 9.8 %collective-permute-start = (bf16[128,128]{1,0:T(8,128)(2,1)}, bf16[128,128]{1,0:T(8,128)(2,1)S(1)}, u32[]{:S(2)}, u32[]{:S(2)}) collective-permute-start(bf16[128,128]{1,0:T(8,128)(2,1)} %v_ref.3), channel_id=1, source_target_pairs={{0,4},{1,5},{2,6},{3,7},{4,0},{5,1},{6,2},{7,3},{8,12},{9,13},{10,... | collective-permute-start | bytes 98312 | tf_op jit(solution)/shard_map/ppermute | solution.py:335
  10.5 0.9 copy-start
  11.4 0.9 copy-start.18
  39.5 16.9 %copy-start.1 = (bf16[128,640]{1,0:T(8,128)(2,1)S(1)}, bf16[128,640]{1,0:T(8,128)(2,1)}, u32[]{:S(2)}) copy-start(bf16[128,640]{1,0:T(8,128)(2,1)} %w1.9) | copy-start | bytes 491524
  39.5 16.9 %copy-start.2 = (bf16[128,640]{1,0:T(8,128)(2,1)S(1)}, bf16[128,640]{1,0:T(8,128)(2,1)}, u32[]{:S(2)}) copy-start(bf16[128,640]{1,0:T(8,128)(2,1)} %w2.5) | copy-start | bytes 491524
  39.5 16.9 %copy-start.5 = (bf16[128,128]{1,0:T(8,128)(2,1)S(1)}, bf16[128,128]{1,0:T(8,128)(2,1)}, u32[]{:S(2)}) copy-start(bf16[128,128]{1,0:T(8,128)(2,1)} %v_ref.3) | copy-start | bytes 98308
  78.1 0.8 copy-start.3
  78.9 5.5 %copy-start.6 = (bf16[1,4,256,128]{3,2,1,0:T(8,128)(2,1)S(1)}, bf16[1,4,256,128]{3,2,1,0:T(8,128)(2,1)}, u32[]{:S(2)}) copy-start(bf16[1,4,256,128]{3,2,1,0:T(8,128)(2,1)} %param.7) | copy-start | bytes 786436
  78.9 5.5 %copy-start.15 = (bf16[128,128]{1,0:T(8,128)(2,1)S(1)}, bf16[128,128]{1,0:T(8,128)(2,1)}, u32[]{:S(2)}) copy-start(bf16[128,128]{1,0:T(8,128)(2,1)} %v_ref.2) | copy-start | bytes 98308
  78.9 17.3 %all-to-all-start.3 = ((bf16[64,16,128]{2,1,0:T(8,128)(2,1)}), bf16[64,16,128]{2,1,0:T(8,128)(2,1)S(1)}, u32[]{:S(2)}, u32[]{:S(2)}) async-start(bf16[64,16,128]{2,1,0:T(8,128)(2,1)} %bitcast.7), calls=%async_computation.3 | async-start | bytes 524288 | tf_op jit(solution)/shard_map/all_to_all | solution.py:324
  85.5 0.7 copy-start.9
  96.2 18.2 %copy-start.4 = (bf16[1024,256]{1,0:T(8,128)(2,1)S(1)}, bf16[1024,256]{1,0:T(8,128)(2,1)}, u32[]{:S(2)}) copy-start(bf16[1024,256]{1,0:T(8,128)(2,1)} %copy-done.3) | copy-start | bytes 1572868
  97.1 0.7 copy-start.11
  116.1 4.9 %copy-start.10 = (bf16[512,256]{1,0:T(8,128)(2,1)S(1)}, bf16[512,256]{1,0:T(8,128)(2,1)}, u32[]{:S(2)}) copy-start(bf16[512,256]{1,0:T(8,128)(2,1)} %copy-done.9) | copy-start | bytes 786436
  116.1 4.9 %copy-start.12 = (bf16[512,256]{1,0:T(8,128)(2,1)S(1)}, bf16[512,256]{1,0:T(8,128)(2,1)}, u32[]{:S(2)}) copy-start(bf16[512,256]{1,0:T(8,128)(2,1)} %copy-done.11) | copy-start | bytes 786436
  116.1 18.9 %all-to-all-start.5 = ((bf16[64,16,256]{2,1,0:T(8,128)(2,1)}), bf16[64,16,256]{2,1,0:T(8,128)(2,1)S(1)}, u32[]{:S(2)}, u32[]{:S(2)}) async-start(bf16[64,16,256]{2,1,0:T(8,128)(2,1)} %bitcast.12), calls=%async_computation.5 | async-start | bytes 1048576 | tf_op jit(solution)/shard_map/all_to_all | solution.py:324
  121.9 0.6 copy-start.16
  137.5 0.7 copy-start.13
  138.2 20.7 %copy-start.7 = (bf16[512,256]{1,0:T(8,128)(2,1)}, bf16[512,256]{1,0:T(8,128)(2,1)S(1)}, u32[]{:S(2)}) copy-start(bf16[512,256]{1,0:T(8,128)(2,1)S(1)} %get-tuple-element.52.mix) | copy-start | bytes 786436
  160.5 5.7 %copy-start.17 = (bf16[256,128]{1,0:T(8,128)(2,1)S(1)}, bf16[256,128]{1,0:T(8,128)(2,1)}, u32[]{:S(2)}) copy-start(bf16[256,128]{1,0:T(8,128)(2,1)} %copy-done.16) | copy-start | bytes 196612
  160.5 5.7 %copy-start.8 = (bf16[512,256]{1,0:T(8,128)(2,1)S(1)}, bf16[512,256]{1,0:T(8,128)(2,1)}, u32[]{:S(2)}) copy-start(bf16[512,256]{1,0:T(8,128)(2,1)} %copy-done.7) | copy-start | bytes 786436
  160.5 19.6 %all-to-all-start.7 = ((bf16[64,16,256]{2,1,0:T(8,128)(2,1)}), bf16[64,16,256]{2,1,0:T(8,128)(2,1)S(1)}, u32[]{:S(2)}, u32[]{:S(2)}) async-start(bf16[64,16,256]{2,1,0:T(8,128)(2,1)} %bitcast.16), calls=%async_computation.7 | async-start | bytes 1048576 | tf_op jit(solution)/shard_map/all_to_all | solution.py:324
  167.2 0.9 copy-start.14
  168.1 3.2 %collective-permute-start.1 = (bf16[512,128]{1,0:T(8,128)(2,1)S(1)}, bf16[512,128]{1,0:T(8,128)(2,1)S(1)}, u32[]{:S(2)}, u32[]{:S(2)}) collective-permute-start(bf16[512,128]{1,0:T(8,128)(2,1)S(1)} %get-tuple-element.63), channel_id=1, source_target_pairs={{0,64},{64,0},{128,192},{192,128},{256,320},{320,256},{384,448},{4... | collective-permute-start | bytes 393224 | tf_op jit(solution)/shard_map/ppermute | solution.py:412
  213.4 20.3 %all-to-all-start.10 = ((bf16[64,24,128]{2,1,0:T(8,128)(2,1)}), bf16[64,24,128]{2,1,0:T(8,128)(2,1)S(1)}, u32[]{:S(2)}, u32[]{:S(2)}) async-start(bf16[64,24,128]{2,1,0:T(8,128)(2,1)} %broadcast_in_dim.11), calls=%async_computation.10 | async-start | bytes 786432 | tf_op jit(solution)/shard_map/all_to_all | solution.py:435

commit v8 on v7

--- a/solution.py
+++ b/solution.py
@@ -197,7 +197,7 @@
     sums[pl.ds(C, C), :] = grad_v.astype(BF)
 
 
-def grads_kernel(incoming, gmsg, kept, msg, prod, sides):
+def grads_kernel(incoming, gmsg, kept, turn, msg, prod, sides):
     def put(q, big, rows):
         h, m, r = q // 8, (q // 4) % 2, q % 4
         prod[pl.ds(m * N + 64 * r + 16 * big, 16), pl.ds(128 * h, 128)] = rows
@@ -325,11 +325,11 @@
     return out.reshape(shape)
 
 
-def pass_on(array):
+def pass_on(array, core):
     reps, devices = lax.axis_size("rep"), lax.axis_size("dap")
     pairs = [
         (rep * devices + d, rep * devices + (d ^ 4))
-        for rep in range(0, reps, 2)
+        for rep in range(core, reps, 2)
         for d in range(devices)
     ]
     return lax.ppermute(array, ("rep", "dap"), pairs)
@@ -351,18 +351,18 @@
     )
 
 
-def grads(gmsg, kept, incoming):
+def grads(gmsg, kept, turn, incoming):
     def kernel(*refs):
         grads_kernel(incoming, *refs)
 
     return call(
-        kernel, [(TWO_MSG, BF)], [((2 * N, N), BF), ((4 * N, N), BF)], gmsg, kept, name="grads"
+        kernel, [(TWO_MSG, BF)], [((2 * N, N), BF), ((4 * N, N), BF)], gmsg, kept, turn, name="grads", ordered=1
     )[0]
 
 
 def local(pair_act, cotangent, w1, v1, w2, v2):
     lr1, u_t = call(
-        first_kernel, [(TWO_MSG, BF), (ONE, BF)], [(TWO, BF)], pair_act[0], w1, pass_on(v1), name="first", ordered=1
+        first_kernel, [(TWO_MSG, BF), (ONE, BF)], [(TWO, BF)], pair_act[0], w1, pass_on(v1, 0), name="first", ordered=1
     )
     kept1, pmsg1 = product(exchange(lr1), False)
     lr2, z1, prod1 = call(
@@ -390,7 +390,7 @@
         cot_t, mix2, prod2, z1, w2, v2,
         name="late_incoming",
     )
-    gsides2 = grads(exchange(gmsg2), kept2, True)
+    gsides2 = grads(exchange(gmsg2), kept2, v2, True)
     gmsg1, sums2, grad_u1, mix1 = call(
         back_kernel,
         [(ONE_MSG, BF), ((4 * C, C), BF), (ONE, F32), (ONE, BF)],
@@ -410,7 +410,8 @@
     own = jnp.where(first_core, sums2, gates)
     swaps = [(rep, rep ^ 1) for rep in range(lax.axis_size("rep"))]
     other = lax.ppermute(jnp.where(first_core, gates, sums2), "rep", swaps)
-    gsides1 = grads(exchange(gmsg1), kept1, False)
+    grad_ch = exchange(gmsg1)
+    gsides1 = grads(grad_ch, kept1, pass_on(grad_ch, 1), False)
     wmsg, proj1 = call(
         last_kernel,
         [((8 * C, C), BF), (PROJ, BF)],

time: 235 us -> 230 us (0.979)
  blocking collectives: 129 us -> 125 us
    all_to_all x5, blocking collectives: 97.7 us -> 94.1 us  [exchange(): out = lax.all_to_all(msg.reshape(64, 16, shape[1]), 'dap', 0, 0, tiled=True)]
    ppermute x1 -> x2, starting transfers between devices: 7.73 us -> 8.4 us  [pass_on(): return lax.ppermute(array, ('rep', 'dap'), pairs)]
  transfers between devices with their start and end apart: 6 -> 7, of which waited for: 6 -> 6; matrix products, arithmetic and copies ran while one was open for 0% -> 0% of each run, Pallas kernels for 2% -> 2%
where the time goes in v8:
time: 230 us
  blocking collectives  125 us (54%)
  waiting for transfers between devices  48 us (21%)
  starting transfers between devices  30.5 us (13%)
  Pallas kernels  19.2 us (8%)
  local copies, waits for them, and re-layouts  5.65 us (2%)
    all_to_all x5, blocking collectives, exchange(): out = lax.all_to_all(msg.reshape(64, 16, shape[1]), 'dap', 0, 0, tiled=True)  94.1 us
    all_to_all x3, waiting for transfers between devices, exchange(): out = lax.all_to_all(msg.reshape(64, 16, shape[1]), 'dap', 0, 0, tiled=True)  31.2 us
    pallas_call x14, Pallas kernels, call(): pl.pallas_call(kernel, out_shape=shapes, in_specs=specs, scratch_shapes=[...  19.2 us
    all_to_all x1, blocking collectives, local(): parts = lax.all_to_all(wmsg.reshape(64, 16, C), 'dap', 0, 0, tiled=True)  17 us
    all_to_all x3, starting transfers between devices, exchange(): out = lax.all_to_all(msg.reshape(64, 16, shape[1]), 'dap', 0, 0, tiled=True)  15.3 us
    all_to_all x1, blocking collectives, local(): lax.all_to_all(jnp.broadcast_to(part, (reps, 16, C)), 'rep', 0, 0, tiled=...  14.2 us
    all_to_all x1, waiting for transfers between devices, local(): lax.all_to_all(jnp.broadcast_to(whole, (64, 24, C)), 'dap', 0, 0, tiled=T...  13.3 us
    ppermute x2, starting transfers between devices, pass_on(): return lax.ppermute(array, ('rep', 'dap'), pairs)  8.4 us
  transfers between devices with their start and end apart: 7, of which 6 were waited for; matrix products, arithmetic and copies ran while one was open for 0% of the time, Pallas kernels for 2%

profile of v8, /device:TPU:8, one launch (start us, length us, event | category | flops | bytes accessed | tf_op | source)
XLA Modules:
  0.0 229.6 jit_solution(5355711851994575163)
XLA Ops:
  0.6 7.7 %collective-permute-start = (bf16[128,128]{1,0:T(8,128)(2,1)}, bf16[128,128]{1,0:T(8,128)(2,1)S(1)}, u32[]{:S(2)}, u32[]{:S(2)}) collective-permute-start(bf16[128,128]{1,0:T(8,128)(2,1)} %v_ref.3), channel_id=1, source_target_pairs={{0,4},{1,5},{2,6},{3,7},{4,0},{5,1},{6,2},{7,3},{8,12},{9,13},{10,... | collective-permute-start | bytes 98312 | tf_op jit(solution)/shard_map/ppermute | solution.py:335
  8.4 2.1 collective-permute-done.turn
  10.5 0.9 copy-done
  11.4 0.9 copy-done.18
  12.3 1.3 first.1
  13.7 25.0 %all_to_all.55 = bf16[64,16,256]{2,1,0:T(8,128)(2,1)S(1)} all-to-all(bf16[64,16,256]{2,1,0:T(8,128)(2,1)S(1)} %bitcast.31), channel_id=1, replica_groups=mesh['rep'=8,'dap'=64] {'dap'}, dimensions={0} | all-to-all | bytes 1048576 | tf_op jit(solution)/shard_map/all_to_all | solution.py:324
  38.7 0.8 product.2
  39.5 0.0 copy-start.1
  39.5 0.0 copy-start.2
  39.5 0.0 copy-start.5
  39.5 16.8 %all_to_all.56 = bf16[64,16,128]{2,1,0:T(8,128)(2,1)S(1)} all-to-all(bf16[64,16,128]{2,1,0:T(8,128)(2,1)S(1)} %bitcast.38), channel_id=1, replica_groups=mesh['rep'=8,'dap'=64] {'dap'}, dimensions={0} | all-to-all | bytes 524288 | tf_op jit(solution)/shard_map/all_to_all | solution.py:324
  56.4 1.7 middle.1
  58.1 18.6 %all_to_all.57 = bf16[64,16,256]{2,1,0:T(8,128)(2,1)S(1)} all-to-all(bf16[64,16,256]{2,1,0:T(8,128)(2,1)S(1)} %bitcast.30), channel_id=1, replica_groups=mesh['rep'=8,'dap'=64] {'dap'}, dimensions={0} | all-to-all | bytes 1048576 | tf_op jit(solution)/shard_map/all_to_all | solution.py:324
  76.6 1.5 product.3
  78.1 5.5 %all-to-all-start.3 = ((bf16[64,16,128]{2,1,0:T(8,128)(2,1)}), bf16[64,16,128]{2,1,0:T(8,128)(2,1)S(1)}, u32[]{:S(2)}, u32[]{:S(2)}) async-start(bf16[64,16,128]{2,1,0:T(8,128)(2,1)} %bitcast.7), calls=%async_computation.3 | async-start | bytes 524288 | tf_op jit(solution)/shard_map/all_to_all | solution.py:324
  83.7 1.0 cotangent.1
  84.7 0.0 copy-start.10
  84.7 0.7 copy-done.10
  85.4 10.0 %all-to-all-done.3 = bf16[64,16,128]{2,1,0:T(8,128)(2,1)S(1)} async-done(((bf16[64,16,128]{2,1,0:T(8,128)(2,1)}), bf16[64,16,128]{2,1,0:T(8,128)(2,1)S(1)}, u32[]{:S(2)}, u32[]{:S(2)}) %all-to-all-start.3) | async-done | bytes 262176 | tf_op jit(solution)/shard_map/all_to_all | solution.py:324
  95.4 0.9 turn.1
  96.3 0.7 copy-done.12
  97.0 16.6 %all_to_all.58 = bf16[64,16,128]{2,1,0:T(8,128)(2,1)S(1)} all-to-all(bf16[64,16,128]{2,1,0:T(8,128)(2,1)S(1)} %bitcast.37), channel_id=1, replica_groups=mesh['rep'=8,'dap'=64] {'dap'}, dimensions={0} | all-to-all | bytes 524288 | tf_op jit(solution)/shard_map/all_to_all | solution.py:324
  113.6 1.7 grads.2
  115.3 4.9 %all-to-all-start.5 = ((bf16[64,16,256]{2,1,0:T(8,128)(2,1)}), bf16[64,16,256]{2,1,0:T(8,128)(2,1)S(1)}, u32[]{:S(2)}, u32[]{:S(2)}) async-start(bf16[64,16,256]{2,1,0:T(8,128)(2,1)} %bitcast.12), calls=%async_computation.5 | async-start | bytes 1048576 | tf_op jit(solution)/shard_map/all_to_all | solution.py:324
  120.2 0.9 late_incoming.1
  121.2 0.0 copy-start.16
  121.2 0.6 copy-done.16
  121.8 12.4 %all-to-all-done.5 = bf16[64,16,256]{2,1,0:T(8,128)(2,1)S(1)} async-done(((bf16[64,16,256]{2,1,0:T(8,128)(2,1)}), bf16[64,16,256]{2,1,0:T(8,128)(2,1)S(1)}, u32[]{:S(2)}, u32[]{:S(2)}) %all-to-all-start.5) | async-done | bytes 524320 | tf_op jit(solution)/shard_map/all_to_all | solution.py:324
  134.2 2.5 %back.1 = (bf16[1024,128]{1,0:T(8,128)(2,1)S(1)}, bf16[512,128]{1,0:T(8,128)(2,1)S(1)}, f32[512,256]{1,0:T(8,128)S(1)}, bf16[512,256]{1,0:T(8,128)(2,1)S(1)}) custom-call(bf16[1024,256]{1,0:T(8,128)(2,1)S(1)} %bitcast.23, f32[512,256]{1,0:T(8,128)S(1)} %get-tuple-element.38.z1.state, bf16[512,256]{1,0:T(8,128)(2,1)S(1)} %get-tuple-element.45.gg2, ...), custom_call_target="tpu_custom_call" | custom-call | flops 200000000 | bytes 3637248 | tf_op jit(solution)/shard_map/back/pallas_call | solution.py:309
  136.8 17.1 %all_to_all.59 = bf16[64,16,128]{2,1,0:T(8,128)(2,1)S(1)} all-to-all(bf16[64,16,128]{2,1,0:T(8,128)(2,1)S(1)} %bitcast.35), channel_id=1, replica_groups=mesh['rep'=8,'dap'=64] {'dap'}, dimensions={0} | all-to-all | bytes 524288 | tf_op jit(solution)/shard_map/all_to_all | solution.py:324
  153.9 0.7 collective-permute-start.1
  154.6 1.6 grads.3
  156.2 4.9 %all-to-all-start.7 = ((bf16[64,16,256]{2,1,0:T(8,128)(2,1)}), bf16[64,16,256]{2,1,0:T(8,128)(2,1)S(1)}, u32[]{:S(2)}, u32[]{:S(2)}) async-start(bf16[64,16,256]{2,1,0:T(8,128)(2,1)} %bitcast.16), calls=%async_computation.7 | async-start | bytes 1048576 | tf_op jit(solution)/shard_map/all_to_all | solution.py:324
  161.2 0.9 late_outgoing.1
  162.1 0.0 copy-start.15
  162.2 0.9 copy-done.15
  163.1 1.9 collective-permute-start.2
  165.0 1.3 collective-permute-done.2.other
  166.3 8.8 %all-to-all-done.7 = bf16[64,16,256]{2,1,0:T(8,128)(2,1)S(1)} async-done(((bf16[64,16,256]{2,1,0:T(8,128)(2,1)}), bf16[64,16,256]{2,1,0:T(8,128)(2,1)S(1)}, u32[]{:S(2)}, u32[]{:S(2)}) %all-to-all-start.7) | async-done | bytes 524320 | tf_op jit(solution)/shard_map/all_to_all | solution.py:324
  175.1 1.2 last.1
  176.3 17.0 %all_to_all.60 = bf16[64,16,128]{2,1,0:T(8,128)(2,1)S(1)} all-to-all(bf16[64,16,128]{2,1,0:T(8,128)(2,1)S(1)} %bitcast.36), channel_id=1, replica_groups=mesh['rep'=8,'dap'=64] {'dap'}, dimensions={0} | all-to-all | bytes 524288 | tf_op jit(solution)/shard_map/all_to_all | solution.py:427
  193.2 0.1 convert_reduce_fusion
  193.3 14.2 %all_to_all.61 = f32[8,16,128]{2,1,0:T(8,128)S(1)} all-to-all(f32[8,16,128]{2,1,0:T(8,128)S(1)} %broadcast_in_dim.10), channel_id=1, replica_groups=mesh['rep'=8,'dap'=64] {'rep'}, dimensions={0} | all-to-all | bytes 131072 | tf_op jit(solution)/shard_map/all_to_all | solution.py:430
  207.5 0.8 broadcast_in_dim.11
  208.3 4.8 %all-to-all-start.10 = ((bf16[64,24,128]{2,1,0:T(8,128)(2,1)}), bf16[64,24,128]{2,1,0:T(8,128)(2,1)S(1)}, u32[]{:S(2)}, u32[]{:S(2)}) async-start(bf16[64,24,128]{2,1,0:T(8,128)(2,1)} %broadcast_in_dim.11), calls=%async_computation.10 | async-start | bytes 786432 | tf_op jit(solution)/shard_map/all_to_all | solution.py:436
  213.1 2.2 pair.1
  215.3 13.3 %all-to-all-done.10 = bf16[64,24,128]{2,1,0:T(8,128)(2,1)S(1)} async-done(((bf16[64,24,128]{2,1,0:T(8,128)(2,1)}), bf16[64,24,128]{2,1,0:T(8,128)(2,1)S(1)}, u32[]{:S(2)}, u32[]{:S(2)}) %all-to-all-start.10) | async-done | bytes 393248 | tf_op jit(solution)/shard_map/all_to_all | solution.py:436
  228.6 0.9 finish.1
  (33 shorter events, 0.1 us)
Async XLA Ops:
  0.6 9.8 %collective-permute-start = (bf16[128,128]{1,0:T(8,128)(2,1)}, bf16[128,128]{1,0:T(8,128)(2,1)S(1)}, u32[]{:S(2)}, u32[]{:S(2)}) collective-permute-start(bf16[128,128]{1,0:T(8,128)(2,1)} %v_ref.3), channel_id=1, source_target_pairs={{0,4},{1,5},{2,6},{3,7},{4,0},{5,1},{6,2},{7,3},{8,12},{9,13},{10,... | collective-permute-start | bytes 98312 | tf_op jit(solution)/shard_map/ppermute | solution.py:335
  10.5 0.9 copy-start
  11.4 0.9 copy-start.18
  39.5 16.9 %copy-start.1 = (bf16[128,640]{1,0:T(8,128)(2,1)S(1)}, bf16[128,640]{1,0:T(8,128)(2,1)}, u32[]{:S(2)}) copy-start(bf16[128,640]{1,0:T(8,128)(2,1)} %w1.9) | copy-start | bytes 491524
  39.5 16.9 %copy-start.2 = (bf16[128,640]{1,0:T(8,128)(2,1)S(1)}, bf16[128,640]{1,0:T(8,128)(2,1)}, u32[]{:S(2)}) copy-start(bf16[128,640]{1,0:T(8,128)(2,1)} %w2.5) | copy-start | bytes 491524
  39.5 16.9 %copy-start.5 = (bf16[128,128]{1,0:T(8,128)(2,1)S(1)}, bf16[128,128]{1,0:T(8,128)(2,1)}, u32[]{:S(2)}) copy-start(bf16[128,128]{1,0:T(8,128)(2,1)} %v_ref.3) | copy-start | bytes 98308
  78.1 5.5 %copy-start.3 = (bf16[1024,256]{1,0:T(8,128)(2,1)}, bf16[1024,256]{1,0:T(8,128)(2,1)S(1)}, u32[]{:S(2)}) copy-start(bf16[1024,256]{1,0:T(8,128)(2,1)S(1)} %get-tuple-element.41.refs_1_) | copy-start | bytes 1572868
  78.1 5.5 %copy-start.6 = (bf16[128,128]{1,0:T(8,128)(2,1)S(1)}, bf16[128,128]{1,0:T(8,128)(2,1)}, u32[]{:S(2)}) copy-start(bf16[128,128]{1,0:T(8,128)(2,1)} %v_ref.2) | copy-start | bytes 98308
  78.1 5.5 %copy-start.7 = (bf16[1,4,256,128]{3,2,1,0:T(8,128)(2,1)S(1)}, bf16[1,4,256,128]{3,2,1,0:T(8,128)(2,1)}, u32[]{:S(2)}) copy-start(bf16[1,4,256,128]{3,2,1,0:T(8,128)(2,1)} %param.7) | copy-start | bytes 786436
  78.1 17.3 %all-to-all-start.3 = ((bf16[64,16,128]{2,1,0:T(8,128)(2,1)}), bf16[64,16,128]{2,1,0:T(8,128)(2,1)S(1)}, u32[]{:S(2)}, u32[]{:S(2)}) async-start(bf16[64,16,128]{2,1,0:T(8,128)(2,1)} %bitcast.7), calls=%async_computation.3 | async-start | bytes 524288 | tf_op jit(solution)/shard_map/all_to_all | solution.py:324
  84.7 0.7 copy-start.10
  95.4 18.2 %copy-start.4 = (bf16[1024,256]{1,0:T(8,128)(2,1)S(1)}, bf16[1024,256]{1,0:T(8,128)(2,1)}, u32[]{:S(2)}) copy-start(bf16[1024,256]{1,0:T(8,128)(2,1)} %copy-done.3) | copy-start | bytes 1572868
  96.3 0.7 copy-start.12
  115.3 4.9 %copy-start.11 = (bf16[512,256]{1,0:T(8,128)(2,1)S(1)}, bf16[512,256]{1,0:T(8,128)(2,1)}, u32[]{:S(2)}) copy-start(bf16[512,256]{1,0:T(8,128)(2,1)} %copy-done.10) | copy-start | bytes 786436
  115.3 4.9 %copy-start.13 = (bf16[512,256]{1,0:T(8,128)(2,1)S(1)}, bf16[512,256]{1,0:T(8,128)(2,1)}, u32[]{:S(2)}) copy-start(bf16[512,256]{1,0:T(8,128)(2,1)} %copy-done.12) | copy-start | bytes 786436
  115.3 18.9 %all-to-all-start.5 = ((bf16[64,16,256]{2,1,0:T(8,128)(2,1)}), bf16[64,16,256]{2,1,0:T(8,128)(2,1)S(1)}, u32[]{:S(2)}, u32[]{:S(2)}) async-start(bf16[64,16,256]{2,1,0:T(8,128)(2,1)} %bitcast.12), calls=%async_computation.5 | async-start | bytes 1048576 | tf_op jit(solution)/shard_map/all_to_all | solution.py:324
  121.2 0.6 copy-start.16
  136.8 17.1 %copy-start.8 = (bf16[512,256]{1,0:T(8,128)(2,1)}, bf16[512,256]{1,0:T(8,128)(2,1)S(1)}, u32[]{:S(2)}) copy-start(bf16[512,256]{1,0:T(8,128)(2,1)S(1)} %get-tuple-element.52.mix) | copy-start | bytes 786436
  136.8 17.1 %copy-start.14 = (bf16[512,128]{1,0:T(8,128)(2,1)}, bf16[512,128]{1,0:T(8,128)(2,1)S(1)}, u32[]{:S(2)}) copy-start(bf16[512,128]{1,0:T(8,128)(2,1)S(1)} %get-tuple-element.49) | copy-start | bytes 393220
  153.9 0.7 collective-permute-start.1
  156.2 5.0 %copy-start.17 = (bf16[256,128]{1,0:T(8,128)(2,1)S(1)}, bf16[256,128]{1,0:T(8,128)(2,1)}, u32[]{:S(2)}) copy-start(bf16[256,128]{1,0:T(8,128)(2,1)} %copy-done.16) | copy-start | bytes 196612
  156.2 5.0 %copy-start.9 = (bf16[512,256]{1,0:T(8,128)(2,1)S(1)}, bf16[512,256]{1,0:T(8,128)(2,1)}, u32[]{:S(2)}) copy-start(bf16[512,256]{1,0:T(8,128)(2,1)} %copy-done.8) | copy-start | bytes 786436
  156.2 18.9 %all-to-all-start.7 = ((bf16[64,16,256]{2,1,0:T(8,128)(2,1)}), bf16[64,16,256]{2,1,0:T(8,128)(2,1)S(1)}, u32[]{:S(2)}, u32[]{:S(2)}) async-start(bf16[64,16,256]{2,1,0:T(8,128)(2,1)} %bitcast.16), calls=%async_computation.7 | async-start | bytes 1048576 | tf_op jit(solution)/shard_map/all_to_all | solution.py:324
  162.1 0.9 copy-start.15
  163.1 3.2 %collective-permute-start.2 = (bf16[512,128]{1,0:T(8,128)(2,1)S(1)}, bf16[512,128]{1,0:T(8,128)(2,1)S(1)}, u32[]{:S(2)}, u32[]{:S(2)}) collective-permute-start(bf16[512,128]{1,0:T(8,128)(2,1)S(1)} %get-tuple-element.63), channel_id=1, source_target_pairs={{0,64},{64,0},{128,192},{192,128},{256,320},{320,256},{384,448},{4... | collective-permute-start | bytes 393224 | tf_op jit(solution)/shard_map/ppermute | solution.py:412
  208.3 20.3 %all-to-all-start.10 = ((bf16[64,24,128]{2,1,0:T(8,128)(2,1)}), bf16[64,24,128]{2,1,0:T(8,128)(2,1)S(1)}, u32[]{:S(2)}, u32[]{:S(2)}) async-start(bf16[64,24,128]{2,1,0:T(8,128)(2,1)} %broadcast_in_dim.11), calls=%async_computation.10 | async-start | bytes 786432 | tf_op jit(solution)/shard_map/all_to_all | solution.py:436
